TPU v7x, 128 devices: a whole 4x4x4 slice. The times are simulated.
128 devices in a mesh: dp: 16 (over y, x), tensor: 8 (over z, core).
Axes of the slice: x: 4, y: 4, z: 4, core: 2. Of those that a mesh axis runs over, the one named last changes fastest.
Arguments:
- acts: bfloat16 [16384, 5120], P('dp'), may hold values from -12 to 12
- out_grad: bfloat16 [16384, 5120], P('dp', 'tensor'), may hold values from -0.0625 to 0.0625
- error: bfloat16 [81920, 5120], P('dp', 'tensor'), may hold values from -9 to 9
- q_seed: int32 [5120, 32], P('tensor'), may hold values from -64 to 64
- dither: int32 [5120, 32], P('tensor'), may hold values from 0 to 65535
Outputs:
- q_factor: bfloat16 [5120, 32], P('tensor')
- new_error: bfloat16 [81920, 5120], P('dp', 'tensor')
All inputs are finite; a program needn't handle non-finite values.
Results may differ from a plain program's by a relative error of at most 0.0053.
Values sent between devices are 32-bit elements; how exact they have to be, the bound alone decides.
No kernel may reach another device: no remote copies, remote signals or barrier semaphores. Data moves between devices by JAX's collectives and lax.ppermute only.
A program may use at most 128 MiB of HBM per device.

v0:
```python
import jax
import jax.numpy as jnp
from jax import lax
from jax.sharding import PartitionSpec as P

HIGH = lax.Precision.HIGHEST


def orthonormal(pmat, gram):
    lower = jnp.linalg.cholesky(gram)
    return lax.linalg.triangular_solve(lower, pmat, left_side=False, lower=True, transpose_a=True)


def per_device(acts, out_grad, error, q_seed, dither):
    q_start = q_seed.astype(jnp.float32) / 32.0
    workers = lax.axis_size("dp")
    error_wide = error.astype(jnp.float32)
    grad = lax.dot_general(
        acts, out_grad, (((0,), (0,)), ((), ())), preferred_element_type=jnp.float32
    )
    memory = grad + error_wide
    p_local = jnp.dot(memory, q_start, precision=HIGH)
    pmat = lax.psum(p_local, ("dp", "tensor"))
    gram = jnp.dot(pmat.T, pmat, precision=HIGH)
    p_hat = orthonormal(pmat, gram)
    q_local = jnp.dot(memory.T, p_hat, precision=HIGH)
    qmat = lax.psum(q_local, "dp") / workers
    q_factor = (qmat * (1.0 + (dither.astype(jnp.float32) / 65536.0 - 0.5) / 4.0)).astype(
        jnp.bfloat16
    )
    approx = jnp.dot(p_hat, q_factor.astype(jnp.float32).T, precision=HIGH)
    new_error = (memory - approx).astype(jnp.bfloat16)
    return (q_factor, new_error)


def solution(mesh):
    in_specs = (
        P("dp", None),
        P("dp", "tensor"),
        P("dp", "tensor"),
        P("tensor", None),
        P("tensor", None),
    )
    out_specs = (P("tensor", None), P("dp", "tensor"))
    return jax.shard_map(
        per_device, mesh=mesh, in_specs=in_specs, out_specs=out_specs, check_vma=False
    )
```

profile of v0, /device:TPU:0, one launch (start us, length us, event | category | flops | bytes accessed | tf_op | source)
XLA Modules:
  0.0 305.9 jit_solution(17472055001385686766)
XLA Ops:
  7.2 0.0 copy-start
  7.2 0.0 copy-start.3
  7.2 0.0 all-reduce.3.cloned.1.call-start
  7.2 1.3 copy-done
  8.5 12.8 %convert_add_fusion = f32[5120,640]{1,0:T(8,128)S(1)} fusion(bf16[5120,640]{1,0:T(8,128)(2,1)} %param.7, bf16[1024,5120]{1,0:T(8,128)(2,1)} %param.5, bf16[1024,640]{1,0:T(8,128)(2,1)S(1)} %copy-done), kind=kOutput, calls=%fused_computation.1 | convolution fusion | flops 6717440000 | bytes 31457280 | tf_op jit(solution)/shard_map/dot_general | solution.py:18
  21.3 0.0 copy-start.1
  21.3 4.7 %copy-done.1 = f32[5120,640]{1,0:T(8,128)} copy-done((f32[5120,640]{1,0:T(8,128)}, f32[5120,640]{1,0:T(8,128)S(1)}, u32[]{:S(2)}) %copy-start.1) | copy-done | bytes 13107224
  25.9 0.0 copy-done.3
  25.9 13.3 %fusion = f32[5120,32]{0,1:T(8,128)} fusion(f32[5120,640]{1,0:T(8,128)S(1)} %convert_add_fusion, s32[640,32]{0,1:T(8,128)S(1)} %copy-done.3), kind=kOutput, calls=%fused_computation.3 | convolution fusion | flops 1258332160 | bytes 13844480 | tf_op jit(solution)/shard_map/dot_general | solution.py:22
  39.2 0.0 copy-start.4
  39.2 0.0 all-reduce.3.cloned.1.call-update
  39.3 0.0 all-reduce.5.cloned.1.call-start
  39.3 147.2 %all-reduce.3.cloned.1.call-done = f32[5120,32]{0,1:T(8,128)} async-done(((f32[5120,32]{0,1:T(8,128)}), f32[5120,32]{0,1:T(8,128)}) %all-reduce.3.cloned.1.call-update) | async-done | bytes 655376 | tf_op jit(solution)/shard_map/psum | solution.py:23
  186.5 1.9 fusion.9
  188.4 0.1 copy.7
  188.5 2.9 cholesky.16
  191.5 0.6 compare_reduce_fusion
  192.1 0.7 fusion.4
  192.8 2.4 custom-call.6
  195.2 1.8 fusion.5
  197.0 11.0 %fusion.10 = f32[640,32]{0,1:T(8,128)} fusion(f32[5120,640]{1,0:T(8,128)} %copy-done.1, f32[5120,32]{0,1:T(8,128)S(1)} %fusion.5), kind=kOutput, calls=%fused_computation.19 | convolution fusion | flops 1258291200 | bytes 13844480 | tf_op jit(solution)/shard_map/dot_general | solution.py:26
  208.0 0.0 all-reduce.5.cloned.1.call-update
  208.1 79.7 %all-reduce.5.cloned.1.call-done = f32[640,32]{0,1:T(8,128)} async-done(((f32[640,32]{0,1:T(8,128)}), f32[640,32]{0,1:T(8,128)}) %all-reduce.5.cloned.1.call-update) | async-done | bytes 81936 | tf_op jit(solution)/shard_map/psum | solution.py:27
  287.8 0.0 copy-done.4
  287.8 0.9 multiply_convert_fusion
  288.7 0.0 copy-start.2
  288.7 10.4 %subtract_convert_fusion = bf16[5120,640]{1,0:T(8,128)(2,1)} fusion(f32[5120,640]{1,0:T(8,128)} %copy-done.1, f32[5120,32]{0,1:T(8,128)S(1)} %fusion.5, bf16[640,32]{0,1:T(8,128)(2,1)S(1)} %multiply_convert_fusion), kind=kOutput, calls=%fused_computation | convolution fusion | flops 1264844800 | bytes 20357120 | tf_op jit(solution)/shard_map/dot_general | solution.py:31
  299.1 0.0 copy-done.2
  (2 shorter events, 0.0 us)
Async XLA Ops:
  7.2 1.3 copy-start
  7.2 18.8 %copy-start.3 = (s32[640,32]{0,1:T(8,128)S(1)}, s32[640,32]{0,1:T(8,128)}, u32[]{:S(2)}) copy-start(s32[640,32]{0,1:T(8,128)} %param.8) | copy-start | bytes 245764
  7.2 179.3 %all-reduce.3.cloned.1.call-start = ((), (), s32[]{:S(2)}) async-start(), calls=%async_computation | async-start | bytes 1310720 | tf_op jit(solution)/shard_map/psum | solution.py:23
  21.3 4.7 %copy-start.1 = (f32[5120,640]{1,0:T(8,128)}, f32[5120,640]{1,0:T(8,128)S(1)}, u32[]{:S(2)}) copy-start(f32[5120,640]{1,0:T(8,128)S(1)} %convert_add_fusion) | copy-start | bytes 39321604
  39.2 248.6 %copy-start.4 = (s32[640,32]{0,1:T(8,128)S(1)}, s32[640,32]{0,1:T(8,128)}, u32[]{:S(2)}) copy-start(s32[640,32]{0,1:T(8,128)} %param.9) | copy-start | bytes 245764
  39.3 248.6 %all-reduce.5.cloned.1.call-start = ((), (), s32[]{:S(2)}) async-start(), calls=%async_computation.1 | async-start | bytes 163840 | tf_op jit(solution)/shard_map/psum | solution.py:27
  288.7 10.4 %copy-start.2 = (bf16[640,32]{0,1:T(8,128)(2,1)}, bf16[640,32]{0,1:T(8,128)(2,1)S(1)}, u32[]{:S(2)}) copy-start(bf16[640,32]{0,1:T(8,128)(2,1)S(1)} %multiply_convert_fusion) | copy-start | bytes 122884
Sparse Core Ops, SparseCore 0:
  39.4 147.0 all-reduce.2
  208.2 79.5 all-reduce.4
where the time goes:
time: 306 us
  waiting for transfers between devices  227 us (74%)
  matrix products  51.2 us (17%)
  between operations  14.1 us (5%)
  other arithmetic  7.6 us (2%)
  local copies, waits for them, and re-layouts  6 us (2%)
    psum x1, waiting for transfers between devices, per_device(): pmat = lax.psum(p_local, ('dp', 'tensor'))  147 us
    psum x1, waiting for transfers between devices, per_device(): qmat = lax.psum(q_local, 'dp') / workers  79.7 us
    dot_general x1, matrix products, per_device(): p_local = jnp.dot(memory, q_start, precision=HIGH)  13.3 us
    dot_general x1, matrix products, per_device(): lax.dot_general(acts, out_grad, (((0,), (0,)), ((), ())), preferred_eleme...  12.8 us
    dot_general x1, matrix products, per_device(): q_local = jnp.dot(memory.T, p_hat, precision=HIGH)  11 us
    dot_general x1, matrix products, per_device(): approx = jnp.dot(p_hat, q_factor.astype(jnp.float32).T, precision=HIGH)  10.4 us
  transfers between devices with their start and end apart: 2, of which 2 were waited for; matrix products, arithmetic and copies ran while one was open for 0% of the time, Pallas kernels for 0%

commit v1 on v0

v1 whole, which is shorter than its diff:
```python
import jax
import jax.numpy as jnp
from jax import lax
from jax.experimental import pallas as pl
from jax.experimental.pallas import tpu as pltpu
from jax.sharding import PartitionSpec as P

HIGH = lax.Precision.HIGHEST
F32 = jnp.float32
BF16 = jnp.bfloat16

D = 5120
TOK = 1024
COLS = 640
RANK = 32
NBLK = 8
WORKERS = 16
MB = 1 << 20

NT = (((1,), (1,)), ((), ()))
TN = (((0,), (0,)), ((), ()))


def params(mb, n=1):
    return pltpu.CompilerParams(
        vmem_limit_bytes=mb * MB, dimension_semantics=("arbitrary",) * n
    )


def split3(x):
    hi = x.astype(BF16)
    r = x - hi.astype(F32)
    mid = r.astype(BF16)
    lo = (r - mid.astype(F32)).astype(BF16)
    return jnp.concatenate([hi, mid, lo], axis=0)


def fold3(y):
    return y[:RANK] + y[RANK : 2 * RANK] + y[2 * RANK :]


def left_body(first, t_ref, acts_ref, err_ref, grad_ref, seed_ref, t3_in, *outs):
    if first:
        p_ref, t3_ref, qt_ref = outs

        @pl.when(pl.program_id(0) == 0)
        def _():
            qt = seed_ref[...].astype(F32).T.astype(BF16)
            qt_ref[...] = qt
            tt = lax.dot_general(qt, grad_ref[...], NT, preferred_element_type=F32)
            t3_ref[...] = split3(tt)

        t3 = t3_ref[...]
        qt = qt_ref[...]
    else:
        (p_ref,) = outs
        t3 = t3_in[...]
        qt = seed_ref[...]
    p = fold3(jnp.dot(t3, acts_ref[...], preferred_element_type=F32))
    p = p + lax.dot_general(qt, err_ref[...], NT, preferred_element_type=F32)
    p_ref[0] = p * (1.0 / 32.0)


def left_first(t, acts, error, out_grad, q_seed):
    def body(t_ref, a, e, g, s, *outs):
        left_body(True, t_ref, a, e, g, s, None, *outs)

    return pl.pallas_call(
        body,
        out_shape=(
            jax.ShapeDtypeStruct((4, RANK, COLS), F32),
            jax.ShapeDtypeStruct((3 * RANK, TOK), BF16),
            jax.ShapeDtypeStruct((RANK, COLS), BF16),
        ),
        grid_spec=pltpu.PrefetchScalarGridSpec(
            num_scalar_prefetch=1,
            grid=(4,),
            in_specs=[
                pl.BlockSpec((TOK, COLS), lambda i, t: (0, t[0] ^ (2 * i + 1))),
                pl.BlockSpec((COLS, COLS), lambda i, t: (t[0] ^ (2 * i + 1), 0)),
                pl.BlockSpec((TOK, COLS), lambda i, t: (0, 0)),
                pl.BlockSpec((COLS, RANK), lambda i, t: (0, 0)),
            ],
            out_specs=[
                pl.BlockSpec((1, RANK, COLS), lambda i, t: (i, 0, 0)),
                pl.BlockSpec((3 * RANK, TOK), lambda i, t: (0, 0)),
                pl.BlockSpec((RANK, COLS), lambda i, t: (0, 0)),
            ],
        ),
        compiler_params=params(24),
        cost_estimate=pl.CostEstimate(
            flops=2 * 4 * 256 * COLS * (TOK + COLS), bytes_accessed=10 * MB, transcendentals=0
        ),
        name="left_first",
    )(t, acts, error, out_grad, q_seed)


def left_second(t, acts, error, t3, qt):
    def body(t_ref, a, e, s, t3_in, *outs):
        left_body(False, t_ref, a, e, None, s, t3_in, *outs)

    return pl.pallas_call(
        body,
        out_shape=jax.ShapeDtypeStruct((4, RANK, COLS), F32),
        grid_spec=pltpu.PrefetchScalarGridSpec(
            num_scalar_prefetch=1,
            grid=(4,),
            in_specs=[
                pl.BlockSpec((TOK, COLS), lambda i, t: (0, t[0] ^ (2 * i))),
                pl.BlockSpec((COLS, COLS), lambda i, t: (t[0] ^ (2 * i), 0)),
                pl.BlockSpec((RANK, COLS), lambda i, t: (0, 0)),
                pl.BlockSpec((3 * RANK, TOK), lambda i, t: (0, 0)),
            ],
            out_specs=pl.BlockSpec((1, RANK, COLS), lambda i, t: (i, 0, 0)),
        ),
        compiler_params=params(24),
        cost_estimate=pl.CostEstimate(
            flops=2 * 4 * 256 * COLS * (TOK + COLS), bytes_accessed=9 * MB, transcendentals=0
        ),
        name="left_second",
    )(t, acts, error, qt, t3)


def memory_part(first, count, acts, out_grad, error, held):
    def body(a_ref, g_ref, e_ref, *rest):
        out_ref = rest[-1]
        grad = lax.dot_general(a_ref[...], g_ref[...], TN, preferred_element_type=F32)
        out_ref[...] = grad + e_ref[...].astype(F32)

    in_specs = [
        pl.BlockSpec((TOK, COLS), lambda i: (0, first + i)),
        pl.BlockSpec((TOK, COLS), lambda i: (0, 0)),
        pl.BlockSpec((COLS, COLS), lambda i: (first + i, 0)),
    ]
    args = [acts, out_grad, error]
    aliases = {}
    if held is not None:
        in_specs.append(pl.BlockSpec(memory_space=pl.ANY))
        args.append(held)
        aliases = {3: 0}
    return pl.pallas_call(
        body,
        out_shape=jax.ShapeDtypeStruct((D, COLS), F32),
        grid=(count,),
        in_specs=in_specs,
        out_specs=pl.BlockSpec((COLS, COLS), lambda i: (first + i, 0)),
        input_output_aliases=aliases,
        compiler_params=params(24),
        cost_estimate=pl.CostEstimate(
            flops=2 * count * COLS * COLS * TOK, bytes_accessed=count * 4 * MB, transcendentals=0
        ),
        name="memory_part",
    )(*args)


def right_body(last, t_ref, acts_ref, err_ref, grad_ref, *rest):
    blocks = rest[:4]
    if last:
        tmp_in, q_in, q_ref, p3, tmp = rest[4:]
    else:
        tmp, q_ref, p3 = rest[4:]
    i = pl.program_id(0)

    @pl.when(i == 0)
    def _():
        for k in range(4):
            p3[k] = split3(blocks[k][...])
        if last:
            tmp[...] = tmp_in[...]
            q_ref[...] = q_in[...]
        else:
            tmp[...] = jnp.zeros_like(tmp)
            q_ref[...] = jnp.zeros_like(q_ref)

    p = p3[i]
    tmp[...] += fold3(lax.dot_general(p, acts_ref[...], NT, preferred_element_type=F32))
    q_ref[...] += fold3(jnp.dot(p, err_ref[...], preferred_element_type=F32))
    if last:

        @pl.when(i == 3)
        def _():
            t3 = split3(tmp[...])
            q_ref[...] += fold3(jnp.dot(t3, grad_ref[...], preferred_element_type=F32))


def right_part(last, t, acts, error, out_grad, blocks, tmp=None, q=None):
    rc = 1 if last else 0

    def whole(*shape):
        return pl.BlockSpec(shape, lambda i, t: (0,) * len(shape))

    in_specs = [
        pl.BlockSpec((TOK, COLS), lambda i, t: (0, t[0] ^ (2 * i + rc))),
        pl.BlockSpec((COLS, COLS), lambda i, t: (t[0] ^ (2 * i + rc), 0)),
        whole(TOK, COLS),
    ] + [whole(RANK, COLS)] * 4
    args = [acts, error, out_grad, *blocks]
    scratch = [pltpu.VMEM((4, 3 * RANK, COLS), BF16)]
    q_shape = jax.ShapeDtypeStruct((RANK, COLS), F32)
    tmp_shape = jax.ShapeDtypeStruct((RANK, TOK), F32)
    if last:
        in_specs += [whole(RANK, TOK), whole(RANK, COLS)]
        args += [tmp, q]
        scratch.append(pltpu.VMEM((RANK, TOK), F32))
        out_shape, out_specs = q_shape, whole(RANK, COLS)
    else:
        out_shape, out_specs = (tmp_shape, q_shape), [whole(RANK, TOK), whole(RANK, COLS)]

    def body(*refs):
        right_body(last, *refs)

    return pl.pallas_call(
        body,
        out_shape=out_shape,
        grid_spec=pltpu.PrefetchScalarGridSpec(
            num_scalar_prefetch=1,
            grid=(4,),
            in_specs=in_specs,
            out_specs=out_specs,
            scratch_shapes=scratch,
        ),
        compiler_params=params(24),
        cost_estimate=pl.CostEstimate(
            flops=2 * 4 * 256 * COLS * (TOK + COLS), bytes_accessed=10 * MB, transcendentals=0
        ),
        name="right_last" if last else "right_first",
    )(t, *args)


def orthonormal_body(*refs):
    blocks = refs[:NBLK]
    p3_ref, inv_ref = refs[NBLK:]
    gram = jnp.zeros((RANK, RANK), F32)
    for b in blocks:
        x = b[...]
        gram = gram + lax.dot_general(x, x, NT, precision=HIGH, preferred_element_type=F32)
    rows = lax.broadcasted_iota(jnp.int32, (RANK, RANK), 0)
    cols = lax.broadcasted_iota(jnp.int32, (RANK, RANK), 1)
    eye = (rows == cols).astype(F32)
    work = jnp.concatenate([gram, eye], axis=1)
    below = lax.broadcasted_iota(jnp.int32, (RANK, 1), 0)
    for k in range(RANK):
        row = work[k : k + 1, :]
        factor = jnp.where(below > k, work[:, k : k + 1] / row[:, k : k + 1], 0.0)
        work = work - factor * row
    diag = jnp.sum(work[:, :RANK] * eye, axis=1, keepdims=True)
    inv = work[:, RANK:] / jnp.sqrt(diag)
    inv_ref[...] = inv
    for k in range(NBLK):
        p = jnp.dot(inv, blocks[k][...], precision=HIGH, preferred_element_type=F32)
        hi = p.astype(BF16).astype(F32)
        r = p - hi
        mid = r.astype(BF16).astype(F32)
        stacked = jnp.concatenate([hi, mid, r - mid, jnp.zeros_like(p)], axis=0)
        p3_ref[k] = stacked.T.astype(BF16)


def orthonormal(blocks):
    return pl.pallas_call(
        orthonormal_body,
        out_shape=(
            jax.ShapeDtypeStruct((NBLK, COLS, 4 * RANK), BF16),
            jax.ShapeDtypeStruct((RANK, RANK), F32),
        ),
        compiler_params=pltpu.CompilerParams(vmem_limit_bytes=24 * MB),
        cost_estimate=pl.CostEstimate(flops=1 << 31, bytes_accessed=2 * MB, transcendentals=0),
        name="orthonormal",
    )(*blocks)


def update_body(t_ref, a_ref, b_ref, inv_ref, dither_ref, p3_ref, mem_ref, qf_ref, out_ref, q3):
    @pl.when(pl.program_id(0) == 0)
    def _():
        total = a_ref[...] + b_ref[...]
        qmat = jnp.dot(inv_ref[...], total, precision=HIGH, preferred_element_type=F32) / WORKERS
        scale = 1.0 + (dither_ref[...].astype(F32) / 65536.0 - 0.5) / 4.0
        qt = (qmat * scale.T).astype(BF16)
        for k in range(3):
            q3[k * RANK : (k + 1) * RANK, :] = qt
        q3[3 * RANK :, :] = jnp.zeros((RANK, COLS), BF16)
        qf_ref[...] = qt.astype(F32).T.astype(BF16)

    approx = jnp.dot(p3_ref[0], q3[...], preferred_element_type=F32)
    out_ref[...] = (mem_ref[...] - approx).astype(BF16)


def update(t, part_a, part_b, inv, dither, p3, memory):
    def whole(*shape):
        return pl.BlockSpec(shape, lambda i, t: (0,) * len(shape))

    return pl.pallas_call(
        update_body,
        out_shape=(
            jax.ShapeDtypeStruct((COLS, RANK), BF16),
            jax.ShapeDtypeStruct((D, COLS), BF16),
        ),
        grid_spec=pltpu.PrefetchScalarGridSpec(
            num_scalar_prefetch=1,
            grid=(NBLK,),
            in_specs=[
                whole(RANK, COLS),
                whole(RANK, COLS),
                whole(RANK, RANK),
                whole(COLS, RANK),
                pl.BlockSpec((1, COLS, 4 * RANK), lambda i, t: (t[0] ^ i, 0, 0)),
                pl.BlockSpec((COLS, COLS), lambda i, t: (i, 0)),
            ],
            out_specs=[
                whole(COLS, RANK),
                pl.BlockSpec((COLS, COLS), lambda i, t: (i, 0)),
            ],
            scratch_shapes=[pltpu.VMEM((4 * RANK, COLS), BF16)],
        ),
        compiler_params=params(24),
        cost_estimate=pl.CostEstimate(
            flops=2 * D * COLS * 256, bytes_accessed=20 * MB, transcendentals=0
        ),
        name="update",
    )(t, part_a, part_b, inv, dither, p3, memory)


def swap(x, axis, size, mask):
    return lax.ppermute(x, axis, [(i, i ^ mask) for i in range(size)])


def per_device(acts, out_grad, error, q_seed, dither):
    t = lax.axis_index("tensor").astype(jnp.int32).reshape(1)

    def over_tensor(x, mask):
        return swap(x, "tensor", NBLK, mask)

    def over_dp(x, mask):
        return swap(x, "dp", WORKERS, mask)

    away, t3, qt = left_first(t, acts, error, out_grad, q_seed)
    came = over_tensor(away, 1)
    kept = left_second(t, acts, error, t3, qt)
    part = kept + came
    from_z = [over_tensor(part[r], 2 * r) for r in (1, 2, 3)]
    own = part[0] + from_z[0] + from_z[1] + from_z[2]
    memory = None
    for first in range(0, NBLK, 2):
        memory = memory_part(first, 2, acts, out_grad, error, memory)
    for mask in (1, 3, 4, 12):
        own = own + over_dp(own, mask)

    mine = [own] + [over_tensor(own, 2 * r) for r in (1, 2, 3)]
    theirs = [over_tensor(x, 1) for x in mine]
    tmp, q = right_part(False, t, acts, error, out_grad, mine)
    q = right_part(True, t, acts, error, out_grad, theirs, tmp, q)

    blocks = [b for pair in zip(mine, theirs) for b in pair]
    p3, inv = orthonormal(blocks)
    for mask in (1, 3, 4):
        q = q + over_dp(q, mask)
    last = over_dp(q, 12)
    q_factor, new_error = update(t, q, last, inv, dither, p3, memory)
    return (q_factor, new_error)


def solution(mesh):
    in_specs = (
        P("dp", None),
        P("dp", "tensor"),
        P("dp", "tensor"),
        P("tensor", None),
        P("tensor", None),
    )
    out_specs = (P("tensor", None), P("dp", "tensor"))
    return jax.shard_map(
        per_device, mesh=mesh, in_specs=in_specs, out_specs=out_specs, check_vma=False
    )
```

time: 306 us -> 108 us (0.35)
  waiting for transfers between devices: 227 us -> 17.8 us
  matrix products: 51.2 us -> 0 us
  Pallas kernels: 0 us -> 39.4 us
  starting transfers between devices: 0.08 us -> 27.6 us
  local copies, waits for them, and re-layouts: 6 us -> 21.9 us
  between operations: 14.1 us -> 0.84 us
  other arithmetic: 7.6 us -> 0.14 us
    psum x2 -> x0, waiting for transfers between devices: 227 us -> none  [the longest x1 147 us: per_device(): pmat = lax.psum(p_local, ('dp', 'tensor'))]
    dot_general x5 -> x0, matrix products: 49.4 us -> none  [the longest x1 13.3 us: per_device(): p_local = jnp.dot(memory, q_start, precision=HIGH)]
    pallas_call x0 -> x10, Pallas kernels: none -> 39.4 us  [the longest x4 15.8 us: memory_part(): pl.pallas_call(body, out_shape=jax.ShapeDtypeStruct((D, COLS), F32), grid...]
    ppermute x0 -> x19, starting transfers between devices: none -> 27.6 us  [swap(): return lax.ppermute(x, axis, [(i, i ^ mask) for i in range(size)])]
    ppermute x0 -> x19, waiting for transfers between devices: none -> 17.8 us  [swap(): return lax.ppermute(x, axis, [(i, i ^ mask) for i in range(size)])]
    unnamed x10 -> x20, local copies, waits for them, and re-layouts: 5.93 us -> 21.2 us
    another operation x5 -> x0, other arithmetic: 6.68 us -> none  [the longest x3 3.6 us: orthonormal(): lower = jnp.linalg.cholesky(gram)]
  transfers between devices with their start and end apart: 2 -> 19, of which waited for: 2 -> 8; matrix products, arithmetic and copies ran while one was open for 0% -> 0% of each run, Pallas kernels for 0% -> 25%
where the time goes in v1:
time: 108 us
  Pallas kernels  39.4 us (36%)
  starting transfers between devices  27.6 us (26%)
  local copies, waits for them, and re-layouts  21.9 us (20%)
  waiting for transfers between devices  17.8 us (16%)
    ppermute x19, starting transfers between devices, swap(): return lax.ppermute(x, axis, [(i, i ^ mask) for i in range(size)])  27.6 us
    unnamed x20, local copies, waits for them, and re-layouts  21.2 us
    ppermute x19, waiting for transfers between devices, swap(): return lax.ppermute(x, axis, [(i, i ^ mask) for i in range(size)])  17.8 us
    pallas_call x4, Pallas kernels, memory_part(): pl.pallas_call(body, out_shape=jax.ShapeDtypeStruct((D, COLS), F32), grid...  15.8 us
    pallas_call x2, Pallas kernels, right_part(): pl.pallas_call(body, out_shape=out_shape, grid_spec=pltpu.PrefetchScalarG...  7.25 us
    pallas_call x1, Pallas kernels, update(): pl.pallas_call(update_body, out_shape=(jax.ShapeDtypeStruct((COLS, RANK),...  5.73 us
    pallas_call x1, Pallas kernels, orthonormal(): pl.pallas_call(orthonormal_body, out_shape=(jax.ShapeDtypeStruct((NBLK, C...  4.31 us
    pallas_call x1, Pallas kernels, left_first(): pl.pallas_call(body, out_shape=(jax.ShapeDtypeStruct((4, RANK, COLS), F32...  3.43 us
  transfers between devices with their start and end apart: 19, of which 8 were waited for; matrix products, arithmetic and copies ran while one was open for 0% of the time, Pallas kernels for 25%

profile of v1, /device:TPU:0, one launch (start us, length us, event | category | flops | bytes accessed | tf_op | source)
XLA Modules:
  0.0 107.8 jit_solution(2345496483943224094)
XLA Ops:
  1.7 4.0 %copy-done = bf16[1024,5120]{1,0:T(8,128)(2,1)S(1)} copy-done((bf16[1024,5120]{1,0:T(8,128)(2,1)S(1)}, bf16[1024,5120]{1,0:T(8,128)(2,1)}, u32[]{:S(2)}) %copy-start) | copy-done | bytes 10485784
  5.7 2.9 %copy-done.3 = bf16[5120,640]{1,0:T(8,128)(2,1)S(1)} copy-done((bf16[5120,640]{1,0:T(8,128)(2,1)S(1)}, bf16[5120,640]{1,0:T(8,128)(2,1)}, u32[]{:S(2)}) %copy-start.3) | copy-done | bytes 6553624
  8.6 1.3 %copy-done.6 = bf16[1024,640]{1,0:T(8,128)(2,1)S(1)} copy-done((bf16[1024,640]{1,0:T(8,128)(2,1)S(1)}, bf16[1024,640]{1,0:T(8,128)(2,1)}, u32[]{:S(2)}) %copy-start.6) | copy-done | bytes 1310744
  9.9 3.4 %left_first.1 = (f32[4,32,640]{2,1,0:T(8,128)S(1)}, bf16[96,1024]{1,0:T(8,128)(2,1)S(1)}, bf16[32,640]{1,0:T(8,128)(2,1)S(1)}) custom-call(s32[1]{0:T(128)} %bitcast.t_ref.refs_0_, bf16[1024,5120]{1,0:T(8,128)(2,1)S(1)} %copy-done, bf16[5120,640]{1,0:T(8,128)(2,1)S(1)} %copy-done.3, bf16[1024,640]{1,0:T(8,128)(2,1)S(1)} %copy-done.6, s32[640,32]{1,0:T(8,128)S(1)} %copy.10.s), custom_call_target="tpu_custom_call" | custom-call | flops 2181038080 | bytes 10485760 | tf_op jit(solution)/shard_map/left_first/pallas_call | solution.py:68
  13.4 2.9 %left_second.1 = f32[4,32,640]{2,1,0:T(8,128)S(1)} custom-call(s32[1]{0:T(128)} %bitcast.t_ref.refs_0_, bf16[1024,5120]{1,0:T(8,128)(2,1)S(1)} %copy-done, bf16[5120,640]{1,0:T(8,128)(2,1)S(1)} %copy-done.3, bf16[32,640]{1,0:T(8,128)(2,1)S(1)} %get-tuple-element.9.s, bf16[96,1024]{1,0:T(8,128)(2,1)S(1)} %get-tuple-element.10.t3_in), custom_call_target="tpu_custom_call" | custom-call | flops 2181038080 | bytes 9437184 | tf_op jit(solution)/shard_map/left_second/pallas_call | solution.py:102
  16.4 2.1 %collective-permute-start.1 = (f32[32,640]{1,0:T(8,128)S(1)}, f32[32,640]{1,0:T(8,128)S(1)}, u32[]{:S(2)}, u32[]{:S(2)}) collective-permute-start(f32[32,640]{1,0:T(8,128)S(1)} %get-tuple-element.18), channel_id=1, source_target_pairs={{0,2},{1,3},{2,0},{3,1},{4,6},{5,7},{6,4},{7,5},{8,10},{9,11},{10,... | collective-permute-start | bytes 245768 | tf_op jit(solution)/shard_map/ppermute | solution.py:323
  18.5 3.6 %collective-permute-start.2 = (f32[32,640]{1,0:T(8,128)S(1)}, f32[32,640]{1,0:T(8,128)S(1)}, u32[]{:S(2)}, u32[]{:S(2)}) collective-permute-start(f32[32,640]{1,0:T(8,128)S(1)} %get-tuple-element.20), channel_id=1, source_target_pairs={{0,4},{1,5},{2,6},{3,7},{4,0},{5,1},{6,2},{7,3},{8,12},{9,13},{10,... | collective-permute-start | bytes 245768 | tf_op jit(solution)/shard_map/ppermute | solution.py:323
  22.1 4.6 %collective-permute-done.2 = f32[32,640]{1,0:T(8,128)S(1)} collective-permute-done((f32[32,640]{1,0:T(8,128)S(1)}, f32[32,640]{1,0:T(8,128)S(1)}, u32[]{:S(2)}, u32[]{:S(2)}) %collective-permute-start.2) | collective-permute-done | bytes 81952 | tf_op jit(solution)/shard_map/ppermute | solution.py:323
  26.7 1.7 %collective-permute-done.3 = f32[32,640]{1,0:T(8,128)S(1)} collective-permute-done((f32[32,640]{1,0:T(8,128)S(1)}, f32[32,640]{1,0:T(8,128)S(1)}, u32[]{:S(2)}, u32[]{:S(2)}) %collective-permute-start.3) | collective-permute-done | bytes 81952 | tf_op jit(solution)/shard_map/ppermute | solution.py:323
  28.4 1.6 %collective-permute-start.4 = (f32[32,640]{1,0:T(8,128)S(1)}, f32[32,640]{1,0:T(8,128)S(1)}, u32[]{:S(2)}, u32[]{:S(2)}) collective-permute-start(f32[32,640]{1,0:T(8,128)S(1)} %fusion.2), channel_id=1, source_target_pairs={{0,8},{8,0},{16,24},{24,16},{32,40},{40,32},{48,56},{56,48},{64,72... | collective-permute-start | bytes 245768 | tf_op jit(solution)/shard_map/ppermute | solution.py:323
  30.0 2.9 %collective-permute-done.4 = f32[32,640]{1,0:T(8,128)S(1)} collective-permute-done((f32[32,640]{1,0:T(8,128)S(1)}, f32[32,640]{1,0:T(8,128)S(1)}, u32[]{:S(2)}, u32[]{:S(2)}) %collective-permute-start.4) | collective-permute-done | bytes 81952 | tf_op jit(solution)/shard_map/ppermute | solution.py:323
  32.9 2.8 %collective-permute-start.5 = (f32[32,640]{1,0:T(8,128)S(1)}, f32[32,640]{1,0:T(8,128)S(1)}, u32[]{:S(2)}, u32[]{:S(2)}) collective-permute-start(f32[32,640]{1,0:T(8,128)S(1)} %add.37), channel_id=1, source_target_pairs={{0,24},{8,16},{16,8},{24,0},{32,56},{40,48},{48,40},{56,32},{64,88... | collective-permute-start | bytes 245768 | tf_op jit(solution)/shard_map/ppermute | solution.py:323
  35.8 2.9 %collective-permute-done.5 = f32[32,640]{1,0:T(8,128)S(1)} collective-permute-done((f32[32,640]{1,0:T(8,128)S(1)}, f32[32,640]{1,0:T(8,128)S(1)}, u32[]{:S(2)}, u32[]{:S(2)}) %collective-permute-start.5) | collective-permute-done | bytes 81952 | tf_op jit(solution)/shard_map/ppermute | solution.py:323
  38.7 1.7 %collective-permute-start.6 = (f32[32,640]{1,0:T(8,128)S(1)}, f32[32,640]{1,0:T(8,128)S(1)}, u32[]{:S(2)}, u32[]{:S(2)}) collective-permute-start(f32[32,640]{1,0:T(8,128)S(1)} %add.38), channel_id=1, source_target_pairs={{0,32},{8,40},{16,48},{24,56},{32,0},{40,8},{48,16},{56,24},{64,96... | collective-permute-start | bytes 245768 | tf_op jit(solution)/shard_map/ppermute | solution.py:323
  40.4 2.9 %collective-permute-done.6 = f32[32,640]{1,0:T(8,128)S(1)} collective-permute-done((f32[32,640]{1,0:T(8,128)S(1)}, f32[32,640]{1,0:T(8,128)S(1)}, u32[]{:S(2)}, u32[]{:S(2)}) %collective-permute-start.6) | collective-permute-done | bytes 81952 | tf_op jit(solution)/shard_map/ppermute | solution.py:323
  43.2 3.1 %collective-permute-start.7 = (f32[32,640]{1,0:T(8,128)S(1)}, f32[32,640]{1,0:T(8,128)S(1)}, u32[]{:S(2)}, u32[]{:S(2)}) collective-permute-start(f32[32,640]{1,0:T(8,128)S(1)} %add.39), channel_id=1, source_target_pairs={{0,96},{8,104},{16,112},{24,120},{32,64},{40,72},{48,80},{56,88},{... | collective-permute-start | bytes 245768 | tf_op jit(solution)/shard_map/ppermute | solution.py:323
  46.5 2.5 %collective-permute-done.7 = f32[32,640]{1,0:T(8,128)S(1)} collective-permute-done((f32[32,640]{1,0:T(8,128)S(1)}, f32[32,640]{1,0:T(8,128)S(1)}, u32[]{:S(2)}, u32[]{:S(2)}) %collective-permute-start.7) | collective-permute-done | bytes 81952 | tf_op jit(solution)/shard_map/ppermute | solution.py:323
  49.1 1.9 %collective-permute-start.11 = (f32[32,640]{1,0:T(8,128)S(1)}, f32[32,640]{1,0:T(8,128)S(1)}, u32[]{:S(2)}, u32[]{:S(2)}) collective-permute-start(f32[32,640]{1,0:T(8,128)S(1)} %add.40.refs_4_.refs_0_), channel_id=1, source_target_pairs={{0,4},{1,5},{2,6},{3,7},{4,0},{5,1},{6,2},{7,3},{8,12},{9,13},{10,... | collective-permute-start | bytes 245768 | tf_op jit(solution)/shard_map/ppermute | solution.py:323
  51.0 2.8 %collective-permute-start.13 = (f32[32,640]{1,0:T(8,128)S(1)}, f32[32,640]{1,0:T(8,128)S(1)}, u32[]{:S(2)}, u32[]{:S(2)}) collective-permute-start(f32[32,640]{1,0:T(8,128)S(1)} %add.40.refs_4_.refs_0_), channel_id=1, source_target_pairs={{0,6},{1,7},{2,4},{3,5},{4,2},{5,3},{6,0},{7,1},{8,14},{9,15},{10,... | collective-permute-start | bytes 245768 | tf_op jit(solution)/shard_map/ppermute | solution.py:323
  53.8 4.0 %copy-done.1 = bf16[1024,5120]{1,0:T(8,128)(2,1)S(1)} copy-done((bf16[1024,5120]{1,0:T(8,128)(2,1)S(1)}, bf16[1024,5120]{1,0:T(8,128)(2,1)}, u32[]{:S(2)}) %copy-start.1) | copy-done | bytes 10485784
  57.8 2.9 %copy-done.4 = bf16[5120,640]{1,0:T(8,128)(2,1)S(1)} copy-done((bf16[5120,640]{1,0:T(8,128)(2,1)S(1)}, bf16[5120,640]{1,0:T(8,128)(2,1)}, u32[]{:S(2)}) %copy-start.4) | copy-done | bytes 6553624
  60.6 3.9 %memory_part.4.rest_0_ = f32[5120,640]{1,0:T(8,128)} custom-call(bf16[1024,5120]{1,0:T(8,128)(2,1)S(1)} %copy-done.1, bf16[1024,640]{1,0:T(8,128)(2,1)S(1)} %copy-done.7, bf16[5120,640]{1,0:T(8,128)(2,1)S(1)} %copy-done.4), custom_call_target="tpu_custom_call" | custom-call | flops 1677721600 | bytes 8388608 | tf_op jit(solution)/shard_map/memory_part/pallas_call | solution.py:141
  65.8 3.4 %right_first.1 = (f32[32,1024]{1,0:T(8,128)S(1)}, f32[32,640]{1,0:T(8,128)S(1)}) custom-call(s32[1]{0:T(128)} %bitcast.t_ref.refs_0_, bf16[1024,5120]{1,0:T(8,128)(2,1)S(1)} %copy-done.2, bf16[5120,640]{1,0:T(8,128)(2,1)S(1)} %copy-done.4, bf16[1024,640]{1,0:T(8,128)(2,1)S(1)} %copy-done.7, f32[32,640]{1,0:T(8,128)S(1)} %add.40.refs_4_.refs_0_, ...), custom_call_target="tpu_custom_call" | custom-call | flops 2181038080 | bytes 10485760 | tf_op jit(solution)/shard_map/right_first/pallas_call | solution.py:212
  69.3 3.8 %right_last.1 = f32[32,640]{1,0:T(8,128)S(1)} custom-call(s32[1]{0:T(128)} %bitcast.t_ref.refs_0_, bf16[1024,5120]{1,0:T(8,128)(2,1)S(1)} %copy-done.2, bf16[5120,640]{1,0:T(8,128)(2,1)S(1)} %copy-done.4, bf16[1024,640]{1,0:T(8,128)(2,1)S(1)} %copy-done.7, f32[32,640]{1,0:T(8,128)S(1)} %collective-permute-done.8.refs_4_.refs_1_, ...), custom_call_target="tpu_custom_call" | custom-call | flops 2181038080 | bytes 10485760 | tf_op jit(solution)/shard_map/right_last/pallas_call | solution.py:212
  73.5 3.9 %memory_part.5.rest_0_ = f32[5120,640]{1,0:T(8,128)} custom-call(bf16[1024,5120]{1,0:T(8,128)(2,1)S(1)} %copy-done.2, bf16[1024,640]{1,0:T(8,128)(2,1)S(1)} %copy-done.7, bf16[5120,640]{1,0:T(8,128)(2,1)S(1)} %copy-done.4, f32[5120,640]{1,0:T(8,128)} %memory_part.4.rest_0_), custom_call_target="tpu_custom_call", output_to_operand_aliasing={{}: (3, {})} | custom-call | flops 1677721600 | bytes 8388608 | tf_op jit(solution)/shard_map/memory_part/pallas_call | solution.py:141
  77.6 2.8 %collective-permute-start.16 = (f32[32,640]{1,0:T(8,128)S(1)}, f32[32,640]{1,0:T(8,128)S(1)}, u32[]{:S(2)}, u32[]{:S(2)}) collective-permute-start(f32[32,640]{1,0:T(8,128)S(1)} %add.41), channel_id=1, source_target_pairs={{0,24},{8,16},{16,8},{24,0},{32,56},{40,48},{48,40},{56,32},{64,88... | collective-permute-start | bytes 245768 | tf_op jit(solution)/shard_map/ppermute | solution.py:323
  80.5 4.0 %memory_part.6.rest_0_ = f32[5120,640]{1,0:T(8,128)} custom-call(bf16[1024,5120]{1,0:T(8,128)(2,1)S(1)} %copy-done.2, bf16[1024,640]{1,0:T(8,128)(2,1)S(1)} %copy-done.7, bf16[5120,640]{1,0:T(8,128)(2,1)S(1)} %copy-done.4, f32[5120,640]{1,0:T(8,128)} %memory_part.5.rest_0_), custom_call_target="tpu_custom_call", output_to_operand_aliasing={{}: (3, {})} | custom-call | flops 1677721600 | bytes 8388608 | tf_op jit(solution)/shard_map/memory_part/pallas_call | solution.py:141
  85.1 4.0 %memory_part.7.mem_ref = f32[5120,640]{1,0:T(8,128)} custom-call(bf16[1024,5120]{1,0:T(8,128)(2,1)S(1)} %copy-done.2, bf16[1024,640]{1,0:T(8,128)(2,1)S(1)} %copy-done.7, bf16[5120,640]{1,0:T(8,128)(2,1)S(1)} %copy-done.4, f32[5120,640]{1,0:T(8,128)} %memory_part.6.rest_0_), custom_call_target="tpu_custom_call", output_to_operand_aliasing={{}: (3, {})} | custom-call | flops 1677721600 | bytes 8388608 | tf_op jit(solution)/shard_map/memory_part/pallas_call | solution.py:141
  89.2 3.1 %collective-permute-start.18 = (f32[32,640]{1,0:T(8,128)S(1)}, f32[32,640]{1,0:T(8,128)S(1)}, u32[]{:S(2)}, u32[]{:S(2)}) collective-permute-start(f32[32,640]{1,0:T(8,128)S(1)} %add.43.a_ref), channel_id=1, source_target_pairs={{0,96},{8,104},{16,112},{24,120},{32,64},{40,72},{48,80},{56,88},{... | collective-permute-start | bytes 245768 | tf_op jit(solution)/shard_map/ppermute | solution.py:323
  92.3 4.3 %orthonormal.1 = (bf16[8,640,128]{2,1,0:T(8,128)(2,1)S(1)}, f32[32,32]{1,0:T(8,128)S(1)}) custom-call(f32[32,640]{1,0:T(8,128)S(1)} %add.40.refs_4_.refs_0_, f32[32,640]{1,0:T(8,128)S(1)} %collective-permute-done.8.refs_4_.refs_1_, f32[32,640]{1,0:T(8,128)S(1)} %collective-permute-done.9.refs_5_.refs_2_, ...), custom_call_target="tpu_custom_call" | custom-call | flops 2147483648 | bytes 2097152 | tf_op jit(solution)/shard_map/orthonormal/pallas_call | solution.py:259
  96.6 4.7 %copy-done.5 = f32[5120,640]{1,0:T(8,128)S(1)} copy-done((f32[5120,640]{1,0:T(8,128)S(1)}, f32[5120,640]{1,0:T(8,128)}, u32[]{:S(2)}) %copy-start.5) | copy-done | bytes 13107224
  101.3 5.7 %update.1 = (bf16[640,32]{1,0:T(8,128)(2,1)S(1)}, bf16[5120,640]{1,0:T(8,128)(2,1)}) custom-call(s32[1]{0:T(128)} %bitcast.t_ref.refs_0_, f32[32,640]{1,0:T(8,128)S(1)} %add.43.a_ref, f32[32,640]{1,0:T(8,128)S(1)} %collective-permute-done.18.b_ref, f32[32,32]{1,0:T(8,128)S(1)} %get-tuple-element.14.inv_ref, s32[640,32]{1,0:T(8,128)S(1)} %copy.11.dither_ref, ...), custom_call_target="tpu_custom_call" | custom-call | flops 1677721600 | bytes 20971520 | tf_op jit(solution)/shard_map/update/pallas_call | solution.py:291
  (47 shorter events, 4.8 us)
Async XLA Ops:
  1.7 4.0 %copy-start = (bf16[1024,5120]{1,0:T(8,128)(2,1)S(1)}, bf16[1024,5120]{1,0:T(8,128)(2,1)}, u32[]{:S(2)}) copy-start(bf16[1024,5120]{1,0:T(8,128)(2,1)} %a_ref.7) | copy-start | bytes 31457284
  5.7 2.9 %copy-start.3 = (bf16[5120,640]{1,0:T(8,128)(2,1)S(1)}, bf16[5120,640]{1,0:T(8,128)(2,1)}, u32[]{:S(2)}) copy-start(bf16[5120,640]{1,0:T(8,128)(2,1)} %e_ref.7) | copy-start | bytes 19660804
  8.6 1.3 %copy-start.6 = (bf16[1024,640]{1,0:T(8,128)(2,1)S(1)}, bf16[1024,640]{1,0:T(8,128)(2,1)}, u32[]{:S(2)}) copy-start(bf16[1024,640]{1,0:T(8,128)(2,1)} %g_ref.7) | copy-start | bytes 3932164
  13.3 33.0 %copy-start.8 = (s32[640,32]{0,1:T(8,128)S(1)}, s32[640,32]{0,1:T(8,128)}, u32[]{:S(2)}) copy-start(s32[640,32]{0,1:T(8,128)} %param.9) | copy-start | bytes 245764
  13.3 40.4 %copy-start.7 = (bf16[1024,640]{1,0:T(8,128)(2,1)S(1)}, bf16[1024,640]{1,0:T(8,128)(2,1)}, u32[]{:S(2)}) copy-start(bf16[1024,640]{1,0:T(8,128)(2,1)} %g_ref.7) | copy-start | bytes 3932164
  13.3 3.0 %collective-permute-start = (f32[4,32,640]{2,1,0:T(8,128)S(1)}, f32[4,32,640]{2,1,0:T(8,128)S(1)}, u32[]{:S(2)}, u32[]{:S(2)}) collective-permute-start(f32[4,32,640]{2,1,0:T(8,128)S(1)} %get-tuple-element.11), channel_id=1, source_target_pairs={{0,1},{1,0},{2,3},{3,2},{4,5},{5,4},{6,7},{7,6},{8,9},{9,8},{10,11... | collective-permute-start | bytes 983048 | tf_op jit(solution)/shard_map/ppermute | solution.py:323
  16.4 5.7 %collective-permute-start.1 = (f32[32,640]{1,0:T(8,128)S(1)}, f32[32,640]{1,0:T(8,128)S(1)}, u32[]{:S(2)}, u32[]{:S(2)}) collective-permute-start(f32[32,640]{1,0:T(8,128)S(1)} %get-tuple-element.18), channel_id=1, source_target_pairs={{0,2},{1,3},{2,0},{3,1},{4,6},{5,7},{6,4},{7,5},{8,10},{9,11},{10,... | collective-permute-start | bytes 245768 | tf_op jit(solution)/shard_map/ppermute | solution.py:323
  18.5 8.2 %collective-permute-start.2 = (f32[32,640]{1,0:T(8,128)S(1)}, f32[32,640]{1,0:T(8,128)S(1)}, u32[]{:S(2)}, u32[]{:S(2)}) collective-permute-start(f32[32,640]{1,0:T(8,128)S(1)} %get-tuple-element.20), channel_id=1, source_target_pairs={{0,4},{1,5},{2,6},{3,7},{4,0},{5,1},{6,2},{7,3},{8,12},{9,13},{10,... | collective-permute-start | bytes 245768 | tf_op jit(solution)/shard_map/ppermute | solution.py:323
  22.1 6.3 %collective-permute-start.3 = (f32[32,640]{1,0:T(8,128)S(1)}, f32[32,640]{1,0:T(8,128)S(1)}, u32[]{:S(2)}, u32[]{:S(2)}) collective-permute-start(f32[32,640]{1,0:T(8,128)S(1)} %get-tuple-element.19), channel_id=1, source_target_pairs={{0,6},{1,7},{2,4},{3,5},{4,2},{5,3},{6,0},{7,1},{8,14},{9,15},{10,... | collective-permute-start | bytes 245768 | tf_op jit(solution)/shard_map/ppermute | solution.py:323
  28.4 4.5 %collective-permute-start.4 = (f32[32,640]{1,0:T(8,128)S(1)}, f32[32,640]{1,0:T(8,128)S(1)}, u32[]{:S(2)}, u32[]{:S(2)}) collective-permute-start(f32[32,640]{1,0:T(8,128)S(1)} %fusion.2), channel_id=1, source_target_pairs={{0,8},{8,0},{16,24},{24,16},{32,40},{40,32},{48,56},{56,48},{64,72... | collective-permute-start | bytes 245768 | tf_op jit(solution)/shard_map/ppermute | solution.py:323
  32.9 5.7 %collective-permute-start.5 = (f32[32,640]{1,0:T(8,128)S(1)}, f32[32,640]{1,0:T(8,128)S(1)}, u32[]{:S(2)}, u32[]{:S(2)}) collective-permute-start(f32[32,640]{1,0:T(8,128)S(1)} %add.37), channel_id=1, source_target_pairs={{0,24},{8,16},{16,8},{24,0},{32,56},{40,48},{48,40},{56,32},{64,88... | collective-permute-start | bytes 245768 | tf_op jit(solution)/shard_map/ppermute | solution.py:323
  38.7 4.5 %collective-permute-start.6 = (f32[32,640]{1,0:T(8,128)S(1)}, f32[32,640]{1,0:T(8,128)S(1)}, u32[]{:S(2)}, u32[]{:S(2)}) collective-permute-start(f32[32,640]{1,0:T(8,128)S(1)} %add.38), channel_id=1, source_target_pairs={{0,32},{8,40},{16,48},{24,56},{32,0},{40,8},{48,16},{56,24},{64,96... | collective-permute-start | bytes 245768 | tf_op jit(solution)/shard_map/ppermute | solution.py:323
  43.2 5.7 %collective-permute-start.7 = (f32[32,640]{1,0:T(8,128)S(1)}, f32[32,640]{1,0:T(8,128)S(1)}, u32[]{:S(2)}, u32[]{:S(2)}) collective-permute-start(f32[32,640]{1,0:T(8,128)S(1)} %add.39), channel_id=1, source_target_pairs={{0,96},{8,104},{16,112},{24,120},{32,64},{40,72},{48,80},{56,88},{... | collective-permute-start | bytes 245768 | tf_op jit(solution)/shard_map/ppermute | solution.py:323
  49.0 15.6 %collective-permute-start.9 = (f32[32,640]{1,0:T(8,128)S(1)}, f32[32,640]{1,0:T(8,128)S(1)}, u32[]{:S(2)}, u32[]{:S(2)}) collective-permute-start(f32[32,640]{1,0:T(8,128)S(1)} %add.40.refs_4_.refs_0_), channel_id=1, source_target_pairs={{0,2},{1,3},{2,0},{3,1},{4,6},{5,7},{6,4},{7,5},{8,10},{9,11},{10,... | collective-permute-start | bytes 245768 | tf_op jit(solution)/shard_map/ppermute | solution.py:323
  49.1 16.0 %collective-permute-start.11 = (f32[32,640]{1,0:T(8,128)S(1)}, f32[32,640]{1,0:T(8,128)S(1)}, u32[]{:S(2)}, u32[]{:S(2)}) collective-permute-start(f32[32,640]{1,0:T(8,128)S(1)} %add.40.refs_4_.refs_0_), channel_id=1, source_target_pairs={{0,4},{1,5},{2,6},{3,7},{4,0},{5,1},{6,2},{7,3},{8,12},{9,13},{10,... | collective-permute-start | bytes 245768 | tf_op jit(solution)/shard_map/ppermute | solution.py:323
  51.0 14.2 %collective-permute-start.13 = (f32[32,640]{1,0:T(8,128)S(1)}, f32[32,640]{1,0:T(8,128)S(1)}, u32[]{:S(2)}, u32[]{:S(2)}) collective-permute-start(f32[32,640]{1,0:T(8,128)S(1)} %add.40.refs_4_.refs_0_), channel_id=1, source_target_pairs={{0,6},{1,7},{2,4},{3,5},{4,2},{5,3},{6,0},{7,1},{8,14},{9,15},{10,... | collective-permute-start | bytes 245768 | tf_op jit(solution)/shard_map/ppermute | solution.py:323
  53.8 4.0 %copy-start.1 = (bf16[1024,5120]{1,0:T(8,128)(2,1)S(1)}, bf16[1024,5120]{1,0:T(8,128)(2,1)}, u32[]{:S(2)}) copy-start(bf16[1024,5120]{1,0:T(8,128)(2,1)} %a_ref.7) | copy-start | bytes 31457284
  57.8 2.9 %copy-start.4 = (bf16[5120,640]{1,0:T(8,128)(2,1)S(1)}, bf16[5120,640]{1,0:T(8,128)(2,1)}, u32[]{:S(2)}) copy-start(bf16[5120,640]{1,0:T(8,128)(2,1)} %e_ref.7) | copy-start | bytes 19660804
  60.6 5.2 %copy-start.2 = (bf16[1024,5120]{1,0:T(8,128)(2,1)S(1)}, bf16[1024,5120]{1,0:T(8,128)(2,1)}, u32[]{:S(2)}) copy-start(bf16[1024,5120]{1,0:T(8,128)(2,1)} %a_ref.7) | copy-start | bytes 31457284
  64.5 4.7 %collective-permute-start.8 = (f32[32,640]{1,0:T(8,128)S(1)}, f32[32,640]{1,0:T(8,128)S(1)}, u32[]{:S(2)}, u32[]{:S(2)}) collective-permute-start(f32[32,640]{1,0:T(8,128)S(1)} %add.40.refs_4_.refs_0_), channel_id=1, source_target_pairs={{0,1},{1,0},{2,3},{3,2},{4,5},{5,4},{6,7},{7,6},{8,9},{9,8},{10,11... | collective-permute-start | bytes 245768 | tf_op jit(solution)/shard_map/ppermute | solution.py:323
  64.5 4.7 %collective-permute-start.10 = (f32[32,640]{1,0:T(8,128)S(1)}, f32[32,640]{1,0:T(8,128)S(1)}, u32[]{:S(2)}, u32[]{:S(2)}) collective-permute-start(f32[32,640]{1,0:T(8,128)S(1)} %collective-permute-done.9.refs_5_.refs_2_), channel_id=1, source_target_pairs={{0,1},{1,0},{2,3},{3,2},{4,5},{5,4},{6,7},{7,6},{8,9},{9,8},{10,11... | collective-permute-start | bytes 245768 | tf_op jit(solution)/shard_map/ppermute | solution.py:323
  65.0 4.2 %collective-permute-start.12 = (f32[32,640]{1,0:T(8,128)S(1)}, f32[32,640]{1,0:T(8,128)S(1)}, u32[]{:S(2)}, u32[]{:S(2)}) collective-permute-start(f32[32,640]{1,0:T(8,128)S(1)} %collective-permute-done.11.refs_6_.refs_4_), channel_id=1, source_target_pairs={{0,1},{1,0},{2,3},{3,2},{4,5},{5,4},{6,7},{7,6},{8,9},{9,8},{10,11... | collective-permute-start | bytes 245768 | tf_op jit(solution)/shard_map/ppermute | solution.py:323
  65.1 4.1 %collective-permute-start.14 = (f32[32,640]{1,0:T(8,128)S(1)}, f32[32,640]{1,0:T(8,128)S(1)}, u32[]{:S(2)}, u32[]{:S(2)}) collective-permute-start(f32[32,640]{1,0:T(8,128)S(1)} %collective-permute-done.13.refs_7_.refs_6_), channel_id=1, source_target_pairs={{0,1},{1,0},{2,3},{3,2},{4,5},{5,4},{6,7},{7,6},{8,9},{9,8},{10,11... | collective-permute-start | bytes 245768 | tf_op jit(solution)/shard_map/ppermute | solution.py:323
  73.1 4.5 %collective-permute-start.15 = (f32[32,640]{1,0:T(8,128)S(1)}, f32[32,640]{1,0:T(8,128)S(1)}, u32[]{:S(2)}, u32[]{:S(2)}) collective-permute-start(f32[32,640]{1,0:T(8,128)S(1)} %right_last.1), channel_id=1, source_target_pairs={{0,8},{8,0},{16,24},{24,16},{32,40},{40,32},{48,56},{56,48},{64,72... | collective-permute-start | bytes 245768 | tf_op jit(solution)/shard_map/ppermute | solution.py:323
  77.6 6.8 %collective-permute-start.16 = (f32[32,640]{1,0:T(8,128)S(1)}, f32[32,640]{1,0:T(8,128)S(1)}, u32[]{:S(2)}, u32[]{:S(2)}) collective-permute-start(f32[32,640]{1,0:T(8,128)S(1)} %add.41), channel_id=1, source_target_pairs={{0,24},{8,16},{16,8},{24,0},{32,56},{40,48},{48,40},{56,32},{64,88... | collective-permute-start | bytes 245768 | tf_op jit(solution)/shard_map/ppermute | solution.py:323
  84.4 4.7 %collective-permute-start.17 = (f32[32,640]{1,0:T(8,128)S(1)}, f32[32,640]{1,0:T(8,128)S(1)}, u32[]{:S(2)}, u32[]{:S(2)}) collective-permute-start(f32[32,640]{1,0:T(8,128)S(1)} %add.42), channel_id=1, source_target_pairs={{0,32},{8,40},{16,48},{24,56},{32,0},{40,8},{48,16},{56,24},{64,96... | collective-permute-start | bytes 245768 | tf_op jit(solution)/shard_map/ppermute | solution.py:323
  89.2 7.4 %collective-permute-start.18 = (f32[32,640]{1,0:T(8,128)S(1)}, f32[32,640]{1,0:T(8,128)S(1)}, u32[]{:S(2)}, u32[]{:S(2)}) collective-permute-start(f32[32,640]{1,0:T(8,128)S(1)} %add.43.a_ref), channel_id=1, source_target_pairs={{0,96},{8,104},{16,112},{24,120},{32,64},{40,72},{48,80},{56,88},{... | collective-permute-start | bytes 245768 | tf_op jit(solution)/shard_map/ppermute | solution.py:323
  96.6 4.7 %copy-start.5 = (f32[5120,640]{1,0:T(8,128)S(1)}, f32[5120,640]{1,0:T(8,128)}, u32[]{:S(2)}) copy-start(f32[5120,640]{1,0:T(8,128)} %memory_part.7.mem_ref) | copy-start | bytes 39321604

commit v2 on v0

v2 whole, which is shorter than its diff:
```python
import jax
import jax.numpy as jnp
from jax import lax
from jax.experimental import pallas as pl
from jax.experimental.pallas import tpu as pltpu
from jax.sharding import PartitionSpec as P

HIGH = lax.Precision.HIGHEST
F32 = jnp.float32
BF16 = jnp.bfloat16

D = 5120
TOK = 1024
COLS = 640
RANK = 32
TRI = 3 * RANK
NBLK = 8
HALF = 4
WORKERS = 16
MB = 1 << 20
RING = (1, 3, 2)

NT = (((1,), (1,)), ((), ()))
TN = (((0,), (0,)), ((), ()))

VM = pl.BlockSpec(memory_space=pltpu.VMEM)
SM = pl.BlockSpec(memory_space=pltpu.SMEM)
ANY = pl.BlockSpec(memory_space=pl.ANY)


def params(mb):
    return pltpu.CompilerParams(vmem_limit_bytes=mb * MB)


def cost(flops, bytes_accessed=0):
    return pl.CostEstimate(flops=flops, bytes_accessed=bytes_accessed, transcendentals=0)


def split3(x):
    hi = x.astype(BF16)
    r = x - hi.astype(F32)
    mid = r.astype(BF16)
    lo = (r - mid.astype(F32)).astype(BF16)
    return jnp.concatenate([hi, mid, lo], axis=0)


def fold3(y):
    return y[:RANK] + y[RANK : 2 * RANK] + y[2 * RANK :]


def left(rc, t, acts, error, out_grad, q_seed, t3=None, qt=None):
    first = t3 is None

    def body(t_ref, acts_hbm, err_hbm, grad_in, seed_in, *rest):
        if first:
            p_ref, acts_v, err_v, grad_v, t3_ref, qt_ref, sem, gsem = rest
        else:
            t3_ref, p_ref, acts_v, err_v, sem = rest
            qt_ref = seed_in

        def columns(k):
            return pl.ds(pl.multiple_of((t_ref[0] ^ (2 * k + rc)) * COLS, COLS), COLS)

        acts_copy = [
            pltpu.make_async_copy(acts_hbm.at[:, columns(k)], acts_v.at[k], sem.at[0, k])
            for k in range(HALF)
        ]
        err_copy = [
            pltpu.make_async_copy(err_hbm.at[columns(k), :], err_v.at[k], sem.at[1, k])
            for k in range(HALF)
        ]
        if first:
            grad_copy = pltpu.make_async_copy(grad_in, grad_v, gsem)
            grad_copy.start()
            err_copy[0].start()
            err_copy[1].start()
            qt_ref[...] = seed_in[...].astype(F32).astype(BF16)
            grad_copy.wait()
            err_copy[2].start()
            err_copy[3].start()
            acts_copy[0].start()
            tt = lax.dot_general(qt_ref[...], grad_v[...], NT, preferred_element_type=F32)
            t3_ref[...] = split3(tt)
        else:
            for k in range(HALF):
                err_copy[k].start()
            acts_copy[0].start()
        for k in range(HALF):
            err_copy[k].wait()
            if k + 1 < HALF:
                acts_copy[k + 1].start()
            p_ref[k] = lax.dot_general(qt_ref[...], err_v[k], NT, preferred_element_type=F32)
        for k in range(HALF):
            acts_copy[k].wait()
            p = fold3(jnp.dot(t3_ref[...], acts_v[k], preferred_element_type=F32))
            p_ref[k] = (p + p_ref[k]) * (1.0 / 32.0)

    out_shape = [
        jax.ShapeDtypeStruct((HALF, RANK, COLS), F32),
        pltpu.VMEM((HALF, TOK, COLS), BF16),
        pltpu.VMEM((HALF, COLS, COLS), BF16),
    ]
    scratch = [pltpu.SemaphoreType.DMA((2, HALF))]
    if first:
        out_shape += [
            pltpu.VMEM((TOK, COLS), BF16),
            pltpu.VMEM((TRI, TOK), BF16),
            pltpu.VMEM((RANK, COLS), BF16),
        ]
        scratch.append(pltpu.SemaphoreType.DMA)
        args = (t, acts, error, out_grad, q_seed)
        in_specs = [SM, ANY, ANY, ANY, VM]
    else:
        args = (t, acts, error, out_grad, qt, t3)
        in_specs = [SM, ANY, ANY, VM, VM, VM]
    return pl.pallas_call(
        body,
        out_shape=out_shape,
        in_specs=in_specs,
        out_specs=[VM] * len(out_shape),
        scratch_shapes=scratch,
        compiler_params=params(44 if first else 40),
        cost_estimate=cost(2 * HALF * 256 * COLS * (TOK + COLS), 9 * MB),
        name="left_first" if first else "left_second",
    )(*args)


def memory_blocks(ks, half, grad_v, after):
    def body(a_ref, e_ref, g_ref, after_ref, *outs):
        for k, out_ref in zip(ks, outs):
            grad = lax.dot_general(a_ref[k], g_ref[...], TN, preferred_element_type=F32)
            out_ref[...] = grad + e_ref[k].astype(F32)

    return pl.pallas_call(
        body,
        out_shape=[pltpu.VMEM((COLS, COLS), F32)] * len(ks),
        in_specs=[VM, VM, VM, ANY],
        out_specs=[VM] * len(ks),
        compiler_params=params(8),
        cost_estimate=cost(2 * len(ks) * COLS * COLS * TOK),
        name="memory_blocks",
    )(*half, grad_v, after)


def right(work, grad_v, halves, earlier=(), last=False):
    n, m = len(work), len(earlier)

    def body(a0, e0, a1, e1, g_ref, *rest):
        acts_v, err_v = (a0, a1), (e0, e1)
        blocks, rest = rest[:n], rest[n:]
        given, outs = rest[: 3 * m], rest[3 * m :]
        tmp = q = gram = 0.0
        for (h, k, _), block in zip(work, blocks):
            p = split3(block[...])
            tmp = tmp + fold3(lax.dot_general(p, acts_v[h][k], NT, preferred_element_type=F32))
            q = q + fold3(jnp.dot(p, err_v[h][k], preferred_element_type=F32))
            gram = gram + lax.dot_general(p, p, NT, preferred_element_type=F32)
        for i in range(m):
            tmp = tmp + given[3 * i][...]
            q = q + given[3 * i + 1][...]
            gram = gram + given[3 * i + 2][...]
        if last:
            q = q + fold3(jnp.dot(split3(tmp), g_ref[...], preferred_element_type=F32))
            outs[0][...] = q
            outs[1][...] = gram
        else:
            outs[0][...] = tmp
            outs[1][...] = q
            outs[2][...] = gram

    shapes = [
        jax.ShapeDtypeStruct((RANK, TOK), F32),
        jax.ShapeDtypeStruct((RANK, COLS), F32),
        jax.ShapeDtypeStruct((TRI, TRI), F32),
    ]
    if last:
        shapes = shapes[1:]
    args = [*halves[0], *halves[1], grad_v, *(b for _, _, b in work), *(x for e in earlier for x in e)]
    return pl.pallas_call(
        body,
        out_shape=shapes,
        in_specs=[VM] * len(args),
        out_specs=[VM] * len(shapes),
        compiler_params=params(8),
        cost_estimate=cost(2 * n * 256 * COLS * (TOK + COLS)),
        name="right_last" if last else "right_part",
    )(*args)


def orthonormal_body(gram_ref, *refs):
    blocks = refs[:NBLK]
    p3_ref, inv_ref = refs[NBLK:]
    wide = fold3(gram_ref[...])
    gram = wide[:, :RANK] + wide[:, RANK : 2 * RANK] + wide[:, 2 * RANK :]
    rows = lax.broadcasted_iota(jnp.int32, (RANK, RANK), 0)
    cols = lax.broadcasted_iota(jnp.int32, (RANK, RANK), 1)
    eye = (rows == cols).astype(F32)
    work = jnp.concatenate([gram, eye], axis=1)
    below = lax.broadcasted_iota(jnp.int32, (RANK, 1), 0)
    for k in range(RANK):
        row = work[k : k + 1, :]
        factor = jnp.where(below > k, work[:, k : k + 1] / row[:, k : k + 1], 0.0)
        work = work - factor * row
    diag = jnp.sum(work[:, :RANK] * eye, axis=1, keepdims=True)
    inv = work[:, RANK:] / jnp.sqrt(diag)
    inv_ref[...] = inv
    for k in range(NBLK):
        p = jnp.dot(inv, blocks[k][...], precision=HIGH, preferred_element_type=F32)
        hi = p.astype(BF16).astype(F32)
        r = p - hi
        mid = r.astype(BF16).astype(F32)
        stacked = jnp.concatenate([hi, mid, r - mid, jnp.zeros_like(p)], axis=0)
        p3_ref[k] = stacked.T.astype(BF16)


def orthonormal(gram, blocks):
    return pl.pallas_call(
        orthonormal_body,
        out_shape=(
            pltpu.VMEM((NBLK, COLS, 4 * RANK), BF16),
            jax.ShapeDtypeStruct((RANK, RANK), F32),
        ),
        in_specs=[VM] * (1 + NBLK),
        out_specs=(VM, VM),
        compiler_params=params(8),
        cost_estimate=cost(1 << 31),
        name="orthonormal",
    )(gram, *blocks)


def update_body(t_ref, a_ref, b_ref, c_ref, d_ref, inv_ref, dither_ref, p3_ref, *rest):
    mem = rest[:NBLK]
    qf_ref, out_hbm, stage, sem = rest[NBLK:]
    total = (a_ref[...] + b_ref[...]) + (c_ref[...] + d_ref[...])
    qmat = jnp.dot(inv_ref[...], total, precision=HIGH, preferred_element_type=F32) / WORKERS
    scale = 1.0 + (dither_ref[...].astype(F32) / 65536.0 - 0.5) / 4.0
    qt = (qmat * scale).astype(BF16)
    qf_ref[...] = qt
    q3 = jnp.concatenate([qt, qt, qt, jnp.zeros((RANK, COLS), BF16)], axis=0)
    copies = []
    for r in range(NBLK):
        approx = jnp.dot(p3_ref[r], q3, preferred_element_type=F32)
        stage[r] = (mem[r][...] - approx).astype(BF16)
        at = pl.ds(pl.multiple_of((t_ref[0] ^ r) * COLS, COLS), COLS)
        copies.append(pltpu.make_async_copy(stage.at[r], out_hbm.at[at, :], sem.at[r]))
        copies[-1].start()
    for c in copies:
        c.wait()


def update(t, parts, inv, dither, p3, memory):
    return pl.pallas_call(
        update_body,
        out_shape=(
            jax.ShapeDtypeStruct((RANK, COLS), BF16),
            jax.ShapeDtypeStruct((D, COLS), BF16),
        ),
        in_specs=[SM] + [VM] * (len(parts) + 3 + NBLK),
        out_specs=(VM, ANY),
        scratch_shapes=[
            pltpu.VMEM((NBLK, COLS, COLS), BF16),
            pltpu.SemaphoreType.DMA((NBLK,)),
        ],
        compiler_params=params(16),
        cost_estimate=cost(2 * D * COLS * 256, 7 * MB),
        name="update",
    )(t, *parts, inv, dither, p3, *memory)


def sum_after(parts, after):
    def body(a, b, c, d, *rest):
        rest[-1][...] = (a[...] + b[...]) + (c[...] + d[...])

    return pl.pallas_call(
        body,
        out_shape=jax.ShapeDtypeStruct(parts[0].shape, F32),
        in_specs=[VM] * 4 + [ANY] * len(after),
        out_specs=VM,
        compiler_params=params(8),
        cost_estimate=cost(1000),
        name="sum_after",
    )(*parts, *after)


def swap(x, axis, size, mask):
    return lax.ppermute(x, axis, [(i, i ^ mask) for i in range(size)])


def per_device(acts, out_grad, error, q_seed, dither):
    t = lax.axis_index("tensor").astype(jnp.int32).reshape(1)

    def core(x):
        return swap(x, "tensor", NBLK, 1)

    def ring_z(x, r):
        return swap(x, "tensor", NBLK, 2 * r)

    def ring_x(x):
        return [swap(x, "dp", WORKERS, r) for r in RING]

    def ring_y(x):
        return [swap(x, "dp", WORKERS, 4 * r) for r in RING]

    away, acts_1, err_1, grad_v, t3, qt = left(1, t, acts, error, out_grad, q_seed.T)
    came = core(away)
    kept, acts_0, err_0 = left(0, t, acts, error, grad_v, None, t3, qt)
    part = kept + came
    halves = ((acts_0, err_0), (acts_1, err_1))
    from_z = [ring_z(part[r], r) for r in RING]
    even = memory_blocks((0, 1, 2), halves[0], grad_v, part)
    own = sum_after([part[0], *from_z], even[:1])

    from_x = ring_x(own)
    odd = memory_blocks((0, 1, 2), halves[1], grad_v, own)
    own = sum_after([own, *from_x], odd[:1])
    from_y = ring_y(own)
    even += memory_blocks((3,), halves[0], grad_v, own)
    odd += memory_blocks((3,), halves[1], grad_v, own)
    own = sum_after([own, *from_y], [even[3], odd[3]])

    mine, theirs = {0: own}, {0: core(own)}
    for r in RING:
        mine[r] = ring_z(own, r)
        theirs[r] = core(mine[r])
    early = right([(0, 0, mine[0]), (1, 0, theirs[0])], grad_v, halves)
    mid = right([(0, r, mine[r]) for r in RING], grad_v, halves, (early,))
    q, gram = right([(1, r, theirs[r]) for r in RING], grad_v, halves, (mid,), True)

    from_x = ring_x(q)
    p3, inv = orthonormal(gram, [b[r] for r in range(HALF) for b in (mine, theirs)])
    q = sum_after([q, *from_x], [inv])
    memory = [m[k] for k in range(HALF) for m in (even, odd)]
    q_factor, new_error = update(t, [q, *ring_y(q)], inv, dither.T, p3, memory)
    return (q_factor.T, new_error)


def solution(mesh):
    in_specs = (
        P("dp", None),
        P("dp", "tensor"),
        P("dp", "tensor"),
        P("tensor", None),
        P("tensor", None),
    )
    out_specs = (P("tensor", None), P("dp", "tensor"))
    return jax.shard_map(
        per_device, mesh=mesh, in_specs=in_specs, out_specs=out_specs, check_vma=False
    )
```

time: 306 us -> 74.8 us (0.24)
  waiting for transfers between devices: 227 us -> 13 us
  matrix products: 51.2 us -> 0 us
  Pallas kernels: 0 us -> 32.4 us
  starting transfers between devices: 0.08 us -> 27.3 us
  between operations: 14.1 us -> 0.97 us
  other arithmetic: 7.6 us -> 0.05 us
  local copies, waits for them, and re-layouts: 6 us -> 0.91 us
    psum x2 -> x0, waiting for transfers between devices: 227 us -> none  [the longest x1 147 us: per_device(): pmat = lax.psum(p_local, ('dp', 'tensor'))]
    dot_general x5 -> x0, matrix products: 49.4 us -> none  [the longest x1 13.3 us: per_device(): p_local = jnp.dot(memory, q_start, precision=HIGH)]
    pallas_call x0 -> x15, Pallas kernels: none -> 32.4 us  [the longest x2 10.3 us: left(): pl.pallas_call(body, out_shape=out_shape, in_specs=in_specs, out_specs=[V...]
    ppermute x0 -> x23, starting transfers between devices: none -> 27.3 us  [swap(): return lax.ppermute(x, axis, [(i, i ^ mask) for i in range(size)])]
    ppermute x0 -> x23, waiting for transfers between devices: none -> 13 us  [swap(): return lax.ppermute(x, axis, [(i, i ^ mask) for i in range(size)])]
    another operation x5 -> x0, other arithmetic: 6.68 us -> none  [the longest x3 3.6 us: orthonormal(): lower = jnp.linalg.cholesky(gram)]
    unnamed x10 -> x4, local copies, waits for them, and re-layouts: 5.93 us -> 0.88 us
  transfers between devices with their start and end apart: 2 -> 23, of which waited for: 2 -> 11; matrix products, arithmetic and copies ran while one was open for 0% -> 0% of each run, Pallas kernels for 0% -> 27%
where the time goes in v2:
time: 74.8 us; the launch traced here: 74.6 us
  Pallas kernels  32.4 us (43%)
  starting transfers between devices  27.3 us (36%)
  waiting for transfers between devices  13 us (17%)
  between operations  0.97 us (1%)
  local copies, waits for them, and re-layouts  0.91 us (1%)
    ppermute x23, starting transfers between devices, swap(): return lax.ppermute(x, axis, [(i, i ^ mask) for i in range(size)])  27.3 us
    ppermute x23, waiting for transfers between devices, swap(): return lax.ppermute(x, axis, [(i, i ^ mask) for i in range(size)])  13 us
    pallas_call x2, Pallas kernels, left(): pl.pallas_call(body, out_shape=out_shape, in_specs=in_specs, out_specs=[V...  10.3 us
    pallas_call x4, Pallas kernels, memory_blocks(): pl.pallas_call(body, out_shape=[pltpu.VMEM((COLS, COLS), F32)] * len(ks),...  9.08 us
    pallas_call x3, Pallas kernels, right(): pl.pallas_call(body, out_shape=shapes, in_specs=[VM] * len(args), out_spe...  5.26 us
    pallas_call x1, Pallas kernels, update(): pl.pallas_call(update_body, out_shape=(jax.ShapeDtypeStruct((RANK, COLS),...  4.06 us
    pallas_call x1, Pallas kernels, orthonormal(): pl.pallas_call(orthonormal_body, out_shape=(pltpu.VMEM((NBLK, COLS, 4 * R...  3.62 us
  transfers between devices with their start and end apart: 23, of which 11 were waited for; matrix products, arithmetic and copies ran while one was open for 0% of the time, Pallas kernels for 27%

profile of v2, /device:TPU:0, one launch (start us, length us, event | category | flops | bytes accessed | tf_op | source)
XLA Modules:
  0.0 74.6 jit_solution(13404512275224324426)
XLA Ops:
  0.6 0.9 %copy-done = s32[640,32]{0,1:T(8,128)S(1)} copy-done((s32[640,32]{0,1:T(8,128)S(1)}, s32[640,32]{0,1:T(8,128)}, u32[]{:S(2)}) %copy-start) | copy-done | bytes 81944
  1.5 6.1 %left_first.1 = (f32[4,32,640]{2,1,0:T(8,128)}, bf16[4,1024,640]{2,1,0:T(8,128)(2,1)S(1)}, bf16[4,640,640]{2,1,0:T(8,128)(2,1)S(1)}, bf16[1024,640]{1,0:T(8,128)...) custom-call(s32[1]{0:T(128)} %bitcast.t_ref, bf16[1024,5120]{1,0:T(8,128)(2,1)} %acts_hbm.3, ...), custom_call_target="tpu_custom_call" | custom-call | flops 2181038080 | bytes 9437184 | tf_op jit(solution)/shard_map/left_first/pallas_call | solution.py:116
  7.7 4.3 %left_second.1 = (f32[4,32,640]{2,1,0:T(8,128)S(1)}, bf16[4,1024,640]{2,1,0:T(8,128)(2,1)S(1)}, bf16[4,640,640]{2,1,0:T(8,128)(2,1)S(1)}) custom-call(s32[1]{0:T(128)} %bitcast.t_ref, bf16[1024,5120]{1,0:T(8,128)(2,1)} %acts_hbm.3, bf16[5120,640]{1,0:T(8,128)(2,1)} %err_hbm.3, bf16[1024,640]{1,0:T(8,128)(2,1)S(1)} %get-tuple-element.29.grad_in.g_ref, ...), custom_call_target="tpu_custom_call" | custom-call | flops 2181038080 | bytes 9437184 | tf_op jit(solution)/shard_map/left_second/pallas_call | solution.py:116
  12.0 2.1 %collective-permute-start.1 = (f32[32,640]{1,0:T(8,128)S(1)}, f32[32,640]{1,0:T(8,128)S(1)}, u32[]{:S(2)}, u32[]{:S(2)}) collective-permute-start(f32[32,640]{1,0:T(8,128)S(1)} %get-tuple-element.58), channel_id=1, source_target_pairs={{0,2},{1,3},{2,0},{3,1},{4,6},{5,7},{6,4},{7,5},{8,10},{9,11},{10,... | collective-permute-start | bytes 245768 | tf_op jit(solution)/shard_map/ppermute | solution.py:286
  14.1 2.5 %collective-permute-start.2 = (f32[32,640]{1,0:T(8,128)S(1)}, f32[32,640]{1,0:T(8,128)S(1)}, u32[]{:S(2)}, u32[]{:S(2)}) collective-permute-start(f32[32,640]{1,0:T(8,128)S(1)} %get-tuple-element.57), channel_id=1, source_target_pairs={{0,6},{1,7},{2,4},{3,5},{4,2},{5,3},{6,0},{7,1},{8,14},{9,15},{10,... | collective-permute-start | bytes 245768 | tf_op jit(solution)/shard_map/ppermute | solution.py:286
  16.7 1.1 %collective-permute-start.3 = (f32[32,640]{1,0:T(8,128)S(1)}, f32[32,640]{1,0:T(8,128)S(1)}, u32[]{:S(2)}, u32[]{:S(2)}) collective-permute-start(f32[32,640]{1,0:T(8,128)S(1)} %get-tuple-element.56), channel_id=1, source_target_pairs={{0,4},{1,5},{2,6},{3,7},{4,0},{5,1},{6,2},{7,3},{8,12},{9,13},{10,... | collective-permute-start | bytes 245768 | tf_op jit(solution)/shard_map/ppermute | solution.py:286
  17.7 3.3 %memory_blocks.4 = (f32[640,640]{1,0:T(8,128)S(1)}, f32[640,640]{1,0:T(8,128)S(1)}, f32[640,640]{1,0:T(8,128)S(1)}) custom-call(bf16[4,1024,640]{2,1,0:T(8,128)(2,1)S(1)} %get-tuple-element.32.a_ref.a0, bf16[4,640,640]{2,1,0:T(8,128)(2,1)S(1)} %get-tuple-element.33.e_ref.e0, bf16[1024,640]{1,0:T(8,128)(2,1)S(1)} %get-tuple-element.29.grad_in.g_ref, ...), custom_call_target="tpu_custom_call" | custom-call | flops 2516582400 | tf_op jit(solution)/shard_map/memory_blocks/pallas_call | solution.py:134
  21.0 1.6 %collective-permute-done.3.d = f32[32,640]{1,0:T(8,128)S(1)} collective-permute-done((f32[32,640]{1,0:T(8,128)S(1)}, f32[32,640]{1,0:T(8,128)S(1)}, u32[]{:S(2)}, u32[]{:S(2)}) %collective-permute-start.3) | collective-permute-done | bytes 81952 | tf_op jit(solution)/shard_map/ppermute | solution.py:286
  22.6 1.6 %collective-permute-start.4 = (f32[32,640]{1,0:T(8,128)S(1)}, f32[32,640]{1,0:T(8,128)S(1)}, u32[]{:S(2)}, u32[]{:S(2)}) collective-permute-start(f32[32,640]{1,0:T(8,128)S(1)} %sum_after.4.after_ref.a), channel_id=1, source_target_pairs={{0,8},{8,0},{16,24},{24,16},{32,40},{40,32},{48,56},{56,48},{64,72... | collective-permute-start | bytes 245768 | tf_op jit(solution)/shard_map/ppermute | solution.py:286
  24.2 2.1 %collective-permute-start.5 = (f32[32,640]{1,0:T(8,128)S(1)}, f32[32,640]{1,0:T(8,128)S(1)}, u32[]{:S(2)}, u32[]{:S(2)}) collective-permute-start(f32[32,640]{1,0:T(8,128)S(1)} %sum_after.4.after_ref.a), channel_id=1, source_target_pairs={{0,24},{8,16},{16,8},{24,0},{32,56},{40,48},{48,40},{56,32},{64,88... | collective-permute-start | bytes 245768 | tf_op jit(solution)/shard_map/ppermute | solution.py:286
  26.9 3.3 %memory_blocks.5 = (f32[640,640]{1,0:T(8,128)S(1)}, f32[640,640]{1,0:T(8,128)S(1)}, f32[640,640]{1,0:T(8,128)S(1)}) custom-call(bf16[4,1024,640]{2,1,0:T(8,128)(2,1)S(1)} %get-tuple-element.34.a_ref.a1, bf16[4,640,640]{2,1,0:T(8,128)(2,1)S(1)} %get-tuple-element.35.e_ref.e1, bf16[1024,640]{1,0:T(8,128)(2,1)S(1)} %get-tuple-element.29.grad_in.g_ref, ...), custom_call_target="tpu_custom_call" | custom-call | flops 2516582400 | tf_op jit(solution)/shard_map/memory_blocks/pallas_call | solution.py:134
  30.5 1.7 %collective-permute-done.6.d = f32[32,640]{1,0:T(8,128)S(1)} collective-permute-done((f32[32,640]{1,0:T(8,128)S(1)}, f32[32,640]{1,0:T(8,128)S(1)}, u32[]{:S(2)}, u32[]{:S(2)}) %collective-permute-start.6) | collective-permute-done | bytes 81952 | tf_op jit(solution)/shard_map/ppermute | solution.py:286
  32.3 1.7 %collective-permute-start.7 = (f32[32,640]{1,0:T(8,128)S(1)}, f32[32,640]{1,0:T(8,128)S(1)}, u32[]{:S(2)}, u32[]{:S(2)}) collective-permute-start(f32[32,640]{1,0:T(8,128)S(1)} %sum_after.5.after_ref.a), channel_id=1, source_target_pairs={{0,32},{8,40},{16,48},{24,56},{32,0},{40,8},{48,16},{56,24},{64,96... | collective-permute-start | bytes 245768 | tf_op jit(solution)/shard_map/ppermute | solution.py:286
  33.9 2.2 %collective-permute-start.8 = (f32[32,640]{1,0:T(8,128)S(1)}, f32[32,640]{1,0:T(8,128)S(1)}, u32[]{:S(2)}, u32[]{:S(2)}) collective-permute-start(f32[32,640]{1,0:T(8,128)S(1)} %sum_after.5.after_ref.a), channel_id=1, source_target_pairs={{0,96},{8,104},{16,112},{24,120},{32,64},{40,72},{48,80},{56,88},{... | collective-permute-start | bytes 245768 | tf_op jit(solution)/shard_map/ppermute | solution.py:286
  36.8 1.2 %memory_blocks.7.rest_1_.rest_7_ = f32[640,640]{1,0:T(8,128)S(1)} custom-call(bf16[4,1024,640]{2,1,0:T(8,128)(2,1)S(1)} %get-tuple-element.34.a_ref.a1, bf16[4,640,640]{2,1,0:T(8,128)(2,1)S(1)} %get-tuple-element.35.e_ref.e1, bf16[1024,640]{1,0:T(8,128)(2,1)S(1)} %get-tuple-element.29.grad_in.g_ref, f32[32,640]{1,0:T(8,128)S(1)} %sum_after.5.after_ref.a), custom_call_target="tpu_custom_call" | custom-call | flops 838860800 | tf_op jit(solution)/shard_map/memory_blocks/pallas_call | solution.py:134
  38.0 1.2 %memory_blocks.6.rest_0_.rest_6_ = f32[640,640]{1,0:T(8,128)S(1)} custom-call(bf16[4,1024,640]{2,1,0:T(8,128)(2,1)S(1)} %get-tuple-element.32.a_ref.a0, bf16[4,640,640]{2,1,0:T(8,128)(2,1)S(1)} %get-tuple-element.33.e_ref.e0, bf16[1024,640]{1,0:T(8,128)(2,1)S(1)} %get-tuple-element.29.grad_in.g_ref, f32[32,640]{1,0:T(8,128)S(1)} %sum_after.5.after_ref.a), custom_call_target="tpu_custom_call" | custom-call | flops 838860800 | tf_op jit(solution)/shard_map/memory_blocks/pallas_call | solution.py:134
  39.6 2.5 %collective-permute-done.9.d = f32[32,640]{1,0:T(8,128)S(1)} collective-permute-done((f32[32,640]{1,0:T(8,128)S(1)}, f32[32,640]{1,0:T(8,128)S(1)}, u32[]{:S(2)}, u32[]{:S(2)}) %collective-permute-start.9) | collective-permute-done | bytes 81952 | tf_op jit(solution)/shard_map/ppermute | solution.py:286
  42.0 1.1 %collective-permute-start.10 = (f32[32,640]{1,0:T(8,128)S(1)}, f32[32,640]{1,0:T(8,128)S(1)}, u32[]{:S(2)}, u32[]{:S(2)}) collective-permute-start(f32[32,640]{1,0:T(8,128)S(1)} %sum_after.6.rest_0_.refs_0_), channel_id=1, source_target_pairs={{0,2},{1,3},{2,0},{3,1},{4,6},{5,7},{6,4},{7,5},{8,10},{9,11},{10,... | collective-permute-start | bytes 245768 | tf_op jit(solution)/shard_map/ppermute | solution.py:286
  43.2 1.0 %collective-permute-start.12 = (f32[32,640]{1,0:T(8,128)S(1)}, f32[32,640]{1,0:T(8,128)S(1)}, u32[]{:S(2)}, u32[]{:S(2)}) collective-permute-start(f32[32,640]{1,0:T(8,128)S(1)} %sum_after.6.rest_0_.refs_0_), channel_id=1, source_target_pairs={{0,6},{1,7},{2,4},{3,5},{4,2},{5,3},{6,0},{7,1},{8,14},{9,15},{10,... | collective-permute-start | bytes 245768 | tf_op jit(solution)/shard_map/ppermute | solution.py:286
  44.1 2.1 %collective-permute-start.14 = (f32[32,640]{1,0:T(8,128)S(1)}, f32[32,640]{1,0:T(8,128)S(1)}, u32[]{:S(2)}, u32[]{:S(2)}) collective-permute-start(f32[32,640]{1,0:T(8,128)S(1)} %sum_after.6.rest_0_.refs_0_), channel_id=1, source_target_pairs={{0,4},{1,5},{2,6},{3,7},{4,0},{5,1},{6,2},{7,3},{8,12},{9,13},{10,... | collective-permute-start | bytes 245768 | tf_op jit(solution)/shard_map/ppermute | solution.py:286
  46.6 2.3 %collective-permute-done.12.rest_1_.refs_6_ = f32[32,640]{1,0:T(8,128)S(1)} collective-permute-done((f32[32,640]{1,0:T(8,128)S(1)}, f32[32,640]{1,0:T(8,128)S(1)}, u32[]{:S(2)}, u32[]{:S(2)}) %collective-permute-start.12) | collective-permute-done | bytes 81952 | tf_op jit(solution)/shard_map/ppermute | solution.py:286
  48.8 1.3 %right_part.2 = (f32[32,1024]{1,0:T(8,128)S(1)}, f32[32,640]{1,0:T(8,128)S(1)}, f32[96,96]{1,0:T(8,128)S(1)}) custom-call(bf16[4,1024,640]{2,1,0:T(8,128)(2,1)S(1)} %get-tuple-element.32.a_ref.a0, bf16[4,640,640]{2,1,0:T(8,128)(2,1)S(1)} %get-tuple-element.33.e_ref.e0, bf16[4,1024,640]{2,1,0:T(8,128)(2,1)S(1)} %get-tuple-element.34.a_ref.a1, ...), custom_call_target="tpu_custom_call" | custom-call | flops 1090519040 | tf_op jit(solution)/shard_map/right_part/pallas_call | solution.py:179
  50.7 1.9 %right_part.3 = (f32[32,1024]{1,0:T(8,128)S(1)}, f32[32,640]{1,0:T(8,128)S(1)}, f32[96,96]{1,0:T(8,128)S(1)}) custom-call(bf16[4,1024,640]{2,1,0:T(8,128)(2,1)S(1)} %get-tuple-element.32.a_ref.a0, bf16[4,640,640]{2,1,0:T(8,128)(2,1)S(1)} %get-tuple-element.33.e_ref.e0, bf16[4,1024,640]{2,1,0:T(8,128)(2,1)S(1)} %get-tuple-element.34.a_ref.a1, ...), custom_call_target="tpu_custom_call" | custom-call | flops 1635778560 | tf_op jit(solution)/shard_map/right_part/pallas_call | solution.py:179
  52.6 2.1 %right_last.1 = (f32[32,640]{1,0:T(8,128)S(1)}, f32[96,96]{1,0:T(8,128)S(1)}) custom-call(bf16[4,1024,640]{2,1,0:T(8,128)(2,1)S(1)} %get-tuple-element.32.a_ref.a0, bf16[4,640,640]{2,1,0:T(8,128)(2,1)S(1)} %get-tuple-element.33.e_ref.e0, bf16[4,1024,640]{2,1,0:T(8,128)(2,1)S(1)} %get-tuple-element.34.a_ref.a1, ...), custom_call_target="tpu_custom_call" | custom-call | flops 1635778560 | tf_op jit(solution)/shard_map/right_last/pallas_call | solution.py:179
  55.4 0.9 %collective-permute-start.18 = (f32[32,640]{1,0:T(8,128)S(1)}, f32[32,640]{1,0:T(8,128)S(1)}, u32[]{:S(2)}, u32[]{:S(2)}) collective-permute-start(f32[32,640]{1,0:T(8,128)S(1)} %get-tuple-element.46.a), channel_id=1, source_target_pairs={{0,24},{8,16},{16,8},{24,0},{32,56},{40,48},{48,40},{56,32},{64,88... | collective-permute-start | bytes 245768 | tf_op jit(solution)/shard_map/ppermute | solution.py:286
  56.3 2.6 %collective-permute-start.19 = (f32[32,640]{1,0:T(8,128)S(1)}, f32[32,640]{1,0:T(8,128)S(1)}, u32[]{:S(2)}, u32[]{:S(2)}) collective-permute-start(f32[32,640]{1,0:T(8,128)S(1)} %get-tuple-element.46.a), channel_id=1, source_target_pairs={{0,16},{8,24},{16,0},{24,8},{32,48},{40,56},{48,32},{56,40},{64,80... | collective-permute-start | bytes 245768 | tf_op jit(solution)/shard_map/ppermute | solution.py:286
  58.9 3.6 %orthonormal.1 = (bf16[8,640,128]{2,1,0:T(8,128)(2,1)S(1)}, f32[32,32]{1,0:T(8,128)S(1)}) custom-call(f32[96,96]{1,0:T(8,128)S(1)} %get-tuple-element.47.gram_ref, f32[32,640]{1,0:T(8,128)S(1)} %sum_after.6.rest_0_.refs_0_, f32[32,640]{1,0:T(8,128)S(1)} %collective-permute-done.16.rest_1_.refs_1_, f32[32,640]{1,0:T(8,128)S(1)} %collective-permute-done.10.rest_0_.refs_2_, ...), custom_call_target="tpu_custom_call" | custom-call | flops 2147483648 | tf_op jit(solution)/shard_map/orthonormal/pallas_call | solution.py:217
  62.8 0.7 collective-permute-start.20
  64.2 2.8 %collective-permute-start.22 = (f32[32,640]{1,0:T(8,128)S(1)}, f32[32,640]{1,0:T(8,128)S(1)}, u32[]{:S(2)}, u32[]{:S(2)}) collective-permute-start(f32[32,640]{1,0:T(8,128)S(1)} %sum_after.7.a_ref), channel_id=1, source_target_pairs={{0,64},{8,72},{16,80},{24,88},{32,96},{40,104},{48,112},{56,120},{... | collective-permute-start | bytes 245768 | tf_op jit(solution)/shard_map/ppermute | solution.py:286
  67.0 0.8 %collective-permute-done.20.b_ref = f32[32,640]{1,0:T(8,128)S(1)} collective-permute-done((f32[32,640]{1,0:T(8,128)S(1)}, f32[32,640]{1,0:T(8,128)S(1)}, u32[]{:S(2)}, u32[]{:S(2)}) %collective-permute-start.20) | collective-permute-done | bytes 81952 | tf_op jit(solution)/shard_map/ppermute | solution.py:286
  67.8 2.5 %collective-permute-done.21.c_ref = f32[32,640]{1,0:T(8,128)S(1)} collective-permute-done((f32[32,640]{1,0:T(8,128)S(1)}, f32[32,640]{1,0:T(8,128)S(1)}, u32[]{:S(2)}, u32[]{:S(2)}) %collective-permute-start.21) | collective-permute-done | bytes 81952 | tf_op jit(solution)/shard_map/ppermute | solution.py:286
  70.4 4.1 %update.1 = (bf16[32,640]{1,0:T(8,128)(2,1)}, bf16[5120,640]{1,0:T(8,128)(2,1)}) custom-call(s32[1]{0:T(128)} %bitcast.t_ref, f32[32,640]{1,0:T(8,128)S(1)} %sum_after.7.a_ref, f32[32,640]{1,0:T(8,128)S(1)} %collective-permute-done.20.b_ref, f32[32,640]{1,0:T(8,128)S(1)} %collective-permute-done.21.c_ref, f32[32,640]{1,0:T(8,128)S(1)} %collective-permute-done.22.d_ref, ...), custom_call_target="tpu_custom_call" | custom-call | flops 1677721600 | bytes 7340032 | tf_op jit(solution)/shard_map/update/pallas_call | solution.py:252
  (35 shorter events, 4.7 us)
Async XLA Ops:
  0.6 0.9 %copy-start = (s32[640,32]{0,1:T(8,128)S(1)}, s32[640,32]{0,1:T(8,128)}, u32[]{:S(2)}) copy-start(s32[640,32]{0,1:T(8,128)} %param.8) | copy-start | bytes 245764
  7.6 4.4 %collective-permute-start = (f32[4,32,640]{2,1,0:T(8,128)}, f32[4,32,640]{2,1,0:T(8,128)S(1)}, u32[]{:S(2)}, u32[]{:S(2)}) collective-permute-start(f32[4,32,640]{2,1,0:T(8,128)} %get-tuple-element.37), channel_id=1, source_target_pairs={{0,1},{1,0},{2,3},{3,2},{4,5},{5,4},{6,7},{7,6},{8,9},{9,8},{10,11... | collective-permute-start | bytes 983048 | tf_op jit(solution)/shard_map/ppermute | solution.py:286
  12.0 9.0 %collective-permute-start.1 = (f32[32,640]{1,0:T(8,128)S(1)}, f32[32,640]{1,0:T(8,128)S(1)}, u32[]{:S(2)}, u32[]{:S(2)}) collective-permute-start(f32[32,640]{1,0:T(8,128)S(1)} %get-tuple-element.58), channel_id=1, source_target_pairs={{0,2},{1,3},{2,0},{3,1},{4,6},{5,7},{6,4},{7,5},{8,10},{9,11},{10,... | collective-permute-start | bytes 245768 | tf_op jit(solution)/shard_map/ppermute | solution.py:286
  14.1 6.9 %collective-permute-start.2 = (f32[32,640]{1,0:T(8,128)S(1)}, f32[32,640]{1,0:T(8,128)S(1)}, u32[]{:S(2)}, u32[]{:S(2)}) collective-permute-start(f32[32,640]{1,0:T(8,128)S(1)} %get-tuple-element.57), channel_id=1, source_target_pairs={{0,6},{1,7},{2,4},{3,5},{4,2},{5,3},{6,0},{7,1},{8,14},{9,15},{10,... | collective-permute-start | bytes 245768 | tf_op jit(solution)/shard_map/ppermute | solution.py:286
  16.7 5.9 %collective-permute-start.3 = (f32[32,640]{1,0:T(8,128)S(1)}, f32[32,640]{1,0:T(8,128)S(1)}, u32[]{:S(2)}, u32[]{:S(2)}) collective-permute-start(f32[32,640]{1,0:T(8,128)S(1)} %get-tuple-element.56), channel_id=1, source_target_pairs={{0,4},{1,5},{2,6},{3,7},{4,0},{5,1},{6,2},{7,3},{8,12},{9,13},{10,... | collective-permute-start | bytes 245768 | tf_op jit(solution)/shard_map/ppermute | solution.py:286
  22.6 7.6 %collective-permute-start.4 = (f32[32,640]{1,0:T(8,128)S(1)}, f32[32,640]{1,0:T(8,128)S(1)}, u32[]{:S(2)}, u32[]{:S(2)}) collective-permute-start(f32[32,640]{1,0:T(8,128)S(1)} %sum_after.4.after_ref.a), channel_id=1, source_target_pairs={{0,8},{8,0},{16,24},{24,16},{32,40},{40,32},{48,56},{56,48},{64,72... | collective-permute-start | bytes 245768 | tf_op jit(solution)/shard_map/ppermute | solution.py:286
  24.2 6.3 %collective-permute-start.5 = (f32[32,640]{1,0:T(8,128)S(1)}, f32[32,640]{1,0:T(8,128)S(1)}, u32[]{:S(2)}, u32[]{:S(2)}) collective-permute-start(f32[32,640]{1,0:T(8,128)S(1)} %sum_after.4.after_ref.a), channel_id=1, source_target_pairs={{0,24},{8,16},{16,8},{24,0},{32,56},{40,48},{48,40},{56,32},{64,88... | collective-permute-start | bytes 245768 | tf_op jit(solution)/shard_map/ppermute | solution.py:286
  26.3 5.9 %collective-permute-start.6 = (f32[32,640]{1,0:T(8,128)S(1)}, f32[32,640]{1,0:T(8,128)S(1)}, u32[]{:S(2)}, u32[]{:S(2)}) collective-permute-start(f32[32,640]{1,0:T(8,128)S(1)} %sum_after.4.after_ref.a), channel_id=1, source_target_pairs={{0,16},{8,24},{16,0},{24,8},{32,48},{40,56},{48,32},{56,40},{64,80... | collective-permute-start | bytes 245768 | tf_op jit(solution)/shard_map/ppermute | solution.py:286
  32.3 7.0 %collective-permute-start.7 = (f32[32,640]{1,0:T(8,128)S(1)}, f32[32,640]{1,0:T(8,128)S(1)}, u32[]{:S(2)}, u32[]{:S(2)}) collective-permute-start(f32[32,640]{1,0:T(8,128)S(1)} %sum_after.5.after_ref.a), channel_id=1, source_target_pairs={{0,32},{8,40},{16,48},{24,56},{32,0},{40,8},{48,16},{56,24},{64,96... | collective-permute-start | bytes 245768 | tf_op jit(solution)/shard_map/ppermute | solution.py:286
  33.9 5.7 %collective-permute-start.8 = (f32[32,640]{1,0:T(8,128)S(1)}, f32[32,640]{1,0:T(8,128)S(1)}, u32[]{:S(2)}, u32[]{:S(2)}) collective-permute-start(f32[32,640]{1,0:T(8,128)S(1)} %sum_after.5.after_ref.a), channel_id=1, source_target_pairs={{0,96},{8,104},{16,112},{24,120},{32,64},{40,72},{48,80},{56,88},{... | collective-permute-start | bytes 245768 | tf_op jit(solution)/shard_map/ppermute | solution.py:286
  36.1 5.9 %collective-permute-start.9 = (f32[32,640]{1,0:T(8,128)S(1)}, f32[32,640]{1,0:T(8,128)S(1)}, u32[]{:S(2)}, u32[]{:S(2)}) collective-permute-start(f32[32,640]{1,0:T(8,128)S(1)} %sum_after.5.after_ref.a), channel_id=1, source_target_pairs={{0,64},{8,72},{16,80},{24,88},{32,96},{40,104},{48,112},{56,120},{... | collective-permute-start | bytes 245768 | tf_op jit(solution)/shard_map/ppermute | solution.py:286
  42.0 4.5 %collective-permute-start.10 = (f32[32,640]{1,0:T(8,128)S(1)}, f32[32,640]{1,0:T(8,128)S(1)}, u32[]{:S(2)}, u32[]{:S(2)}) collective-permute-start(f32[32,640]{1,0:T(8,128)S(1)} %sum_after.6.rest_0_.refs_0_), channel_id=1, source_target_pairs={{0,2},{1,3},{2,0},{3,1},{4,6},{5,7},{6,4},{7,5},{8,10},{9,11},{10,... | collective-permute-start | bytes 245768 | tf_op jit(solution)/shard_map/ppermute | solution.py:286
  43.2 5.7 %collective-permute-start.12 = (f32[32,640]{1,0:T(8,128)S(1)}, f32[32,640]{1,0:T(8,128)S(1)}, u32[]{:S(2)}, u32[]{:S(2)}) collective-permute-start(f32[32,640]{1,0:T(8,128)S(1)} %sum_after.6.rest_0_.refs_0_), channel_id=1, source_target_pairs={{0,6},{1,7},{2,4},{3,5},{4,2},{5,3},{6,0},{7,1},{8,14},{9,15},{10,... | collective-permute-start | bytes 245768 | tf_op jit(solution)/shard_map/ppermute | solution.py:286
  44.1 4.7 %collective-permute-start.16 = (f32[32,640]{1,0:T(8,128)S(1)}, f32[32,640]{1,0:T(8,128)S(1)}, u32[]{:S(2)}, u32[]{:S(2)}) collective-permute-start(f32[32,640]{1,0:T(8,128)S(1)} %sum_after.6.rest_0_.refs_0_), channel_id=1, source_target_pairs={{0,1},{1,0},{2,3},{3,2},{4,5},{5,4},{6,7},{7,6},{8,9},{9,8},{10,11... | collective-permute-start | bytes 245768 | tf_op jit(solution)/shard_map/ppermute | solution.py:286
  44.1 6.4 %collective-permute-start.14 = (f32[32,640]{1,0:T(8,128)S(1)}, f32[32,640]{1,0:T(8,128)S(1)}, u32[]{:S(2)}, u32[]{:S(2)}) collective-permute-start(f32[32,640]{1,0:T(8,128)S(1)} %sum_after.6.rest_0_.refs_0_), channel_id=1, source_target_pairs={{0,4},{1,5},{2,6},{3,7},{4,0},{5,1},{6,2},{7,3},{8,12},{9,13},{10,... | collective-permute-start | bytes 245768 | tf_op jit(solution)/shard_map/ppermute | solution.py:286
  46.6 6.0 %collective-permute-start.11 = (f32[32,640]{1,0:T(8,128)S(1)}, f32[32,640]{1,0:T(8,128)S(1)}, u32[]{:S(2)}, u32[]{:S(2)}) collective-permute-start(f32[32,640]{1,0:T(8,128)S(1)} %collective-permute-done.10.rest_0_.refs_2_), channel_id=1, source_target_pairs={{0,1},{1,0},{2,3},{3,2},{4,5},{5,4},{6,7},{7,6},{8,9},{9,8},{10,11... | collective-permute-start | bytes 245768 | tf_op jit(solution)/shard_map/ppermute | solution.py:286
  48.8 3.8 %collective-permute-start.13 = (f32[32,640]{1,0:T(8,128)S(1)}, f32[32,640]{1,0:T(8,128)S(1)}, u32[]{:S(2)}, u32[]{:S(2)}) collective-permute-start(f32[32,640]{1,0:T(8,128)S(1)} %collective-permute-done.12.rest_1_.refs_6_), channel_id=1, source_target_pairs={{0,1},{1,0},{2,3},{3,2},{4,5},{5,4},{6,7},{7,6},{8,9},{9,8},{10,11... | collective-permute-start | bytes 245768 | tf_op jit(solution)/shard_map/ppermute | solution.py:286
  50.6 2.0 %collective-permute-start.15 = (f32[32,640]{1,0:T(8,128)S(1)}, f32[32,640]{1,0:T(8,128)S(1)}, u32[]{:S(2)}, u32[]{:S(2)}) collective-permute-start(f32[32,640]{1,0:T(8,128)S(1)} %collective-permute-done.14.rest_2_.refs_4_), channel_id=1, source_target_pairs={{0,1},{1,0},{2,3},{3,2},{4,5},{5,4},{6,7},{7,6},{8,9},{9,8},{10,11... | collective-permute-start | bytes 245768 | tf_op jit(solution)/shard_map/ppermute | solution.py:286
  54.7 7.8 %collective-permute-start.17 = (f32[32,640]{1,0:T(8,128)S(1)}, f32[32,640]{1,0:T(8,128)S(1)}, u32[]{:S(2)}, u32[]{:S(2)}) collective-permute-start(f32[32,640]{1,0:T(8,128)S(1)} %get-tuple-element.46.a), channel_id=1, source_target_pairs={{0,8},{8,0},{16,24},{24,16},{32,40},{40,32},{48,56},{56,48},{64,72... | collective-permute-start | bytes 245768 | tf_op jit(solution)/shard_map/ppermute | solution.py:286
  55.4 7.4 %collective-permute-start.18 = (f32[32,640]{1,0:T(8,128)S(1)}, f32[32,640]{1,0:T(8,128)S(1)}, u32[]{:S(2)}, u32[]{:S(2)}) collective-permute-start(f32[32,640]{1,0:T(8,128)S(1)} %get-tuple-element.46.a), channel_id=1, source_target_pairs={{0,24},{8,16},{16,8},{24,0},{32,56},{40,48},{48,40},{56,32},{64,88... | collective-permute-start | bytes 245768 | tf_op jit(solution)/shard_map/ppermute | solution.py:286
  56.3 6.5 %collective-permute-start.19 = (f32[32,640]{1,0:T(8,128)S(1)}, f32[32,640]{1,0:T(8,128)S(1)}, u32[]{:S(2)}, u32[]{:S(2)}) collective-permute-start(f32[32,640]{1,0:T(8,128)S(1)} %get-tuple-element.46.a), channel_id=1, source_target_pairs={{0,16},{8,24},{16,0},{24,8},{32,48},{40,56},{48,32},{56,40},{64,80... | collective-permute-start | bytes 245768 | tf_op jit(solution)/shard_map/ppermute | solution.py:286
  58.9 11.5 %copy-start.1 = (s32[640,32]{0,1:T(8,128)S(1)}, s32[640,32]{0,1:T(8,128)}, u32[]{:S(2)}) copy-start(s32[640,32]{0,1:T(8,128)} %param.9) | copy-start | bytes 245764
  62.8 5.0 %collective-permute-start.20 = (f32[32,640]{1,0:T(8,128)S(1)}, f32[32,640]{1,0:T(8,128)S(1)}, u32[]{:S(2)}, u32[]{:S(2)}) collective-permute-start(f32[32,640]{1,0:T(8,128)S(1)} %sum_after.7.a_ref), channel_id=1, source_target_pairs={{0,32},{8,40},{16,48},{24,56},{32,0},{40,8},{48,16},{56,24},{64,96... | collective-permute-start | bytes 245768 | tf_op jit(solution)/shard_map/ppermute | solution.py:286
  63.6 6.8 %collective-permute-start.21 = (f32[32,640]{1,0:T(8,128)S(1)}, f32[32,640]{1,0:T(8,128)S(1)}, u32[]{:S(2)}, u32[]{:S(2)}) collective-permute-start(f32[32,640]{1,0:T(8,128)S(1)} %sum_after.7.a_ref), channel_id=1, source_target_pairs={{0,96},{8,104},{16,112},{24,120},{32,64},{40,72},{48,80},{56,88},{... | collective-permute-start | bytes 245768 | tf_op jit(solution)/shard_map/ppermute | solution.py:286
  64.2 6.2 %collective-permute-start.22 = (f32[32,640]{1,0:T(8,128)S(1)}, f32[32,640]{1,0:T(8,128)S(1)}, u32[]{:S(2)}, u32[]{:S(2)}) collective-permute-start(f32[32,640]{1,0:T(8,128)S(1)} %sum_after.7.a_ref), channel_id=1, source_target_pairs={{0,64},{8,72},{16,80},{24,88},{32,96},{40,104},{48,112},{56,120},{... | collective-permute-start | bytes 245768 | tf_op jit(solution)/shard_map/ppermute | solution.py:286

commit v3 on v2

v3 whole, which is shorter than its diff:
```python
import jax
import jax.numpy as jnp
from jax import lax
from jax.experimental import pallas as pl
from jax.experimental.pallas import tpu as pltpu
from jax.sharding import PartitionSpec as P

HIGH = lax.Precision.HIGHEST
F32 = jnp.float32
BF16 = jnp.bfloat16

D = 5120
TOK = 1024
COLS = 640
RANK = 32
TRI = 3 * RANK
NBLK = 8
HALF = 4
WORKERS = 16
MB = 1 << 20
RING = (1, 3, 2)
OWNER, SECOND, THIRD = "zx", "xy", "yz"
DP_FIRST, DP_SECOND = "xy", "yx"
GATHER = (0, *RING)
ORDER = tuple(2 * r + c for r in GATHER for c in (0, 1))

NT = (((1,), (1,)), ((), ()))
TN = (((0,), (0,)), ((), ()))

VM = pl.BlockSpec(memory_space=pltpu.VMEM)
SM = pl.BlockSpec(memory_space=pltpu.SMEM)
ANY = pl.BlockSpec(memory_space=pl.ANY)


def params(mb):
    return pltpu.CompilerParams(vmem_limit_bytes=mb * MB)


def cost(flops, bytes_accessed=0):
    return pl.CostEstimate(flops=flops, bytes_accessed=bytes_accessed, transcendentals=0)


def split3(x):
    hi = x.astype(BF16)
    r = x - hi.astype(F32)
    mid = r.astype(BF16)
    lo = (r - mid.astype(F32)).astype(BF16)
    return jnp.concatenate([hi, mid, lo], axis=0)


def fold3(y):
    return y[:RANK] + y[RANK : 2 * RANK] + y[2 * RANK :]


def rows_of(me, r):
    core = (me ^ r) & 1
    z, x = (me >> 1) & 3, (me >> 3) & 3
    block = ((z + core * (x - z)) ^ (r >> 1)) * 2 + core
    return pl.multiple_of(block * COLS, COLS)


def left(rs, limit, me, acts, error, grad, q_seed, t3, after):
    first = t3 is None
    n = len(rs)

    def body(me_ref, acts_hbm, err_hbm, grad_in, seed_in, *rest):
        if first:
            p_ref, acts_v, err_v, grad_v, t3_ref, qt_ref, sem, gsem, seed_v = rest
        else:
            t3_ref, p_ref, acts_v, err_v, sem = rest[:1] + rest[-4:]
            qt_ref = seed_in

        def columns(k):
            return pl.ds(rows_of(me_ref[0], rs[k]), COLS)

        acts_copy = [
            pltpu.make_async_copy(acts_hbm.at[:, columns(k)], acts_v.at[k], sem.at[0, k])
            for k in range(n)
        ]
        err_copy = [
            pltpu.make_async_copy(err_hbm.at[columns(k), :], err_v.at[k], sem.at[1, k])
            for k in range(n)
        ]
        if first:
            seed_copy = pltpu.make_async_copy(seed_in, seed_v, gsem.at[0])
            grad_copy = pltpu.make_async_copy(grad_in, grad_v, gsem.at[1])
            seed_copy.start()
            grad_copy.start()
            for k in range(n):
                err_copy[k].start()
            seed_copy.wait()
            qt_ref[...] = seed_v[...].astype(F32).astype(BF16)
            grad_copy.wait()
            acts_copy[0].start()
            tt = lax.dot_general(qt_ref[...], grad_v[...], NT, preferred_element_type=F32)
            t3_ref[...] = split3(tt)
        else:
            for k in range(n):
                err_copy[k].start()
            acts_copy[0].start()
        for k in range(n):
            err_copy[k].wait()
            if k + 1 < n:
                acts_copy[k + 1].start()
            p_ref[k] = lax.dot_general(qt_ref[...], err_v[k], NT, preferred_element_type=F32)
        for k in range(n):
            acts_copy[k].wait()
            p = fold3(jnp.dot(t3_ref[...], acts_v[k], preferred_element_type=F32))
            p_ref[k] = (p + p_ref[k]) * (1.0 / 32.0)

    out_shape = [
        jax.ShapeDtypeStruct((n, RANK, COLS), F32),
        pltpu.VMEM((n, TOK, COLS), BF16),
        pltpu.VMEM((n, COLS, COLS), BF16),
    ]
    scratch = [pltpu.SemaphoreType.DMA((2, n))]
    if first:
        out_shape += [
            pltpu.VMEM((TOK, COLS), BF16),
            pltpu.VMEM((TRI, TOK), BF16),
            pltpu.VMEM((RANK, COLS), BF16),
        ]
        scratch += [pltpu.SemaphoreType.DMA((2,)), pltpu.VMEM((RANK, COLS), jnp.int32)]
        args = (me, acts, error, grad, q_seed)
        in_specs = [SM, ANY, ANY, ANY, ANY]
    else:
        args = (me, acts, error, grad, q_seed, t3, *after)
        in_specs = [SM, ANY, ANY, VM, VM, VM] + [ANY] * len(after)
    p, acts_v, err_v, *more = pl.pallas_call(
        body,
        out_shape=out_shape,
        in_specs=in_specs,
        out_specs=[VM] * len(out_shape),
        scratch_shapes=scratch,
        compiler_params=params(limit),
        cost_estimate=cost(2 * n * 256 * COLS * (TOK + COLS), n * 2 * MB),
        name="left_first" if first else "left_more",
    )(*args)
    return p, {r: (acts_v, err_v, k) for k, r in enumerate(rs)}, more


def memory_blocks(rs, held, grad_v, after):
    n = len(rs)

    def body(*refs):
        g_ref, outs = refs[2 * n], refs[2 * n + 2 :]
        for i, r in enumerate(rs):
            a_ref, e_ref, k = refs[2 * i], refs[2 * i + 1], held[r][2]
            grad = lax.dot_general(a_ref[k], g_ref[...], TN, preferred_element_type=F32)
            outs[i][...] = grad + e_ref[k].astype(F32)

    out = pl.pallas_call(
        body,
        out_shape=[pltpu.VMEM((COLS, COLS), F32)] * n,
        in_specs=[VM] * (2 * n + 1) + [ANY],
        out_specs=[VM] * n,
        compiler_params=params(8),
        cost_estimate=cost(2 * n * COLS * COLS * TOK),
        name="memory_blocks",
    )(*(x for r in rs for x in held[r][:2]), grad_v, after)
    return dict(zip(rs, out))


def right(work, held, grad_v, earlier=None, last=False):
    n = len(work)

    def body(*refs):
        g_ref, rest = refs[3 * n], refs[3 * n + 1 :]
        given, outs = (rest[:3], rest[3:]) if earlier else ((), rest)
        tmp, q, gram = (x[...] for x in given) if earlier else (0.0, 0.0, 0.0)
        for i, (r, _, entry) in enumerate(work):
            block, a_ref, e_ref = refs[3 * i : 3 * i + 3]
            k = held[r][2]
            p = split3(block[...] if entry is None else block[entry])
            tmp = tmp + fold3(lax.dot_general(p, a_ref[k], NT, preferred_element_type=F32))
            q = q + fold3(jnp.dot(p, e_ref[k], preferred_element_type=F32))
            gram = gram + lax.dot_general(p, p, NT, preferred_element_type=F32)
        if last:
            q = q + fold3(jnp.dot(split3(tmp), g_ref[...], preferred_element_type=F32))
            outs[0][...] = q
            outs[1][...] = gram
        else:
            outs[0][...] = tmp
            outs[1][...] = q
            outs[2][...] = gram

    shapes = [
        jax.ShapeDtypeStruct((RANK, TOK), F32),
        jax.ShapeDtypeStruct((RANK, COLS), F32),
        jax.ShapeDtypeStruct((TRI, TRI), F32),
    ]
    if last:
        shapes = shapes[1:]
    args = [x for r, array, _ in work for x in (array, *held[r][:2])]
    args += [grad_v, *(earlier or ())]
    return pl.pallas_call(
        body,
        out_shape=shapes,
        in_specs=[VM] * len(args),
        out_specs=[VM] * len(shapes),
        compiler_params=params(8),
        cost_estimate=cost(2 * n * 256 * COLS * (TOK + COLS)),
        name="right_last" if last else "right_part",
    )(*args)


def orthonormal_body(gram_ref, *refs):
    mine, theirs, p3_ref, inv_ref = refs[:HALF], *refs[HALF:]
    wide = fold3(gram_ref[...])
    gram = wide[:, :RANK] + wide[:, RANK : 2 * RANK] + wide[:, 2 * RANK :]
    rows = lax.broadcasted_iota(jnp.int32, (RANK, RANK), 0)
    cols = lax.broadcasted_iota(jnp.int32, (RANK, RANK), 1)
    eye = (rows == cols).astype(F32)
    work = jnp.concatenate([gram, eye], axis=1)
    below = lax.broadcasted_iota(jnp.int32, (RANK, 1), 0)
    for k in range(RANK):
        row = work[k : k + 1, :]
        factor = jnp.where(below > k, work[:, k : k + 1] / row[:, k : k + 1], 0.0)
        work = work - factor * row
    diag = jnp.sum(work[:, :RANK] * eye, axis=1, keepdims=True)
    inv = work[:, RANK:] / jnp.sqrt(diag)
    inv_ref[...] = inv
    for k in range(NBLK):
        block = theirs[k // 2] if k % 2 else mine[k // 2][...]
        p = jnp.dot(inv, block, precision=HIGH, preferred_element_type=F32)
        hi = p.astype(BF16).astype(F32)
        r = p - hi
        mid = r.astype(BF16).astype(F32)
        stacked = jnp.concatenate([hi, mid, r - mid, jnp.zeros_like(p)], axis=0)
        p3_ref[k] = stacked.T.astype(BF16)


def orthonormal(gram, mine, theirs):
    return pl.pallas_call(
        orthonormal_body,
        out_shape=(
            pltpu.VMEM((NBLK, COLS, 4 * RANK), BF16),
            jax.ShapeDtypeStruct((RANK, RANK), F32),
        ),
        in_specs=[VM] * (2 + HALF),
        out_specs=(VM, VM),
        compiler_params=params(8),
        cost_estimate=cost(1 << 31),
        name="orthonormal",
    )(gram, *mine, theirs)


def update_body(me_ref, a_ref, b_ref, c_ref, d_ref, inv_ref, dither_ref, p3_ref, *rest):
    mem = rest[:NBLK]
    qf_ref, out_hbm, stage, sem = rest[NBLK:]
    total = (a_ref[...] + b_ref[...]) + (c_ref[...] + d_ref[...])
    qmat = jnp.dot(inv_ref[...], total, precision=HIGH, preferred_element_type=F32) / WORKERS
    scale = 1.0 + (dither_ref[...].astype(F32) / 65536.0 - 0.5) / 4.0
    qt = (qmat * scale).astype(BF16)
    qf_ref[...] = qt
    q3 = jnp.concatenate([qt, qt, qt, jnp.zeros((RANK, COLS), BF16)], axis=0)
    copies = []
    for k, r in enumerate(ORDER):
        approx = jnp.dot(p3_ref[k], q3, preferred_element_type=F32)
        stage[k] = (mem[k][...] - approx).astype(BF16)
        at = pl.ds(rows_of(me_ref[0], r), COLS)
        copies.append(pltpu.make_async_copy(stage.at[k], out_hbm.at[at, :], sem.at[k]))
        copies[-1].start()
    for c in copies:
        c.wait()


def update(me, parts, inv, dither, p3, memory):
    return pl.pallas_call(
        update_body,
        out_shape=(
            jax.ShapeDtypeStruct((RANK, COLS), BF16),
            jax.ShapeDtypeStruct((D, COLS), BF16),
        ),
        in_specs=[SM] + [VM] * (len(parts) + 3 + NBLK),
        out_specs=(VM, ANY),
        scratch_shapes=[
            pltpu.VMEM((NBLK, COLS, COLS), BF16),
            pltpu.SemaphoreType.DMA((NBLK,)),
        ],
        compiler_params=params(16),
        cost_estimate=cost(2 * D * COLS * 256, 7 * MB),
        name="update",
    )(me, *parts, inv, dither, p3, *memory)


def sum_after(parts, after):
    n = len(parts)

    def body(*refs):
        total = refs[0][...]
        for x in refs[1:n]:
            total = total + x[...]
        refs[-1][...] = total

    return pl.pallas_call(
        body,
        out_shape=jax.ShapeDtypeStruct((RANK, COLS), F32),
        in_specs=[VM] * n + [ANY] * len(after),
        out_specs=VM,
        compiler_params=params(8),
        cost_estimate=cost(1000),
        name="sum_after",
    )(*parts, *after)


def stack_after(parts, after):
    n = len(parts)

    def body(*refs):
        for i in range(n):
            refs[-1][i] = refs[i][...]

    return pl.pallas_call(
        body,
        out_shape=jax.ShapeDtypeStruct((n, RANK, COLS), F32),
        in_specs=[VM] * n + [ANY],
        out_specs=VM,
        compiler_params=params(8),
        cost_estimate=cost(1000),
        name="stack_after",
    )(*parts, after)


def place(y, x, z, core):
    return ((y * 4 + x) * 4 + z) * 2 + core


def exchange(v, axes, r):
    pairs = []
    for source in range(128):
        at = {"y": source >> 5, "x": source >> 3 & 3, "z": source >> 1 & 3}
        at[axes[source & 1]] ^= r
        pairs.append((source, place(core=source & 1, **at)))
    return lax.ppermute(v, ("dp", "tensor"), pairs)


def ring(v, axes):
    return [exchange(v, axes, r) for r in RING]


def core(v):
    return lax.ppermute(v, ("dp", "tensor"), [(i, i ^ 1) for i in range(128)])


def per_device(acts, out_grad, error, q_seed, dither):
    me = lax.axis_index(("dp", "tensor")).astype(jnp.int32).reshape(1)
    acts = pltpu.with_memory_space_constraint(acts, pltpu.HBM)
    error = pltpu.with_memory_space_constraint(error, pltpu.HBM)
    out_grad = pltpu.with_memory_space_constraint(out_grad, pltpu.HBM)
    seed = pltpu.with_memory_space_constraint(q_seed.T, pltpu.HBM)

    held = {}

    def left_of(rs, limit, grad, seed, t3, after):
        p, more_held, more = left(rs, limit, me, acts, error, grad, seed, t3, after)
        held.update(more_held)
        return p, more

    away, (grad_v, t3, qt) = left_of((1, 3, 5, 7), 8, out_grad, seed, None, ())
    came = core(away)
    kept, _ = left_of((2, 4, 6), 8, grad_v, qt, t3, ())
    part = kept + came[1:]
    from_ring = [exchange(part[r - 1], OWNER, r) for r in RING]
    kept, _ = left_of((0,), 8, grad_v, qt, t3, (part,))
    own = sum_after([kept[0], came[0], *from_ring], [])

    from_ring = ring(own, SECOND)
    memory = memory_blocks((0, 1, 2), held, grad_v, own)
    own = sum_after([own, *from_ring], [memory[0]])
    from_ring = ring(own, THIRD)
    memory |= memory_blocks((3, 4, 5), held, grad_v, own)
    own = sum_after([own, *from_ring], [memory[3]])

    mine = [own, *ring(own, OWNER)]
    early = right([(0, own, None)], held, grad_v)
    theirs = core(stack_after(mine, early[0]))
    mid = right([(2 * r, x, None) for r, x in zip(RING, mine[1:])], held, grad_v, early)
    q, gram = right([(2 * r + 1, theirs, i) for i, r in enumerate(GATHER)], held, grad_v, mid, True)

    from_ring = ring(q, DP_FIRST)
    p3, inv = orthonormal(gram, mine, theirs)
    q = sum_after([q, *from_ring], [inv])
    from_ring = ring(q, DP_SECOND)
    memory |= memory_blocks((6, 7), held, grad_v, q)
    blocks = [memory[r] for r in ORDER]
    q_factor, new_error = update(me, [q, *from_ring], inv, dither.T, p3, blocks)
    return (q_factor.T, new_error)


def solution(mesh):
    in_specs = (
        P("dp", None),
        P("dp", "tensor"),
        P("dp", "tensor"),
        P("tensor", None),
        P("tensor", None),
    )
    out_specs = (P("tensor", None), P("dp", "tensor"))
    return jax.shard_map(
        per_device, mesh=mesh, in_specs=in_specs, out_specs=out_specs, check_vma=False
    )
```

time: 74.8 us -> 70.1 us (0.937)
  starting transfers between devices: 27.3 us -> 24.5 us
  waiting for transfers between devices: 13 us -> 11.7 us
  local copies, waits for them, and re-layouts: 0.91 us -> 0.03 us
    ppermute x23 -> x20, starting transfers between devices: 27.3 us -> 24.5 us  [the longest x18 24.3 us: exchange(): return lax.ppermute(v, ('dp', 'tensor'), pairs)]
    ppermute x23 -> x20, waiting for transfers between devices: 13 us -> 11.7 us  [the longest x18 11.7 us: exchange(): return lax.ppermute(v, ('dp', 'tensor'), pairs)]
    unnamed x4 -> x2, local copies, waits for them, and re-layouts: 0.88 us -> 0.01 us
    pallas_call x2 -> x3, Pallas kernels: 10.3 us -> 10.9 us  [left(): pl.pallas_call(body, out_shape=out_shape, in_specs=in_specs, out_specs=[V...]
  transfers between devices with their start and end apart: 23 -> 20, of which waited for: 11 -> 8; matrix products, arithmetic and copies ran while one was open for 0% -> 0% of each run, Pallas kernels for 27% -> 29%
where the time goes in v3:
time: 70.1 us; the launch traced here: 69.9 us
  Pallas kernels  32.7 us (47%)
  starting transfers between devices  24.5 us (35%)
  waiting for transfers between devices  11.7 us (17%)
  between operations  0.98 us (1%)
    ppermute x18, starting transfers between devices, exchange(): return lax.ppermute(v, ('dp', 'tensor'), pairs)  24.3 us
    ppermute x18, waiting for transfers between devices, exchange(): return lax.ppermute(v, ('dp', 'tensor'), pairs)  11.7 us
    pallas_call x3, Pallas kernels, left(): pl.pallas_call(body, out_shape=out_shape, in_specs=in_specs, out_specs=[V...  10.9 us
    pallas_call x3, Pallas kernels, memory_blocks(): pl.pallas_call(body, out_shape=[pltpu.VMEM((COLS, COLS), F32)] * n, in_sp...  8.71 us
    pallas_call x3, Pallas kernels, right(): pl.pallas_call(body, out_shape=shapes, in_specs=[VM] * len(args), out_spe...  5.3 us
    pallas_call x1, Pallas kernels, update(): pl.pallas_call(update_body, out_shape=(jax.ShapeDtypeStruct((RANK, COLS),...  4.06 us
    pallas_call x1, Pallas kernels, orthonormal(): pl.pallas_call(orthonormal_body, out_shape=(pltpu.VMEM((NBLK, COLS, 4 * R...  3.61 us
  transfers between devices with their start and end apart: 20, of which 8 were waited for; matrix products, arithmetic and copies ran while one was open for 0% of the time, Pallas kernels for 29%

profile of v3, /device:TPU:0, one launch (start us, length us, event | category | flops | bytes accessed | tf_op | source)
XLA Modules:
  0.0 69.9 jit_solution(5824706207173960100)
XLA Ops:
  0.6 5.4 %left_first.1 = (f32[4,32,640]{2,1,0:T(8,128)S(1)}, bf16[4,1024,640]{2,1,0:T(8,128)(2,1)S(1)}, bf16[4,640,640]{2,1,0:T(8,128)(2,1)S(1)}, bf16[1024,640]{1,0:T(8,...) custom-call(s32[1]{0:T(128)} %bitcast.me_ref, bf16[1024,5120]{1,0:T(8,128)(2,1)} %acts_hbm.5, ...), custom_call_target="tpu_custom_call" | custom-call | flops 2181038080 | bytes 8388608 | tf_op jit(solution)/shard_map/left_first/pallas_call | solution.py:129
  6.2 3.5 %left_more.2 = (f32[3,32,640]{2,1,0:T(8,128)S(1)}, bf16[3,1024,640]{2,1,0:T(8,128)(2,1)S(1)}, bf16[3,640,640]{2,1,0:T(8,128)(2,1)S(1)}) custom-call(s32[1]{0:T(128)} %bitcast.me_ref, bf16[1024,5120]{1,0:T(8,128)(2,1)} %acts_hbm.5, bf16[5120,640]{1,0:T(8,128)(2,1)} %err_hbm.5, ...), custom_call_target="tpu_custom_call" | custom-call | flops 1635778560 | bytes 6291456 | tf_op jit(solution)/shard_map/left_more/pallas_call | solution.py:129
  9.8 4.0 %collective-permute-start.3 = (f32[32,640]{1,0:T(8,128)S(1)}, f32[32,640]{1,0:T(8,128)S(1)}, u32[]{:S(2)}, u32[]{:S(2)}) collective-permute-start(f32[32,640]{1,0:T(8,128)S(1)} %get-tuple-element.66), channel_id=1, source_target_pairs={{0,4},{1,17},{2,6},{3,19},{4,0},{5,21},{6,2},{7,23},{8,12},{9,25},... | collective-permute-start | bytes 245768 | tf_op jit(solution)/shard_map/ppermute | solution.py:335
  13.8 0.7 %collective-permute-start.2 = (f32[32,640]{1,0:T(8,128)S(1)}, f32[32,640]{1,0:T(8,128)S(1)}, u32[]{:S(2)}, u32[]{:S(2)}) collective-permute-start(f32[32,640]{1,0:T(8,128)S(1)} %get-tuple-element.67), channel_id=1, source_target_pairs={{0,6},{1,25},{2,4},{3,27},{4,2},{5,29},{6,0},{7,31},{8,14},{9,17},... | collective-permute-start | bytes 245768 | tf_op jit(solution)/shard_map/ppermute | solution.py:335
  14.5 0.3 collective-permute-start.1
  14.8 2.0 %left_more.3 = (f32[1,32,640]{2,1,0:T(8,128)S(1)}, bf16[1,1024,640]{2,1,0:T(8,128)(2,1)S(1)}, bf16[1,640,640]{2,1,0:T(8,128)(2,1)S(1)}) custom-call(s32[1]{0:T(128)} %bitcast.me_ref, bf16[1024,5120]{1,0:T(8,128)(2,1)} %acts_hbm.5, bf16[5120,640]{1,0:T(8,128)(2,1)} %err_hbm.5, ...), custom_call_target="tpu_custom_call" | custom-call | flops 545259520 | bytes 2097152 | tf_op jit(solution)/shard_map/left_more/pallas_call | solution.py:129
  16.8 2.7 %collective-permute-done.2.refs_3_ = f32[32,640]{1,0:T(8,128)S(1)} collective-permute-done((f32[32,640]{1,0:T(8,128)S(1)}, f32[32,640]{1,0:T(8,128)S(1)}, u32[]{:S(2)}, u32[]{:S(2)}) %collective-permute-start.2) | collective-permute-done | bytes 81952 | tf_op jit(solution)/shard_map/ppermute | solution.py:335
  19.5 3.1 %collective-permute-start.6 = (f32[32,640]{1,0:T(8,128)S(1)}, f32[32,640]{1,0:T(8,128)S(1)}, u32[]{:S(2)}, u32[]{:S(2)}) collective-permute-start(f32[32,640]{1,0:T(8,128)S(1)} %sum_after.4.refs_7_.refs_0_), channel_id=1, source_target_pairs={{0,16},{1,65},{2,18},{3,67},{4,20},{5,69},{6,22},{7,71},{8,24},{9,... | collective-permute-start | bytes 245768 | tf_op jit(solution)/shard_map/ppermute | solution.py:335
  22.6 1.1 %collective-permute-start.5 = (f32[32,640]{1,0:T(8,128)S(1)}, f32[32,640]{1,0:T(8,128)S(1)}, u32[]{:S(2)}, u32[]{:S(2)}) collective-permute-start(f32[32,640]{1,0:T(8,128)S(1)} %sum_after.4.refs_7_.refs_0_), channel_id=1, source_target_pairs={{0,24},{1,97},{2,26},{3,99},{4,28},{5,101},{6,30},{7,103},{8,16},{... | collective-permute-start | bytes 245768 | tf_op jit(solution)/shard_map/ppermute | solution.py:335
  23.7 3.2 %memory_blocks.3 = (f32[640,640]{1,0:T(8,128)S(1)}, f32[640,640]{1,0:T(8,128)S(1)}, f32[640,640]{1,0:T(8,128)S(1)}) custom-call(bf16[1,1024,640]{2,1,0:T(8,128)(2,1)S(1)} %get-tuple-element.40.refs_0_.refs_1_, bf16[1,640,640]{2,1,0:T(8,128)(2,1)S(1)} %get-tuple-element.41.refs_1_.refs_2_, ...), custom_call_target="tpu_custom_call" | custom-call | flops 2516582400 | tf_op jit(solution)/shard_map/memory_blocks/pallas_call | solution.py:152
  27.0 1.2 %collective-permute-done.5.refs_2_ = f32[32,640]{1,0:T(8,128)S(1)} collective-permute-done((f32[32,640]{1,0:T(8,128)S(1)}, f32[32,640]{1,0:T(8,128)S(1)}, u32[]{:S(2)}, u32[]{:S(2)}) %collective-permute-start.5) | collective-permute-done | bytes 81952 | tf_op jit(solution)/shard_map/ppermute | solution.py:335
  28.3 3.3 %collective-permute-start.9 = (f32[32,640]{1,0:T(8,128)S(1)}, f32[32,640]{1,0:T(8,128)S(1)}, u32[]{:S(2)}, u32[]{:S(2)}) collective-permute-start(f32[32,640]{1,0:T(8,128)S(1)} %sum_after.5.refs_7_.refs_0_), channel_id=1, source_target_pairs={{0,64},{1,5},{2,66},{3,7},{4,68},{5,1},{6,70},{7,3},{8,72},{9,13},... | collective-permute-start | bytes 245768 | tf_op jit(solution)/shard_map/ppermute | solution.py:335
  31.6 1.1 %collective-permute-start.8 = (f32[32,640]{1,0:T(8,128)S(1)}, f32[32,640]{1,0:T(8,128)S(1)}, u32[]{:S(2)}, u32[]{:S(2)}) collective-permute-start(f32[32,640]{1,0:T(8,128)S(1)} %sum_after.5.refs_7_.refs_0_), channel_id=1, source_target_pairs={{0,96},{1,7},{2,98},{3,5},{4,100},{5,3},{6,102},{7,1},{8,104},{9,1... | collective-permute-start | bytes 245768 | tf_op jit(solution)/shard_map/ppermute | solution.py:335
  32.6 3.2 %memory_blocks.4 = (f32[640,640]{1,0:T(8,128)S(1)}, f32[640,640]{1,0:T(8,128)S(1)}, f32[640,640]{1,0:T(8,128)S(1)}) custom-call(bf16[4,1024,640]{2,1,0:T(8,128)(2,1)S(1)} %get-tuple-element.42.refs_2_.refs_0_.refs_4_.refs_1_.refs_7_.refs_10_, bf16[4,640,640]{2,1,0:T(8,128)(2,1)S(1)} %get-tuple-element.43.refs_3_.refs_1_.refs_5_.refs_2_.refs_8_.refs_11_, ...), custom_call_target="tpu_custom_call" | custom-call | flops 2516582400 | tf_op jit(solution)/shard_map/memory_blocks/pallas_call | solution.py:152
  35.9 1.3 %collective-permute-done.8.refs_2_ = f32[32,640]{1,0:T(8,128)S(1)} collective-permute-done((f32[32,640]{1,0:T(8,128)S(1)}, f32[32,640]{1,0:T(8,128)S(1)}, u32[]{:S(2)}, u32[]{:S(2)}) %collective-permute-start.8) | collective-permute-done | bytes 81952 | tf_op jit(solution)/shard_map/ppermute | solution.py:335
  37.2 1.9 %collective-permute-start.12 = (f32[32,640]{1,0:T(8,128)S(1)}, f32[32,640]{1,0:T(8,128)S(1)}, u32[]{:S(2)}, u32[]{:S(2)}) collective-permute-start(f32[32,640]{1,0:T(8,128)S(1)} %sum_after.6.refs_0_), channel_id=1, source_target_pairs={{0,4},{1,17},{2,6},{3,19},{4,0},{5,21},{6,2},{7,23},{8,12},{9,25},... | collective-permute-start | bytes 245768 | tf_op jit(solution)/shard_map/ppermute | solution.py:335
  39.2 0.6 collective-permute-start.11
  39.8 1.0 %collective-permute-start.10 = (f32[32,640]{1,0:T(8,128)S(1)}, f32[32,640]{1,0:T(8,128)S(1)}, u32[]{:S(2)}, u32[]{:S(2)}) collective-permute-start(f32[32,640]{1,0:T(8,128)S(1)} %sum_after.6.refs_0_), channel_id=1, source_target_pairs={{0,2},{1,9},{2,0},{3,11},{4,6},{5,13},{6,4},{7,15},{8,10},{9,1},{1... | collective-permute-start | bytes 245768 | tf_op jit(solution)/shard_map/ppermute | solution.py:335
  40.8 0.7 %right_part.2 = (f32[32,1024]{1,0:T(8,128)S(1)}, f32[32,640]{1,0:T(8,128)S(1)}, f32[96,96]{1,0:T(8,128)S(1)}) custom-call(f32[32,640]{1,0:T(8,128)S(1)} %sum_after.6.refs_0_, bf16[1,1024,640]{2,1,0:T(8,128)(2,1)S(1)} %get-tuple-element.40.refs_0_.refs_1_, bf16[1,640,640]{2,1,0:T(8,128)(2,1)S(1)} %get-tuple-element.41.refs_1_.refs_2_, ...), custom_call_target="tpu_custom_call" | custom-call | flops 545259520 | tf_op jit(solution)/shard_map/right_part/pallas_call | solution.py:196
  41.5 1.7 %collective-permute-done.12.refs_3_.refs_6_ = f32[32,640]{1,0:T(8,128)S(1)} collective-permute-done((f32[32,640]{1,0:T(8,128)S(1)}, f32[32,640]{1,0:T(8,128)S(1)}, u32[]{:S(2)}, u32[]{:S(2)}) %collective-permute-start.12) | collective-permute-done | bytes 81952 | tf_op jit(solution)/shard_map/ppermute | solution.py:335
  43.3 1.6 %collective-permute-done.11.refs_2_.refs_3_ = f32[32,640]{1,0:T(8,128)S(1)} collective-permute-done((f32[32,640]{1,0:T(8,128)S(1)}, f32[32,640]{1,0:T(8,128)S(1)}, u32[]{:S(2)}, u32[]{:S(2)}) %collective-permute-start.11) | collective-permute-done | bytes 81952 | tf_op jit(solution)/shard_map/ppermute | solution.py:335
  45.0 1.9 %right_part.3 = (f32[32,1024]{1,0:T(8,128)S(1)}, f32[32,640]{1,0:T(8,128)S(1)}, f32[96,96]{1,0:T(8,128)S(1)}) custom-call(f32[32,640]{1,0:T(8,128)S(1)} %collective-permute-done.10.refs_1_.refs_0_, bf16[3,1024,640]{2,1,0:T(8,128)(2,1)S(1)} %get-tuple-element.44.refs_4_.refs_2_.refs_1_.refs_7_.refs_0_, ...), custom_call_target="tpu_custom_call" | custom-call | flops 1635778560 | tf_op jit(solution)/shard_map/right_part/pallas_call | solution.py:196
  46.9 2.7 %right_last.1 = (f32[32,640]{1,0:T(8,128)S(1)}, f32[96,96]{1,0:T(8,128)S(1)}) custom-call(f32[4,32,640]{2,1,0:T(8,128)S(1)} %collective-permute-done.13.refs_0_.refs_3_.refs_6_.refs_9_.refs_4_, bf16[4,1024,640]{2,1,0:T(8,128)(2,1)S(1)} %get-tuple-element.42.refs_2_.refs_0_.refs_4_.refs_1_.refs_7_.refs_10_, ...), custom_call_target="tpu_custom_call" | custom-call | flops 2181038080 | tf_op jit(solution)/shard_map/right_last/pallas_call | solution.py:196
  49.6 2.4 %collective-permute-start.16 = (f32[32,640]{1,0:T(8,128)S(1)}, f32[32,640]{1,0:T(8,128)S(1)}, u32[]{:S(2)}, u32[]{:S(2)}) collective-permute-start(f32[32,640]{1,0:T(8,128)S(1)} %get-tuple-element.54.refs_0_), channel_id=1, source_target_pairs={{0,16},{1,65},{2,18},{3,67},{4,20},{5,69},{6,22},{7,71},{8,24},{9,... | collective-permute-start | bytes 245768 | tf_op jit(solution)/shard_map/ppermute | solution.py:335
  52.0 1.1 %collective-permute-start.15 = (f32[32,640]{1,0:T(8,128)S(1)}, f32[32,640]{1,0:T(8,128)S(1)}, u32[]{:S(2)}, u32[]{:S(2)}) collective-permute-start(f32[32,640]{1,0:T(8,128)S(1)} %get-tuple-element.54.refs_0_), channel_id=1, source_target_pairs={{0,24},{1,97},{2,26},{3,99},{4,28},{5,101},{6,30},{7,103},{8,16},{... | collective-permute-start | bytes 245768 | tf_op jit(solution)/shard_map/ppermute | solution.py:335
  53.1 3.6 %orthonormal.1 = (bf16[8,640,128]{2,1,0:T(8,128)(2,1)S(1)}, f32[32,32]{1,0:T(8,128)S(1)}) custom-call(f32[96,96]{1,0:T(8,128)S(1)} %get-tuple-element.55.gram_ref, f32[32,640]{1,0:T(8,128)S(1)} %sum_after.6.refs_0_, f32[32,640]{1,0:T(8,128)S(1)} %collective-permute-done.10.refs_1_.refs_0_, f32[32,640]{1,0:T(8,128)S(1)} %collective-permute-done.11.refs_2_.refs_3_, ...), custom_call_target="tpu_custom_call" | custom-call | flops 2147483648 | tf_op jit(solution)/shard_map/orthonormal/pallas_call | solution.py:234
  56.8 0.9 %collective-permute-done.15.refs_2_ = f32[32,640]{1,0:T(8,128)S(1)} collective-permute-done((f32[32,640]{1,0:T(8,128)S(1)}, f32[32,640]{1,0:T(8,128)S(1)}, u32[]{:S(2)}, u32[]{:S(2)}) %collective-permute-start.15) | collective-permute-done | bytes 81952 | tf_op jit(solution)/shard_map/ppermute | solution.py:335
  57.7 2.4 %collective-permute-start.19 = (f32[32,640]{1,0:T(8,128)S(1)}, f32[32,640]{1,0:T(8,128)S(1)}, u32[]{:S(2)}, u32[]{:S(2)}) collective-permute-start(f32[32,640]{1,0:T(8,128)S(1)} %sum_after.7.refs_5_.a_ref), channel_id=1, source_target_pairs={{0,64},{1,17},{2,66},{3,19},{4,68},{5,21},{6,70},{7,23},{8,72},{9,... | collective-permute-start | bytes 245768 | tf_op jit(solution)/shard_map/ppermute | solution.py:335
  60.1 1.1 %collective-permute-start.18 = (f32[32,640]{1,0:T(8,128)S(1)}, f32[32,640]{1,0:T(8,128)S(1)}, u32[]{:S(2)}, u32[]{:S(2)}) collective-permute-start(f32[32,640]{1,0:T(8,128)S(1)} %sum_after.7.refs_5_.a_ref), channel_id=1, source_target_pairs={{0,96},{1,25},{2,98},{3,27},{4,100},{5,29},{6,102},{7,31},{8,104},... | collective-permute-start | bytes 245768 | tf_op jit(solution)/shard_map/ppermute | solution.py:335
  61.2 2.2 %memory_blocks.5 = (f32[640,640]{1,0:T(8,128)S(1)}, f32[640,640]{1,0:T(8,128)S(1)}) custom-call(bf16[3,1024,640]{2,1,0:T(8,128)(2,1)S(1)} %get-tuple-element.44.refs_4_.refs_2_.refs_1_.refs_7_.refs_0_, bf16[3,640,640]{2,1,0:T(8,128)(2,1)S(1)} %get-tuple-element.45.refs_5_.refs_3_.refs_2_.refs_8_.refs_1_, ...), custom_call_target="tpu_custom_call" | custom-call | flops 1677721600 | tf_op jit(solution)/shard_map/memory_blocks/pallas_call | solution.py:152
  63.7 2.0 %collective-permute-done.18.c_ref = f32[32,640]{1,0:T(8,128)S(1)} collective-permute-done((f32[32,640]{1,0:T(8,128)S(1)}, f32[32,640]{1,0:T(8,128)S(1)}, u32[]{:S(2)}, u32[]{:S(2)}) %collective-permute-start.18) | collective-permute-done | bytes 81952 | tf_op jit(solution)/shard_map/ppermute | solution.py:335
  65.7 4.1 %update.1 = (bf16[32,640]{1,0:T(8,128)(2,1)}, bf16[5120,640]{1,0:T(8,128)(2,1)}) custom-call(s32[1]{0:T(128)} %bitcast.me_ref, f32[32,640]{1,0:T(8,128)S(1)} %sum_after.7.refs_5_.a_ref, f32[32,640]{1,0:T(8,128)S(1)} %collective-permute-done.17.b_ref, f32[32,640]{1,0:T(8,128)S(1)} %collective-permute-done.18.c_ref, ...), custom_call_target="tpu_custom_call" | custom-call | flops 1677721600 | bytes 7340032 | tf_op jit(solution)/shard_map/update/pallas_call | solution.py:269
  (29 shorter events, 0.7 us)
Async XLA Ops:
  6.1 3.6 %collective-permute-start = (f32[4,32,640]{2,1,0:T(8,128)S(1)}, f32[4,32,640]{2,1,0:T(8,128)S(1)}, u32[]{:S(2)}, u32[]{:S(2)}) collective-permute-start(f32[4,32,640]{2,1,0:T(8,128)S(1)} %get-tuple-element.38), channel_id=1, source_target_pairs={{0,1},{1,0},{2,3},{3,2},{4,5},{5,4},{6,7},{7,6},{8,9},{9,8},{10,11... | collective-permute-start | bytes 983048 | tf_op jit(solution)/shard_map/ppermute | solution.py:343
  9.8 7.0 %collective-permute-start.3 = (f32[32,640]{1,0:T(8,128)S(1)}, f32[32,640]{1,0:T(8,128)S(1)}, u32[]{:S(2)}, u32[]{:S(2)}) collective-permute-start(f32[32,640]{1,0:T(8,128)S(1)} %get-tuple-element.66), channel_id=1, source_target_pairs={{0,4},{1,17},{2,6},{3,19},{4,0},{5,21},{6,2},{7,23},{8,12},{9,25},... | collective-permute-start | bytes 245768 | tf_op jit(solution)/shard_map/ppermute | solution.py:335
  13.8 5.7 %collective-permute-start.2 = (f32[32,640]{1,0:T(8,128)S(1)}, f32[32,640]{1,0:T(8,128)S(1)}, u32[]{:S(2)}, u32[]{:S(2)}) collective-permute-start(f32[32,640]{1,0:T(8,128)S(1)} %get-tuple-element.67), channel_id=1, source_target_pairs={{0,6},{1,25},{2,4},{3,27},{4,2},{5,29},{6,0},{7,31},{8,14},{9,17},... | collective-permute-start | bytes 245768 | tf_op jit(solution)/shard_map/ppermute | solution.py:335
  14.5 4.9 %collective-permute-start.1 = (f32[32,640]{1,0:T(8,128)S(1)}, f32[32,640]{1,0:T(8,128)S(1)}, u32[]{:S(2)}, u32[]{:S(2)}) collective-permute-start(f32[32,640]{1,0:T(8,128)S(1)} %get-tuple-element.68), channel_id=1, source_target_pairs={{0,2},{1,9},{2,0},{3,11},{4,6},{5,13},{6,4},{7,15},{8,10},{9,1},{1... | collective-permute-start | bytes 245768 | tf_op jit(solution)/shard_map/ppermute | solution.py:335
  19.5 7.5 %collective-permute-start.6 = (f32[32,640]{1,0:T(8,128)S(1)}, f32[32,640]{1,0:T(8,128)S(1)}, u32[]{:S(2)}, u32[]{:S(2)}) collective-permute-start(f32[32,640]{1,0:T(8,128)S(1)} %sum_after.4.refs_7_.refs_0_), channel_id=1, source_target_pairs={{0,16},{1,65},{2,18},{3,67},{4,20},{5,69},{6,22},{7,71},{8,24},{9,... | collective-permute-start | bytes 245768 | tf_op jit(solution)/shard_map/ppermute | solution.py:335
  22.6 5.7 %collective-permute-start.5 = (f32[32,640]{1,0:T(8,128)S(1)}, f32[32,640]{1,0:T(8,128)S(1)}, u32[]{:S(2)}, u32[]{:S(2)}) collective-permute-start(f32[32,640]{1,0:T(8,128)S(1)} %sum_after.4.refs_7_.refs_0_), channel_id=1, source_target_pairs={{0,24},{1,97},{2,26},{3,99},{4,28},{5,101},{6,30},{7,103},{8,16},{... | collective-permute-start | bytes 245768 | tf_op jit(solution)/shard_map/ppermute | solution.py:335
  23.7 4.5 %collective-permute-start.4 = (f32[32,640]{1,0:T(8,128)S(1)}, f32[32,640]{1,0:T(8,128)S(1)}, u32[]{:S(2)}, u32[]{:S(2)}) collective-permute-start(f32[32,640]{1,0:T(8,128)S(1)} %sum_after.4.refs_7_.refs_0_), channel_id=1, source_target_pairs={{0,8},{1,33},{2,10},{3,35},{4,12},{5,37},{6,14},{7,39},{8,0},{9,41... | collective-permute-start | bytes 245768 | tf_op jit(solution)/shard_map/ppermute | solution.py:335
  28.3 7.6 %collective-permute-start.9 = (f32[32,640]{1,0:T(8,128)S(1)}, f32[32,640]{1,0:T(8,128)S(1)}, u32[]{:S(2)}, u32[]{:S(2)}) collective-permute-start(f32[32,640]{1,0:T(8,128)S(1)} %sum_after.5.refs_7_.refs_0_), channel_id=1, source_target_pairs={{0,64},{1,5},{2,66},{3,7},{4,68},{5,1},{6,70},{7,3},{8,72},{9,13},... | collective-permute-start | bytes 245768 | tf_op jit(solution)/shard_map/ppermute | solution.py:335
  31.6 5.7 %collective-permute-start.8 = (f32[32,640]{1,0:T(8,128)S(1)}, f32[32,640]{1,0:T(8,128)S(1)}, u32[]{:S(2)}, u32[]{:S(2)}) collective-permute-start(f32[32,640]{1,0:T(8,128)S(1)} %sum_after.5.refs_7_.refs_0_), channel_id=1, source_target_pairs={{0,96},{1,7},{2,98},{3,5},{4,100},{5,3},{6,102},{7,1},{8,104},{9,1... | collective-permute-start | bytes 245768 | tf_op jit(solution)/shard_map/ppermute | solution.py:335
  32.6 4.6 %collective-permute-start.7 = (f32[32,640]{1,0:T(8,128)S(1)}, f32[32,640]{1,0:T(8,128)S(1)}, u32[]{:S(2)}, u32[]{:S(2)}) collective-permute-start(f32[32,640]{1,0:T(8,128)S(1)} %sum_after.5.refs_7_.refs_0_), channel_id=1, source_target_pairs={{0,32},{1,3},{2,34},{3,1},{4,36},{5,7},{6,38},{7,5},{8,40},{9,11},... | collective-permute-start | bytes 245768 | tf_op jit(solution)/shard_map/ppermute | solution.py:335
  37.2 6.0 %collective-permute-start.12 = (f32[32,640]{1,0:T(8,128)S(1)}, f32[32,640]{1,0:T(8,128)S(1)}, u32[]{:S(2)}, u32[]{:S(2)}) collective-permute-start(f32[32,640]{1,0:T(8,128)S(1)} %sum_after.6.refs_0_), channel_id=1, source_target_pairs={{0,4},{1,17},{2,6},{3,19},{4,0},{5,21},{6,2},{7,23},{8,12},{9,25},... | collective-permute-start | bytes 245768 | tf_op jit(solution)/shard_map/ppermute | solution.py:335
  39.2 5.7 %collective-permute-start.11 = (f32[32,640]{1,0:T(8,128)S(1)}, f32[32,640]{1,0:T(8,128)S(1)}, u32[]{:S(2)}, u32[]{:S(2)}) collective-permute-start(f32[32,640]{1,0:T(8,128)S(1)} %sum_after.6.refs_0_), channel_id=1, source_target_pairs={{0,6},{1,25},{2,4},{3,27},{4,2},{5,29},{6,0},{7,31},{8,14},{9,17},... | collective-permute-start | bytes 245768 | tf_op jit(solution)/shard_map/ppermute | solution.py:335
  39.8 5.0 %collective-permute-start.10 = (f32[32,640]{1,0:T(8,128)S(1)}, f32[32,640]{1,0:T(8,128)S(1)}, u32[]{:S(2)}, u32[]{:S(2)}) collective-permute-start(f32[32,640]{1,0:T(8,128)S(1)} %sum_after.6.refs_0_), channel_id=1, source_target_pairs={{0,2},{1,9},{2,0},{3,11},{4,6},{5,13},{6,4},{7,15},{8,10},{9,1},{1... | collective-permute-start | bytes 245768 | tf_op jit(solution)/shard_map/ppermute | solution.py:335
  44.9 2.0 %collective-permute-start.13 = (f32[4,32,640]{2,1,0:T(8,128)S(1)}, f32[4,32,640]{2,1,0:T(8,128)S(1)}, u32[]{:S(2)}, u32[]{:S(2)}) collective-permute-start(f32[4,32,640]{2,1,0:T(8,128)S(1)} %stack_after.1), channel_id=1, source_target_pairs={{0,1},{1,0},{2,3},{3,2},{4,5},{5,4},{6,7},{7,6},{8,9},{9,8},{10,11... | collective-permute-start | bytes 983048 | tf_op jit(solution)/shard_map/ppermute | solution.py:343
  49.6 7.2 %collective-permute-start.16 = (f32[32,640]{1,0:T(8,128)S(1)}, f32[32,640]{1,0:T(8,128)S(1)}, u32[]{:S(2)}, u32[]{:S(2)}) collective-permute-start(f32[32,640]{1,0:T(8,128)S(1)} %get-tuple-element.54.refs_0_), channel_id=1, source_target_pairs={{0,16},{1,65},{2,18},{3,67},{4,20},{5,69},{6,22},{7,71},{8,24},{9,... | collective-permute-start | bytes 245768 | tf_op jit(solution)/shard_map/ppermute | solution.py:335
  52.0 5.7 %collective-permute-start.15 = (f32[32,640]{1,0:T(8,128)S(1)}, f32[32,640]{1,0:T(8,128)S(1)}, u32[]{:S(2)}, u32[]{:S(2)}) collective-permute-start(f32[32,640]{1,0:T(8,128)S(1)} %get-tuple-element.54.refs_0_), channel_id=1, source_target_pairs={{0,24},{1,97},{2,26},{3,99},{4,28},{5,101},{6,30},{7,103},{8,16},{... | collective-permute-start | bytes 245768 | tf_op jit(solution)/shard_map/ppermute | solution.py:335
  53.1 4.5 %collective-permute-start.14 = (f32[32,640]{1,0:T(8,128)S(1)}, f32[32,640]{1,0:T(8,128)S(1)}, u32[]{:S(2)}, u32[]{:S(2)}) collective-permute-start(f32[32,640]{1,0:T(8,128)S(1)} %get-tuple-element.54.refs_0_), channel_id=1, source_target_pairs={{0,8},{1,33},{2,10},{3,35},{4,12},{5,37},{6,14},{7,39},{8,0},{9,41... | collective-permute-start | bytes 245768 | tf_op jit(solution)/shard_map/ppermute | solution.py:335
  57.6 8.1 %copy-start = (s32[640,32]{0,1:T(8,128)S(1)}, s32[640,32]{0,1:T(8,128)}, u32[]{:S(2)}) copy-start(s32[640,32]{0,1:T(8,128)} %param.9) | copy-start | bytes 245764
  57.7 6.0 %collective-permute-start.19 = (f32[32,640]{1,0:T(8,128)S(1)}, f32[32,640]{1,0:T(8,128)S(1)}, u32[]{:S(2)}, u32[]{:S(2)}) collective-permute-start(f32[32,640]{1,0:T(8,128)S(1)} %sum_after.7.refs_5_.a_ref), channel_id=1, source_target_pairs={{0,64},{1,17},{2,66},{3,19},{4,68},{5,21},{6,70},{7,23},{8,72},{9,... | collective-permute-start | bytes 245768 | tf_op jit(solution)/shard_map/ppermute | solution.py:335
  60.1 5.7 %collective-permute-start.18 = (f32[32,640]{1,0:T(8,128)S(1)}, f32[32,640]{1,0:T(8,128)S(1)}, u32[]{:S(2)}, u32[]{:S(2)}) collective-permute-start(f32[32,640]{1,0:T(8,128)S(1)} %sum_after.7.refs_5_.a_ref), channel_id=1, source_target_pairs={{0,96},{1,25},{2,98},{3,27},{4,100},{5,29},{6,102},{7,31},{8,104},... | collective-permute-start | bytes 245768 | tf_op jit(solution)/shard_map/ppermute | solution.py:335
  61.1 4.6 %collective-permute-start.17 = (f32[32,640]{1,0:T(8,128)S(1)}, f32[32,640]{1,0:T(8,128)S(1)}, u32[]{:S(2)}, u32[]{:S(2)}) collective-permute-start(f32[32,640]{1,0:T(8,128)S(1)} %sum_after.7.refs_5_.a_ref), channel_id=1, source_target_pairs={{0,32},{1,9},{2,34},{3,11},{4,36},{5,13},{6,38},{7,15},{8,40},{9,1... | collective-permute-start | bytes 245768 | tf_op jit(solution)/shard_map/ppermute | solution.py:335

commit v4 on v3

--- a/solution.py
+++ b/solution.py
@@ -18,11 +18,10 @@
 HALF = 4
 WORKERS = 16
 MB = 1 << 20
-RING = (1, 3, 2)
+RING = (1, 2, 3)
 OWNER, SECOND, THIRD = "zx", "xy", "yz"
 DP_FIRST, DP_SECOND = "xy", "yx"
-GATHER = (0, *RING)
-ORDER = tuple(2 * r + c for r in GATHER for c in (0, 1))
+ORDER = (0, 1, *(2 * r for r in RING), *(2 * r + 1 for r in RING))
 
 NT = (((1,), (1,)), ((), ()))
 TN = (((0,), (0,)), ((), ()))
@@ -205,23 +204,32 @@
 
 
 def orthonormal_body(gram_ref, *refs):
-    mine, theirs, p3_ref, inv_ref = refs[:HALF], *refs[HALF:]
+    blocks, theirs, p3_ref, inv_ref = refs[: HALF + 1], *refs[HALF + 1 :]
     wide = fold3(gram_ref[...])
     gram = wide[:, :RANK] + wide[:, RANK : 2 * RANK] + wide[:, 2 * RANK :]
     rows = lax.broadcasted_iota(jnp.int32, (RANK, RANK), 0)
     cols = lax.broadcasted_iota(jnp.int32, (RANK, RANK), 1)
     eye = (rows == cols).astype(F32)
     work = jnp.concatenate([gram, eye], axis=1)
-    below = lax.broadcasted_iota(jnp.int32, (RANK, 1), 0)
-    for k in range(RANK):
-        row = work[k : k + 1, :]
-        factor = jnp.where(below > k, work[:, k : k + 1] / row[:, k : k + 1], 0.0)
-        work = work - factor * row
+    wide = (RANK, 2 * RANK)
+    below = lax.broadcasted_iota(jnp.int32, wide, 0)
+    for k in range(0, RANK, 8):
+        col = [jnp.broadcast_to(work[:, k + i : k + i + 1], wide) for i in range(8)]
+        row = [work[k + i : k + i + 1, :] for i in range(8)]
+        factor = []
+        for i in range(8):
+            f = jnp.where(below > k + i, col[i] / col[i][k + i : k + i + 1, :], 0.0)
+            factor.append(f)
+            for j in range(i + 1, 8):
+                col[j] = col[j] - f * col[j][k + i : k + i + 1, :]
+                row[j] = row[j] - f[k + j : k + j + 1, :] * row[i]
+        for f, r in zip(factor, row):
+            work = work - f * r
     diag = jnp.sum(work[:, :RANK] * eye, axis=1, keepdims=True)
     inv = work[:, RANK:] / jnp.sqrt(diag)
     inv_ref[...] = inv
     for k in range(NBLK):
-        block = theirs[k // 2] if k % 2 else mine[k // 2][...]
+        block = theirs[k - HALF - 1] if k > HALF else blocks[k][...]
         p = jnp.dot(inv, block, precision=HIGH, preferred_element_type=F32)
         hi = p.astype(BF16).astype(F32)
         r = p - hi
@@ -230,19 +238,19 @@
         p3_ref[k] = stacked.T.astype(BF16)
 
 
-def orthonormal(gram, mine, theirs):
+def orthonormal(gram, blocks, theirs):
     return pl.pallas_call(
         orthonormal_body,
         out_shape=(
             pltpu.VMEM((NBLK, COLS, 4 * RANK), BF16),
             jax.ShapeDtypeStruct((RANK, RANK), F32),
         ),
-        in_specs=[VM] * (2 + HALF),
+        in_specs=[VM] * (3 + HALF),
         out_specs=(VM, VM),
         compiler_params=params(8),
         cost_estimate=cost(1 << 31),
         name="orthonormal",
-    )(gram, *mine, theirs)
+    )(gram, *blocks, theirs)
 
 
 def update_body(me_ref, a_ref, b_ref, c_ref, d_ref, inv_ref, dither_ref, p3_ref, *rest):
@@ -314,12 +322,12 @@
     return pl.pallas_call(
         body,
         out_shape=jax.ShapeDtypeStruct((n, RANK, COLS), F32),
-        in_specs=[VM] * n + [ANY],
+        in_specs=[VM] * n + [ANY] * len(after),
         out_specs=VM,
         compiler_params=params(8),
         cost_estimate=cost(1000),
         name="stack_after",
-    )(*parts, after)
+    )(*parts, *after)
 
 
 def place(y, x, z, core):
@@ -363,28 +371,31 @@
     part = kept + came[1:]
     from_ring = [exchange(part[r - 1], OWNER, r) for r in RING]
     kept, _ = left_of((0,), 8, grad_v, qt, t3, (part,))
-    own = sum_after([kept[0], came[0], *from_ring], [])
+    memory = memory_blocks((2,), held, grad_v, part)
+    own = sum_after([kept[0], came[0], *from_ring], [memory[2]])
 
     from_ring = ring(own, SECOND)
-    memory = memory_blocks((0, 1, 2), held, grad_v, own)
+    memory |= memory_blocks((0, 3), held, grad_v, own)
     own = sum_after([own, *from_ring], [memory[0]])
     from_ring = ring(own, THIRD)
-    memory |= memory_blocks((3, 4, 5), held, grad_v, own)
-    own = sum_after([own, *from_ring], [memory[3]])
-
-    mine = [own, *ring(own, OWNER)]
-    early = right([(0, own, None)], held, grad_v)
-    theirs = core(stack_after(mine, early[0]))
-    mid = right([(2 * r, x, None) for r, x in zip(RING, mine[1:])], held, grad_v, early)
-    q, gram = right([(2 * r + 1, theirs, i) for i, r in enumerate(GATHER)], held, grad_v, mid, True)
+    memory |= memory_blocks((1, 4), held, grad_v, own)
+    own = sum_after([own, *from_ring], [memory[1]])
+
+    other = core(own)
+    mine = ring(own, OWNER)
+    memory |= memory_blocks((5,), held, grad_v, own)
+    early = right([(0, own, None), (1, other, None)], held, grad_v)
+    theirs = core(stack_after(mine, [early[0], memory[5]]))
+    mid = right([(2 * r, x, None) for r, x in zip(RING, mine)], held, grad_v, early)
+    q, gram = right([(2 * r + 1, theirs, i) for i, r in enumerate(RING)], held, grad_v, mid, True)
 
     from_ring = ring(q, DP_FIRST)
-    p3, inv = orthonormal(gram, mine, theirs)
-    q = sum_after([q, *from_ring], [inv])
+    p3, inv = orthonormal(gram, [own, other, *mine], theirs)
+    memory |= memory_blocks((6,), held, grad_v, q)
+    q = sum_after([q, *from_ring], [inv, memory[6]])
     from_ring = ring(q, DP_SECOND)
-    memory |= memory_blocks((6, 7), held, grad_v, q)
-    blocks = [memory[r] for r in ORDER]
-    q_factor, new_error = update(me, [q, *from_ring], inv, dither.T, p3, blocks)
+    memory |= memory_blocks((7,), held, grad_v, q)
+    q_factor, new_error = update(me, [q, *from_ring], inv, dither.T, p3, [memory[r] for r in ORDER])
     return (q_factor.T, new_error)
 
 

time: 70.1 us -> 68.9 us (0.983)
  waiting for transfers between devices: 11.7 us -> 9.87 us
  starting transfers between devices: 24.5 us -> 26.3 us
  Pallas kernels: 32.7 us -> 31.5 us
    ppermute x18, waiting for transfers between devices: 11.7 us -> 9.86 us  [exchange(): return lax.ppermute(v, ('dp', 'tensor'), pairs)]
    pallas_call x1, Pallas kernels: 3.61 us -> 1.86 us  [orthonormal(): pl.pallas_call(orthonormal_body, out_shape=(pltpu.VMEM((NBLK, COLS, 4 * R...]
    ppermute x18, starting transfers between devices: 24.3 us -> 26 us  [exchange(): return lax.ppermute(v, ('dp', 'tensor'), pairs)]
    pallas_call x3 -> x6, Pallas kernels: 8.71 us -> 9.31 us  [memory_blocks(): pl.pallas_call(body, out_shape=[pltpu.VMEM((COLS, COLS), F32)] * n, in_sp...]
  transfers between devices with their start and end apart: 20 -> 21, of which waited for: 8 -> 7; matrix products, arithmetic and copies ran while one was open for 0% -> 0% of each run, Pallas kernels for 29% -> 29%
where the time goes in v4:
time: 68.9 us; the launch traced here: 68.7 us
  Pallas kernels  31.5 us (46%)
  starting transfers between devices  26.3 us (38%)
  waiting for transfers between devices  9.87 us (14%)
  between operations  1.01 us (1%)
    ppermute x18, starting transfers between devices, exchange(): return lax.ppermute(v, ('dp', 'tensor'), pairs)  26 us
    pallas_call x3, Pallas kernels, left(): pl.pallas_call(body, out_shape=out_shape, in_specs=in_specs, out_specs=[V...  10.9 us
    ppermute x18, waiting for transfers between devices, exchange(): return lax.ppermute(v, ('dp', 'tensor'), pairs)  9.86 us
    pallas_call x6, Pallas kernels, memory_blocks(): pl.pallas_call(body, out_shape=[pltpu.VMEM((COLS, COLS), F32)] * n, in_sp...  9.31 us
    pallas_call x3, Pallas kernels, right(): pl.pallas_call(body, out_shape=shapes, in_specs=[VM] * len(args), out_spe...  5.27 us
    pallas_call x1, Pallas kernels, update(): pl.pallas_call(update_body, out_shape=(jax.ShapeDtypeStruct((RANK, COLS),...  4.05 us
    pallas_call x1, Pallas kernels, orthonormal(): pl.pallas_call(orthonormal_body, out_shape=(pltpu.VMEM((NBLK, COLS, 4 * R...  1.86 us
  transfers between devices with their start and end apart: 21, of which 7 were waited for; matrix products, arithmetic and copies ran while one was open for 0% of the time, Pallas kernels for 29%

profile of v4, /device:TPU:0, one launch (start us, length us, event | category | flops | bytes accessed | tf_op | source)
XLA Modules:
  0.0 68.7 jit_solution(3565297491869391176)
XLA Ops:
  0.6 5.4 %left_first.1 = (f32[4,32,640]{2,1,0:T(8,128)S(1)}, bf16[4,1024,640]{2,1,0:T(8,128)(2,1)S(1)}, bf16[4,640,640]{2,1,0:T(8,128)(2,1)S(1)}, bf16[1024,640]{1,0:T(8,...) custom-call(s32[1]{0:T(128)} %bitcast.me_ref, bf16[1024,5120]{1,0:T(8,128)(2,1)} %acts_hbm.5, ...), custom_call_target="tpu_custom_call" | custom-call | flops 2181038080 | bytes 8388608 | tf_op jit(solution)/shard_map/left_first/pallas_call | solution.py:128
  6.2 3.5 %left_more.2 = (f32[3,32,640]{2,1,0:T(8,128)S(1)}, bf16[3,1024,640]{2,1,0:T(8,128)(2,1)S(1)}, bf16[3,640,640]{2,1,0:T(8,128)(2,1)S(1)}) custom-call(s32[1]{0:T(128)} %bitcast.me_ref, bf16[1024,5120]{1,0:T(8,128)(2,1)} %acts_hbm.5, bf16[5120,640]{1,0:T(8,128)(2,1)} %err_hbm.5, bf16[1024,640]{1,0:T(8,128)(2,1)S(1)} %get-tuple-element.30.grad_in.refs_2_.refs_4_.refs_6_.refs_9_, ...), custom_call_target="tpu_custom_call" | custom-call | flops 1635778560 | bytes 6291456 | tf_op jit(solution)/shard_map/left_more/pallas_call | solution.py:128
  9.8 4.2 %collective-permute-start.3 = (f32[32,640]{1,0:T(8,128)S(1)}, f32[32,640]{1,0:T(8,128)S(1)}, u32[]{:S(2)}, u32[]{:S(2)}) collective-permute-start(f32[32,640]{1,0:T(8,128)S(1)} %get-tuple-element.58), channel_id=1, source_target_pairs={{0,6},{1,25},{2,4},{3,27},{4,2},{5,29},{6,0},{7,31},{8,14},{9,17},... | collective-permute-start | bytes 245768 | tf_op jit(solution)/shard_map/ppermute | solution.py:343
  14.0 0.9 %collective-permute-start.1 = (f32[32,640]{1,0:T(8,128)S(1)}, f32[32,640]{1,0:T(8,128)S(1)}, u32[]{:S(2)}, u32[]{:S(2)}) collective-permute-start(f32[32,640]{1,0:T(8,128)S(1)} %get-tuple-element.60), channel_id=1, source_target_pairs={{0,2},{1,9},{2,0},{3,11},{4,6},{5,13},{6,4},{7,15},{8,10},{9,1},{1... | collective-permute-start | bytes 245768 | tf_op jit(solution)/shard_map/ppermute | solution.py:343
  14.9 2.0 %left_more.3 = (f32[1,32,640]{2,1,0:T(8,128)S(1)}, bf16[1,1024,640]{2,1,0:T(8,128)(2,1)S(1)}, bf16[1,640,640]{2,1,0:T(8,128)(2,1)S(1)}) custom-call(s32[1]{0:T(128)} %bitcast.me_ref, bf16[1024,5120]{1,0:T(8,128)(2,1)} %acts_hbm.5, bf16[5120,640]{1,0:T(8,128)(2,1)} %err_hbm.5, bf16[1024,640]{1,0:T(8,128)(2,1)S(1)} %get-tuple-element.30.grad_in.refs_2_.refs_4_.refs_6_.refs_9_, ...), custom_call_target="tpu_custom_call" | custom-call | flops 545259520 | bytes 2097152 | tf_op jit(solution)/shard_map/left_more/pallas_call | solution.py:128
  16.9 1.2 %memory_blocks.6.refs_5_.rest_2_ = f32[640,640]{1,0:T(8,128)S(1)} custom-call(bf16[3,1024,640]{2,1,0:T(8,128)(2,1)S(1)} %get-tuple-element.36.refs_0_.refs_2_.refs_1_.refs_4_.refs_7_, bf16[3,640,640]{2,1,0:T(8,128)(2,1)S(1)} %get-tuple-element.37.refs_1_.refs_3_.refs_2_.refs_5_.refs_8_, ...), custom_call_target="tpu_custom_call" | custom-call | flops 838860800 | tf_op jit(solution)/shard_map/memory_blocks/pallas_call | solution.py:151
  18.1 1.8 %collective-permute-done.2.refs_3_ = f32[32,640]{1,0:T(8,128)S(1)} collective-permute-done((f32[32,640]{1,0:T(8,128)S(1)}, f32[32,640]{1,0:T(8,128)S(1)}, u32[]{:S(2)}, u32[]{:S(2)}) %collective-permute-start.2) | collective-permute-done | bytes 81952 | tf_op jit(solution)/shard_map/ppermute | solution.py:343
  19.9 2.8 %collective-permute-start.6 = (f32[32,640]{1,0:T(8,128)S(1)}, f32[32,640]{1,0:T(8,128)S(1)}, u32[]{:S(2)}, u32[]{:S(2)}) collective-permute-start(f32[32,640]{1,0:T(8,128)S(1)} %sum_after.4.refs_5_.refs_0_), channel_id=1, source_target_pairs={{0,24},{1,97},{2,26},{3,99},{4,28},{5,101},{6,30},{7,103},{8,16},{... | collective-permute-start | bytes 245768 | tf_op jit(solution)/shard_map/ppermute | solution.py:343
  22.8 0.8 %collective-permute-start.5 = (f32[32,640]{1,0:T(8,128)S(1)}, f32[32,640]{1,0:T(8,128)S(1)}, u32[]{:S(2)}, u32[]{:S(2)}) collective-permute-start(f32[32,640]{1,0:T(8,128)S(1)} %sum_after.4.refs_5_.refs_0_), channel_id=1, source_target_pairs={{0,16},{1,65},{2,18},{3,67},{4,20},{5,69},{6,22},{7,71},{8,24},{9,... | collective-permute-start | bytes 245768 | tf_op jit(solution)/shard_map/ppermute | solution.py:343
  24.1 2.2 %memory_blocks.7 = (f32[640,640]{1,0:T(8,128)S(1)}, f32[640,640]{1,0:T(8,128)S(1)}) custom-call(bf16[1,1024,640]{2,1,0:T(8,128)(2,1)S(1)} %get-tuple-element.38.refs_0_.refs_1_, bf16[1,640,640]{2,1,0:T(8,128)(2,1)S(1)} %get-tuple-element.39.refs_1_.refs_2_, bf16[4,1024,640]{2,1,0:T(8,128)(2,1)S(1)} %get-tuple-element.40.refs_2_.refs_0_.refs_4_.refs_1_.refs_7_, ...), custom_call_target="tpu_custom_call" | custom-call | flops 1677721600 | tf_op jit(solution)/shard_map/memory_blocks/pallas_call | solution.py:151
  26.3 2.4 %collective-permute-done.5.refs_2_ = f32[32,640]{1,0:T(8,128)S(1)} collective-permute-done((f32[32,640]{1,0:T(8,128)S(1)}, f32[32,640]{1,0:T(8,128)S(1)}, u32[]{:S(2)}, u32[]{:S(2)}) %collective-permute-start.5) | collective-permute-done | bytes 81952 | tf_op jit(solution)/shard_map/ppermute | solution.py:343
  28.8 3.1 %collective-permute-start.9 = (f32[32,640]{1,0:T(8,128)S(1)}, f32[32,640]{1,0:T(8,128)S(1)}, u32[]{:S(2)}, u32[]{:S(2)}) collective-permute-start(f32[32,640]{1,0:T(8,128)S(1)} %sum_after.5.refs_5_.refs_0_), channel_id=1, source_target_pairs={{0,96},{1,7},{2,98},{3,5},{4,100},{5,3},{6,102},{7,1},{8,104},{9,1... | collective-permute-start | bytes 245768 | tf_op jit(solution)/shard_map/ppermute | solution.py:343
  32.9 2.2 %memory_blocks.8 = (f32[640,640]{1,0:T(8,128)S(1)}, f32[640,640]{1,0:T(8,128)S(1)}) custom-call(bf16[4,1024,640]{2,1,0:T(8,128)(2,1)S(1)} %get-tuple-element.40.refs_2_.refs_0_.refs_4_.refs_1_.refs_7_, bf16[4,640,640]{2,1,0:T(8,128)(2,1)S(1)} %get-tuple-element.41.refs_3_.refs_1_.refs_5_.refs_2_.refs_8_, ...), custom_call_target="tpu_custom_call" | custom-call | flops 1677721600 | tf_op jit(solution)/shard_map/memory_blocks/pallas_call | solution.py:151
  35.2 2.6 %collective-permute-done.8.refs_2_ = f32[32,640]{1,0:T(8,128)S(1)} collective-permute-done((f32[32,640]{1,0:T(8,128)S(1)}, f32[32,640]{1,0:T(8,128)S(1)}, u32[]{:S(2)}, u32[]{:S(2)}) %collective-permute-start.8) | collective-permute-done | bytes 81952 | tf_op jit(solution)/shard_map/ppermute | solution.py:343
  37.9 1.5 %collective-permute-start.12 = (f32[32,640]{1,0:T(8,128)S(1)}, f32[32,640]{1,0:T(8,128)S(1)}, u32[]{:S(2)}, u32[]{:S(2)}) collective-permute-start(f32[32,640]{1,0:T(8,128)S(1)} %sum_after.6.refs_0_.refs_3_), channel_id=1, source_target_pairs={{0,6},{1,25},{2,4},{3,27},{4,2},{5,29},{6,0},{7,31},{8,14},{9,17},... | collective-permute-start | bytes 245768 | tf_op jit(solution)/shard_map/ppermute | solution.py:343
  40.1 2.0 %collective-permute-start.10 = (f32[32,640]{1,0:T(8,128)S(1)}, f32[32,640]{1,0:T(8,128)S(1)}, u32[]{:S(2)}, u32[]{:S(2)}) collective-permute-start(f32[32,640]{1,0:T(8,128)S(1)} %sum_after.6.refs_0_.refs_3_), channel_id=1, source_target_pairs={{0,2},{1,9},{2,0},{3,11},{4,6},{5,13},{6,4},{7,15},{8,10},{9,1},{1... | collective-permute-start | bytes 245768 | tf_op jit(solution)/shard_map/ppermute | solution.py:343
  42.1 1.2 %memory_blocks.9.refs_4_.rest_6_ = f32[640,640]{1,0:T(8,128)S(1)} custom-call(bf16[4,1024,640]{2,1,0:T(8,128)(2,1)S(1)} %get-tuple-element.40.refs_2_.refs_0_.refs_4_.refs_1_.refs_7_, bf16[4,640,640]{2,1,0:T(8,128)(2,1)S(1)} %get-tuple-element.41.refs_3_.refs_1_.refs_5_.refs_2_.refs_8_, ...), custom_call_target="tpu_custom_call" | custom-call | flops 838860800 | tf_op jit(solution)/shard_map/memory_blocks/pallas_call | solution.py:151
  43.3 1.3 %right_part.2 = (f32[32,1024]{1,0:T(8,128)S(1)}, f32[32,640]{1,0:T(8,128)S(1)}, f32[96,96]{1,0:T(8,128)S(1)}) custom-call(f32[32,640]{1,0:T(8,128)S(1)} %sum_after.6.refs_0_.refs_3_, bf16[1,1024,640]{2,1,0:T(8,128)(2,1)S(1)} %get-tuple-element.38.refs_0_.refs_1_, bf16[1,640,640]{2,1,0:T(8,128)(2,1)S(1)} %get-tuple-element.39.refs_1_.refs_2_, ...), custom_call_target="tpu_custom_call" | custom-call | flops 1090519040 | tf_op jit(solution)/shard_map/right_part/pallas_call | solution.py:195
  44.6 0.8 %collective-permute-done.11.refs_1_.refs_3_ = f32[32,640]{1,0:T(8,128)S(1)} collective-permute-done((f32[32,640]{1,0:T(8,128)S(1)}, f32[32,640]{1,0:T(8,128)S(1)}, u32[]{:S(2)}, u32[]{:S(2)}) %collective-permute-start.11) | collective-permute-done | bytes 81952 | tf_op jit(solution)/shard_map/ppermute | solution.py:343
  45.5 1.9 %right_part.3 = (f32[32,1024]{1,0:T(8,128)S(1)}, f32[32,640]{1,0:T(8,128)S(1)}, f32[96,96]{1,0:T(8,128)S(1)}) custom-call(f32[32,640]{1,0:T(8,128)S(1)} %collective-permute-done.10.refs_0_.refs_2_, bf16[3,1024,640]{2,1,0:T(8,128)(2,1)S(1)} %get-tuple-element.36.refs_0_.refs_2_.refs_1_.refs_4_.refs_7_, ...), custom_call_target="tpu_custom_call" | custom-call | flops 1635778560 | tf_op jit(solution)/shard_map/right_part/pallas_call | solution.py:195
  47.4 2.1 %right_last.1 = (f32[32,640]{1,0:T(8,128)S(1)}, f32[96,96]{1,0:T(8,128)S(1)}) custom-call(f32[3,32,640]{2,1,0:T(8,128)S(1)} %collective-permute-done.14.refs_0_.refs_3_.refs_6_.refs_5_, bf16[4,1024,640]{2,1,0:T(8,128)(2,1)S(1)} %get-tuple-element.40.refs_2_.refs_0_.refs_4_.refs_1_.refs_7_, ...), custom_call_target="tpu_custom_call" | custom-call | flops 1635778560 | tf_op jit(solution)/shard_map/right_last/pallas_call | solution.py:195
  49.5 1.5 %collective-permute-start.17 = (f32[32,640]{1,0:T(8,128)S(1)}, f32[32,640]{1,0:T(8,128)S(1)}, u32[]{:S(2)}, u32[]{:S(2)}) collective-permute-start(f32[32,640]{1,0:T(8,128)S(1)} %get-tuple-element.50.refs_3_.refs_0_), channel_id=1, source_target_pairs={{0,24},{1,97},{2,26},{3,99},{4,28},{5,101},{6,30},{7,103},{8,16},{... | collective-permute-start | bytes 245768 | tf_op jit(solution)/shard_map/ppermute | solution.py:343
  51.0 0.8 %collective-permute-start.16 = (f32[32,640]{1,0:T(8,128)S(1)}, f32[32,640]{1,0:T(8,128)S(1)}, u32[]{:S(2)}, u32[]{:S(2)}) collective-permute-start(f32[32,640]{1,0:T(8,128)S(1)} %get-tuple-element.50.refs_3_.refs_0_), channel_id=1, source_target_pairs={{0,16},{1,65},{2,18},{3,67},{4,20},{5,69},{6,22},{7,71},{8,24},{9,... | collective-permute-start | bytes 245768 | tf_op jit(solution)/shard_map/ppermute | solution.py:343
  51.9 1.8 %collective-permute-start.15 = (f32[32,640]{1,0:T(8,128)S(1)}, f32[32,640]{1,0:T(8,128)S(1)}, u32[]{:S(2)}, u32[]{:S(2)}) collective-permute-start(f32[32,640]{1,0:T(8,128)S(1)} %get-tuple-element.50.refs_3_.refs_0_), channel_id=1, source_target_pairs={{0,8},{1,33},{2,10},{3,35},{4,12},{5,37},{6,14},{7,39},{8,0},{9,41... | collective-permute-start | bytes 245768 | tf_op jit(solution)/shard_map/ppermute | solution.py:343
  53.7 1.9 %orthonormal.1 = (bf16[8,640,128]{2,1,0:T(8,128)(2,1)S(1)}, f32[32,32]{1,0:T(8,128)S(1)}) custom-call(f32[96,96]{1,0:T(8,128)S(1)} %get-tuple-element.51.gram_ref, f32[32,640]{1,0:T(8,128)S(1)} %sum_after.6.refs_0_.refs_3_, f32[32,640]{1,0:T(8,128)S(1)} %collective-permute-done.13.refs_3_.refs_1_, f32[32,640]{1,0:T(8,128)S(1)} %collective-permute-done.10.refs_0_.refs_2_, ...), custom_call_target="tpu_custom_call" | custom-call | flops 2147483648 | tf_op jit(solution)/shard_map/orthonormal/pallas_call | solution.py:242
  55.6 1.2 %memory_blocks.10.refs_5_.rest_4_ = f32[640,640]{1,0:T(8,128)S(1)} custom-call(bf16[3,1024,640]{2,1,0:T(8,128)(2,1)S(1)} %get-tuple-element.36.refs_0_.refs_2_.refs_1_.refs_4_.refs_7_, bf16[3,640,640]{2,1,0:T(8,128)(2,1)S(1)} %get-tuple-element.37.refs_1_.refs_3_.refs_2_.refs_5_.refs_8_, ...), custom_call_target="tpu_custom_call" | custom-call | flops 838860800 | tf_op jit(solution)/shard_map/memory_blocks/pallas_call | solution.py:151
  57.0 1.5 %collective-permute-start.20 = (f32[32,640]{1,0:T(8,128)S(1)}, f32[32,640]{1,0:T(8,128)S(1)}, u32[]{:S(2)}, u32[]{:S(2)}) collective-permute-start(f32[32,640]{1,0:T(8,128)S(1)} %sum_after.7.refs_3_.a_ref), channel_id=1, source_target_pairs={{0,96},{1,25},{2,98},{3,27},{4,100},{5,29},{6,102},{7,31},{8,104},... | collective-permute-start | bytes 245768 | tf_op jit(solution)/shard_map/ppermute | solution.py:343
  58.5 0.8 %collective-permute-start.19 = (f32[32,640]{1,0:T(8,128)S(1)}, f32[32,640]{1,0:T(8,128)S(1)}, u32[]{:S(2)}, u32[]{:S(2)}) collective-permute-start(f32[32,640]{1,0:T(8,128)S(1)} %sum_after.7.refs_3_.a_ref), channel_id=1, source_target_pairs={{0,64},{1,17},{2,66},{3,19},{4,68},{5,21},{6,70},{7,23},{8,72},{9,... | collective-permute-start | bytes 245768 | tf_op jit(solution)/shard_map/ppermute | solution.py:343
  59.3 1.9 %collective-permute-start.18 = (f32[32,640]{1,0:T(8,128)S(1)}, f32[32,640]{1,0:T(8,128)S(1)}, u32[]{:S(2)}, u32[]{:S(2)}) collective-permute-start(f32[32,640]{1,0:T(8,128)S(1)} %sum_after.7.refs_3_.a_ref), channel_id=1, source_target_pairs={{0,32},{1,9},{2,34},{3,11},{4,36},{5,13},{6,38},{7,15},{8,40},{9,1... | collective-permute-start | bytes 245768 | tf_op jit(solution)/shard_map/ppermute | solution.py:343
  61.2 1.2 %memory_blocks.11.rest_7_ = f32[640,640]{1,0:T(8,128)S(1)} custom-call(bf16[4,1024,640]{2,1,0:T(8,128)(2,1)S(1)} %get-tuple-element.40.refs_2_.refs_0_.refs_4_.refs_1_.refs_7_, bf16[4,640,640]{2,1,0:T(8,128)(2,1)S(1)} %get-tuple-element.41.refs_3_.refs_1_.refs_5_.refs_2_.refs_8_, ...), custom_call_target="tpu_custom_call" | custom-call | flops 838860800 | tf_op jit(solution)/shard_map/memory_blocks/pallas_call | solution.py:151
  62.8 1.7 %collective-permute-done.19.c_ref = f32[32,640]{1,0:T(8,128)S(1)} collective-permute-done((f32[32,640]{1,0:T(8,128)S(1)}, f32[32,640]{1,0:T(8,128)S(1)}, u32[]{:S(2)}, u32[]{:S(2)}) %collective-permute-start.19) | collective-permute-done | bytes 81952 | tf_op jit(solution)/shard_map/ppermute | solution.py:343
  64.5 4.1 %update.1 = (bf16[32,640]{1,0:T(8,128)(2,1)}, bf16[5120,640]{1,0:T(8,128)(2,1)}) custom-call(s32[1]{0:T(128)} %bitcast.me_ref, f32[32,640]{1,0:T(8,128)S(1)} %sum_after.7.refs_3_.a_ref, f32[32,640]{1,0:T(8,128)S(1)} %collective-permute-done.18.b_ref, f32[32,640]{1,0:T(8,128)S(1)} %collective-permute-done.19.c_ref, ...), custom_call_target="tpu_custom_call" | custom-call | flops 1677721600 | bytes 7340032 | tf_op jit(solution)/shard_map/update/pallas_call | solution.py:277
  (34 shorter events, 3.3 us)
Async XLA Ops:
  6.1 3.6 %collective-permute-start = (f32[4,32,640]{2,1,0:T(8,128)S(1)}, f32[4,32,640]{2,1,0:T(8,128)S(1)}, u32[]{:S(2)}, u32[]{:S(2)}) collective-permute-start(f32[4,32,640]{2,1,0:T(8,128)S(1)} %get-tuple-element.34), channel_id=1, source_target_pairs={{0,1},{1,0},{2,3},{3,2},{4,5},{5,4},{6,7},{7,6},{8,9},{9,8},{10,11... | collective-permute-start | bytes 983048 | tf_op jit(solution)/shard_map/ppermute | solution.py:351
  9.8 8.3 %collective-permute-start.3 = (f32[32,640]{1,0:T(8,128)S(1)}, f32[32,640]{1,0:T(8,128)S(1)}, u32[]{:S(2)}, u32[]{:S(2)}) collective-permute-start(f32[32,640]{1,0:T(8,128)S(1)} %get-tuple-element.58), channel_id=1, source_target_pairs={{0,6},{1,25},{2,4},{3,27},{4,2},{5,29},{6,0},{7,31},{8,14},{9,17},... | collective-permute-start | bytes 245768 | tf_op jit(solution)/shard_map/ppermute | solution.py:343
  14.0 5.9 %collective-permute-start.2 = (f32[32,640]{1,0:T(8,128)S(1)}, f32[32,640]{1,0:T(8,128)S(1)}, u32[]{:S(2)}, u32[]{:S(2)}) collective-permute-start(f32[32,640]{1,0:T(8,128)S(1)} %get-tuple-element.59), channel_id=1, source_target_pairs={{0,4},{1,17},{2,6},{3,19},{4,0},{5,21},{6,2},{7,23},{8,12},{9,25},... | collective-permute-start | bytes 245768 | tf_op jit(solution)/shard_map/ppermute | solution.py:343
  14.0 5.9 %collective-permute-start.1 = (f32[32,640]{1,0:T(8,128)S(1)}, f32[32,640]{1,0:T(8,128)S(1)}, u32[]{:S(2)}, u32[]{:S(2)}) collective-permute-start(f32[32,640]{1,0:T(8,128)S(1)} %get-tuple-element.60), channel_id=1, source_target_pairs={{0,2},{1,9},{2,0},{3,11},{4,6},{5,13},{6,4},{7,15},{8,10},{9,1},{1... | collective-permute-start | bytes 245768 | tf_op jit(solution)/shard_map/ppermute | solution.py:343
  19.9 6.4 %collective-permute-start.6 = (f32[32,640]{1,0:T(8,128)S(1)}, f32[32,640]{1,0:T(8,128)S(1)}, u32[]{:S(2)}, u32[]{:S(2)}) collective-permute-start(f32[32,640]{1,0:T(8,128)S(1)} %sum_after.4.refs_5_.refs_0_), channel_id=1, source_target_pairs={{0,24},{1,97},{2,26},{3,99},{4,28},{5,101},{6,30},{7,103},{8,16},{... | collective-permute-start | bytes 245768 | tf_op jit(solution)/shard_map/ppermute | solution.py:343
  22.8 5.9 %collective-permute-start.5 = (f32[32,640]{1,0:T(8,128)S(1)}, f32[32,640]{1,0:T(8,128)S(1)}, u32[]{:S(2)}, u32[]{:S(2)}) collective-permute-start(f32[32,640]{1,0:T(8,128)S(1)} %sum_after.4.refs_5_.refs_0_), channel_id=1, source_target_pairs={{0,16},{1,65},{2,18},{3,67},{4,20},{5,69},{6,22},{7,71},{8,24},{9,... | collective-permute-start | bytes 245768 | tf_op jit(solution)/shard_map/ppermute | solution.py:343
  23.6 5.2 %collective-permute-start.4 = (f32[32,640]{1,0:T(8,128)S(1)}, f32[32,640]{1,0:T(8,128)S(1)}, u32[]{:S(2)}, u32[]{:S(2)}) collective-permute-start(f32[32,640]{1,0:T(8,128)S(1)} %sum_after.4.refs_5_.refs_0_), channel_id=1, source_target_pairs={{0,8},{1,33},{2,10},{3,35},{4,12},{5,37},{6,14},{7,39},{8,0},{9,41... | collective-permute-start | bytes 245768 | tf_op jit(solution)/shard_map/ppermute | solution.py:343
  28.8 6.4 %collective-permute-start.9 = (f32[32,640]{1,0:T(8,128)S(1)}, f32[32,640]{1,0:T(8,128)S(1)}, u32[]{:S(2)}, u32[]{:S(2)}) collective-permute-start(f32[32,640]{1,0:T(8,128)S(1)} %sum_after.5.refs_5_.refs_0_), channel_id=1, source_target_pairs={{0,96},{1,7},{2,98},{3,5},{4,100},{5,3},{6,102},{7,1},{8,104},{9,1... | collective-permute-start | bytes 245768 | tf_op jit(solution)/shard_map/ppermute | solution.py:343
  31.9 5.9 %collective-permute-start.8 = (f32[32,640]{1,0:T(8,128)S(1)}, f32[32,640]{1,0:T(8,128)S(1)}, u32[]{:S(2)}, u32[]{:S(2)}) collective-permute-start(f32[32,640]{1,0:T(8,128)S(1)} %sum_after.5.refs_5_.refs_0_), channel_id=1, source_target_pairs={{0,64},{1,5},{2,66},{3,7},{4,68},{5,1},{6,70},{7,3},{8,72},{9,13},... | collective-permute-start | bytes 245768 | tf_op jit(solution)/shard_map/ppermute | solution.py:343
  32.5 5.3 %collective-permute-start.7 = (f32[32,640]{1,0:T(8,128)S(1)}, f32[32,640]{1,0:T(8,128)S(1)}, u32[]{:S(2)}, u32[]{:S(2)}) collective-permute-start(f32[32,640]{1,0:T(8,128)S(1)} %sum_after.5.refs_5_.refs_0_), channel_id=1, source_target_pairs={{0,32},{1,3},{2,34},{3,1},{4,36},{5,7},{6,38},{7,5},{8,40},{9,11},... | collective-permute-start | bytes 245768 | tf_op jit(solution)/shard_map/ppermute | solution.py:343
  37.8 5.5 %collective-permute-start.13 = (f32[32,640]{1,0:T(8,128)S(1)}, f32[32,640]{1,0:T(8,128)S(1)}, u32[]{:S(2)}, u32[]{:S(2)}) collective-permute-start(f32[32,640]{1,0:T(8,128)S(1)} %sum_after.6.refs_0_.refs_3_), channel_id=1, source_target_pairs={{0,1},{1,0},{2,3},{3,2},{4,5},{5,4},{6,7},{7,6},{8,9},{9,8},{10,11... | collective-permute-start | bytes 245768 | tf_op jit(solution)/shard_map/ppermute | solution.py:351
  37.9 6.7 %collective-permute-start.12 = (f32[32,640]{1,0:T(8,128)S(1)}, f32[32,640]{1,0:T(8,128)S(1)}, u32[]{:S(2)}, u32[]{:S(2)}) collective-permute-start(f32[32,640]{1,0:T(8,128)S(1)} %sum_after.6.refs_0_.refs_3_), channel_id=1, source_target_pairs={{0,6},{1,25},{2,4},{3,27},{4,2},{5,29},{6,0},{7,31},{8,14},{9,17},... | collective-permute-start | bytes 245768 | tf_op jit(solution)/shard_map/ppermute | solution.py:343
  39.4 5.9 %collective-permute-start.11 = (f32[32,640]{1,0:T(8,128)S(1)}, f32[32,640]{1,0:T(8,128)S(1)}, u32[]{:S(2)}, u32[]{:S(2)}) collective-permute-start(f32[32,640]{1,0:T(8,128)S(1)} %sum_after.6.refs_0_.refs_3_), channel_id=1, source_target_pairs={{0,4},{1,17},{2,6},{3,19},{4,0},{5,21},{6,2},{7,23},{8,12},{9,25},... | collective-permute-start | bytes 245768 | tf_op jit(solution)/shard_map/ppermute | solution.py:343
  40.1 5.3 %collective-permute-start.10 = (f32[32,640]{1,0:T(8,128)S(1)}, f32[32,640]{1,0:T(8,128)S(1)}, u32[]{:S(2)}, u32[]{:S(2)}) collective-permute-start(f32[32,640]{1,0:T(8,128)S(1)} %sum_after.6.refs_0_.refs_3_), channel_id=1, source_target_pairs={{0,2},{1,9},{2,0},{3,11},{4,6},{5,13},{6,4},{7,15},{8,10},{9,1},{1... | collective-permute-start | bytes 245768 | tf_op jit(solution)/shard_map/ppermute | solution.py:343
  45.4 2.0 %collective-permute-start.14 = (f32[3,32,640]{2,1,0:T(8,128)S(1)}, f32[3,32,640]{2,1,0:T(8,128)S(1)}, u32[]{:S(2)}, u32[]{:S(2)}) collective-permute-start(f32[3,32,640]{2,1,0:T(8,128)S(1)} %stack_after.1), channel_id=1, source_target_pairs={{0,1},{1,0},{2,3},{3,2},{4,5},{5,4},{6,7},{7,6},{8,9},{9,8},{10,11... | collective-permute-start | bytes 737288 | tf_op jit(solution)/shard_map/ppermute | solution.py:351
  49.5 7.3 %collective-permute-start.17 = (f32[32,640]{1,0:T(8,128)S(1)}, f32[32,640]{1,0:T(8,128)S(1)}, u32[]{:S(2)}, u32[]{:S(2)}) collective-permute-start(f32[32,640]{1,0:T(8,128)S(1)} %get-tuple-element.50.refs_3_.refs_0_), channel_id=1, source_target_pairs={{0,24},{1,97},{2,26},{3,99},{4,28},{5,101},{6,30},{7,103},{8,16},{... | collective-permute-start | bytes 245768 | tf_op jit(solution)/shard_map/ppermute | solution.py:343
  51.0 5.9 %collective-permute-start.16 = (f32[32,640]{1,0:T(8,128)S(1)}, f32[32,640]{1,0:T(8,128)S(1)}, u32[]{:S(2)}, u32[]{:S(2)}) collective-permute-start(f32[32,640]{1,0:T(8,128)S(1)} %get-tuple-element.50.refs_3_.refs_0_), channel_id=1, source_target_pairs={{0,16},{1,65},{2,18},{3,67},{4,20},{5,69},{6,22},{7,71},{8,24},{9,... | collective-permute-start | bytes 245768 | tf_op jit(solution)/shard_map/ppermute | solution.py:343
  51.9 5.1 %collective-permute-start.15 = (f32[32,640]{1,0:T(8,128)S(1)}, f32[32,640]{1,0:T(8,128)S(1)}, u32[]{:S(2)}, u32[]{:S(2)}) collective-permute-start(f32[32,640]{1,0:T(8,128)S(1)} %get-tuple-element.50.refs_3_.refs_0_), channel_id=1, source_target_pairs={{0,8},{1,33},{2,10},{3,35},{4,12},{5,37},{6,14},{7,39},{8,0},{9,41... | collective-permute-start | bytes 245768 | tf_op jit(solution)/shard_map/ppermute | solution.py:343
  57.0 7.5 %copy-start = (s32[640,32]{0,1:T(8,128)S(1)}, s32[640,32]{0,1:T(8,128)}, u32[]{:S(2)}) copy-start(s32[640,32]{0,1:T(8,128)} %param.9) | copy-start | bytes 245764
  57.0 5.7 %collective-permute-start.20 = (f32[32,640]{1,0:T(8,128)S(1)}, f32[32,640]{1,0:T(8,128)S(1)}, u32[]{:S(2)}, u32[]{:S(2)}) collective-permute-start(f32[32,640]{1,0:T(8,128)S(1)} %sum_after.7.refs_3_.a_ref), channel_id=1, source_target_pairs={{0,96},{1,25},{2,98},{3,27},{4,100},{5,29},{6,102},{7,31},{8,104},... | collective-permute-start | bytes 245768 | tf_op jit(solution)/shard_map/ppermute | solution.py:343
  58.5 5.9 %collective-permute-start.19 = (f32[32,640]{1,0:T(8,128)S(1)}, f32[32,640]{1,0:T(8,128)S(1)}, u32[]{:S(2)}, u32[]{:S(2)}) collective-permute-start(f32[32,640]{1,0:T(8,128)S(1)} %sum_after.7.refs_3_.a_ref), channel_id=1, source_target_pairs={{0,64},{1,17},{2,66},{3,19},{4,68},{5,21},{6,70},{7,23},{8,72},{9,... | collective-permute-start | bytes 245768 | tf_op jit(solution)/shard_map/ppermute | solution.py:343
  59.3 5.2 %collective-permute-start.18 = (f32[32,640]{1,0:T(8,128)S(1)}, f32[32,640]{1,0:T(8,128)S(1)}, u32[]{:S(2)}, u32[]{:S(2)}) collective-permute-start(f32[32,640]{1,0:T(8,128)S(1)} %sum_after.7.refs_3_.a_ref), channel_id=1, source_target_pairs={{0,32},{1,9},{2,34},{3,11},{4,36},{5,13},{6,38},{7,15},{8,40},{9,1... | collective-permute-start | bytes 245768 | tf_op jit(solution)/shard_map/ppermute | solution.py:343

commit v5 on v4

--- a/solution.py
+++ b/solution.py
@@ -19,7 +19,7 @@
 WORKERS = 16
 MB = 1 << 20
 RING = (1, 2, 3)
-OWNER, SECOND, THIRD = "zx", "xy", "yz"
+OWNER, SECOND, THIRD = "xz", "yx", "zy"
 DP_FIRST, DP_SECOND = "xy", "yx"
 ORDER = (0, 1, *(2 * r for r in RING), *(2 * r + 1 for r in RING))
 
@@ -54,113 +54,218 @@
 def rows_of(me, r):
     core = (me ^ r) & 1
     z, x = (me >> 1) & 3, (me >> 3) & 3
-    block = ((z + core * (x - z)) ^ (r >> 1)) * 2 + core
+    block = ((x + core * (z - x)) ^ (r >> 1)) * 2 + core
     return pl.multiple_of(block * COLS, COLS)
 
 
-def left(rs, limit, me, acts, error, grad, q_seed, t3, after):
-    first = t3 is None
-    n = len(rs)
-
-    def body(me_ref, acts_hbm, err_hbm, grad_in, seed_in, *rest):
-        if first:
-            p_ref, acts_v, err_v, grad_v, t3_ref, qt_ref, sem, gsem, seed_v = rest
-        else:
-            t3_ref, p_ref, acts_v, err_v, sem = rest[:1] + rest[-4:]
-            qt_ref = seed_in
-
-        def columns(k):
-            return pl.ds(rows_of(me_ref[0], rs[k]), COLS)
-
-        acts_copy = [
-            pltpu.make_async_copy(acts_hbm.at[:, columns(k)], acts_v.at[k], sem.at[0, k])
-            for k in range(n)
-        ]
-        err_copy = [
-            pltpu.make_async_copy(err_hbm.at[columns(k), :], err_v.at[k], sem.at[1, k])
-            for k in range(n)
-        ]
-        if first:
-            seed_copy = pltpu.make_async_copy(seed_in, seed_v, gsem.at[0])
-            grad_copy = pltpu.make_async_copy(grad_in, grad_v, gsem.at[1])
-            seed_copy.start()
-            grad_copy.start()
-            for k in range(n):
-                err_copy[k].start()
-            seed_copy.wait()
-            qt_ref[...] = seed_v[...].astype(F32).astype(BF16)
-            grad_copy.wait()
-            acts_copy[0].start()
-            tt = lax.dot_general(qt_ref[...], grad_v[...], NT, preferred_element_type=F32)
-            t3_ref[...] = split3(tt)
-        else:
-            for k in range(n):
-                err_copy[k].start()
-            acts_copy[0].start()
-        for k in range(n):
+def copies_in(me_ref, rs, acts_hbm, acts_v, sem):
+    return [
+        pltpu.make_async_copy(
+            acts_hbm.at[:, pl.ds(rows_of(me_ref[0], r), COLS)], acts_v.at[k], sem.at[k]
+        )
+        for k, r in enumerate(rs)
+    ]
+
+
+def copies_in_rows(me_ref, rs, err_hbm, err_v, sem):
+    return [
+        pltpu.make_async_copy(
+            err_hbm.at[pl.ds(rows_of(me_ref[0], r), COLS), :], err_v.at[k], sem.at[k]
+        )
+        for k, r in enumerate(rs)
+    ]
+
+
+def left_away(me, error, out_grad, seed):
+    rs = (1, 3, 5, 7)
+
+    def body(me_ref, err_hbm, grad_hbm, seed_hbm, away, err_v, grad_v, qt_ref, sem, more, seed_v):
+        seed_copy = pltpu.make_async_copy(seed_hbm, seed_v, more.at[0])
+        grad_copy = pltpu.make_async_copy(grad_hbm, grad_v, more.at[1])
+        err_copy = copies_in_rows(me_ref, rs, err_hbm, err_v, sem)
+        seed_copy.start()
+        err_copy[0].start()
+        err_copy[1].start()
+        grad_copy.start()
+        seed_copy.wait()
+        qt = seed_v[...].astype(F32).astype(BF16)
+        qt_ref[...] = qt
+
+        def multiply(k):
             err_copy[k].wait()
-            if k + 1 < n:
-                acts_copy[k + 1].start()
-            p_ref[k] = lax.dot_general(qt_ref[...], err_v[k], NT, preferred_element_type=F32)
-        for k in range(n):
-            acts_copy[k].wait()
-            p = fold3(jnp.dot(t3_ref[...], acts_v[k], preferred_element_type=F32))
-            p_ref[k] = (p + p_ref[k]) * (1.0 / 32.0)
-
-    out_shape = [
-        jax.ShapeDtypeStruct((n, RANK, COLS), F32),
-        pltpu.VMEM((n, TOK, COLS), BF16),
-        pltpu.VMEM((n, COLS, COLS), BF16),
-    ]
-    scratch = [pltpu.SemaphoreType.DMA((2, n))]
-    if first:
-        out_shape += [
+            if k + 2 < HALF:
+                err_copy[k + 2].start()
+            away[:, k * COLS : (k + 1) * COLS] = lax.dot_general(
+                qt, err_v[k], NT, preferred_element_type=F32
+            )
+
+        multiply(0)
+        multiply(1)
+        grad_copy.wait()
+        away[:, HALF * COLS :] = lax.dot_general(
+            qt, grad_v[...], NT, preferred_element_type=F32
+        )
+        multiply(2)
+        multiply(3)
+
+    away, err_v, grad_v, qt = pl.pallas_call(
+        body,
+        out_shape=[
+            jax.ShapeDtypeStruct((RANK, HALF * COLS + TOK), F32),
+            pltpu.VMEM((HALF, COLS, COLS), BF16),
             pltpu.VMEM((TOK, COLS), BF16),
+            pltpu.VMEM((RANK, COLS), BF16),
+        ],
+        in_specs=[SM, ANY, ANY, ANY],
+        out_specs=[VM] * 4,
+        scratch_shapes=[
+            pltpu.SemaphoreType.DMA((HALF,)),
+            pltpu.SemaphoreType.DMA((2,)),
+            pltpu.VMEM((RANK, COLS), jnp.int32),
+        ],
+        compiler_params=params(8),
+        cost_estimate=cost(2 * HALF * 256 * COLS * COLS, 5 * MB),
+        name="left_away",
+    )(me, error, out_grad, seed)
+    return away, {r: (err_v, k) for k, r in enumerate(rs)}, grad_v, qt
+
+
+def left_kept(me, acts, error, qt):
+    rs = (2, 4, 6)
+
+    def body(me_ref, acts_hbm, err_hbm, qt_ref, kept, acts_v, err_v, sem, acts_sem):
+        err_copy = copies_in_rows(me_ref, rs, err_hbm, err_v, sem)
+        acts_copy = copies_in(me_ref, rs[:1], acts_hbm, acts_v, acts_sem)
+        for c in err_copy + acts_copy:
+            c.start()
+        for k, c in enumerate(err_copy):
+            c.wait()
+            kept[k] = lax.dot_general(qt_ref[...], err_v[k], NT, preferred_element_type=F32)
+        for c in acts_copy:
+            c.wait()
+
+    kept, acts_v, err_v = pl.pallas_call(
+        body,
+        out_shape=[
+            jax.ShapeDtypeStruct((3, RANK, COLS), F32),
+            pltpu.VMEM((1, TOK, COLS), BF16),
+            pltpu.VMEM((3, COLS, COLS), BF16),
+        ],
+        in_specs=[SM, ANY, ANY, VM],
+        out_specs=[VM] * 3,
+        scratch_shapes=[pltpu.SemaphoreType.DMA((3,)), pltpu.SemaphoreType.DMA((1,))],
+        compiler_params=params(8),
+        cost_estimate=cost(2 * 3 * 256 * COLS * COLS, 4 * MB),
+        name="left_kept",
+    )(me, acts, error, qt)
+    return kept, {2: (acts_v, 0)}, {r: (err_v, k) for k, r in enumerate(rs)}
+
+
+def left_sum(me, acts, acts_2, kept, away, came):
+    rs = (4, 6)
+
+    def body(me_ref, acts_hbm, first, kept, away, came, part, acts_v, t3_ref, sem):
+        acts_copy = copies_in(me_ref, rs, acts_hbm, acts_v, sem)
+        for c in acts_copy:
+            c.start()
+        t3_ref[...] = split3(away[:, HALF * COLS :] + came[:, HALF * COLS :])
+        for k in range(3):
+            if k:
+                acts_copy[k - 1].wait()
+            block = acts_v[k - 1] if k else first[0]
+            p = fold3(jnp.dot(t3_ref[...], block, preferred_element_type=F32))
+            p = p + (kept[k] + came[:, (k + 1) * COLS : (k + 2) * COLS])
+            part[k] = p * (1.0 / 32.0)
+
+    part, acts_v, t3 = pl.pallas_call(
+        body,
+        out_shape=[
+            jax.ShapeDtypeStruct((3, RANK, COLS), F32),
+            pltpu.VMEM((2, TOK, COLS), BF16),
             pltpu.VMEM((TRI, TOK), BF16),
-            pltpu.VMEM((RANK, COLS), BF16),
-        ]
-        scratch += [pltpu.SemaphoreType.DMA((2,)), pltpu.VMEM((RANK, COLS), jnp.int32)]
-        args = (me, acts, error, grad, q_seed)
-        in_specs = [SM, ANY, ANY, ANY, ANY]
-    else:
-        args = (me, acts, error, grad, q_seed, t3, *after)
-        in_specs = [SM, ANY, ANY, VM, VM, VM] + [ANY] * len(after)
-    p, acts_v, err_v, *more = pl.pallas_call(
-        body,
-        out_shape=out_shape,
+        ],
+        in_specs=[SM, ANY] + [VM] * 4,
+        out_specs=[VM] * 3,
+        scratch_shapes=[pltpu.SemaphoreType.DMA((2,))],
+        compiler_params=params(8),
+        cost_estimate=cost(2 * 3 * 256 * COLS * TOK, 3 * MB),
+        name="left_sum",
+    )(me, acts, acts_2, kept, away, came)
+    return part, {r: (acts_v, k) for k, r in enumerate(rs)}, t3
+
+
+def left_own(me, acts, error, qt, t3, came, after):
+    def body(me_ref, acts_hbm, err_hbm, qt_ref, t3_ref, came, after_ref, p0, acts_v, err_v, sem):
+        err_copy = copies_in_rows(me_ref, (0,), err_hbm, err_v, sem.at[0])
+        acts_copy = copies_in(me_ref, (0,), acts_hbm, acts_v, sem.at[1])
+        err_copy[0].start()
+        acts_copy[0].start()
+        err_copy[0].wait()
+        p = lax.dot_general(qt_ref[...], err_v[0], NT, preferred_element_type=F32)
+        p = p + came[:, :COLS]
+        acts_copy[0].wait()
+        p = p + fold3(jnp.dot(t3_ref[...], acts_v[0], preferred_element_type=F32))
+        p0[...] = p * (1.0 / 32.0)
+
+    p0, acts_v, err_v = pl.pallas_call(
+        body,
+        out_shape=[
+            jax.ShapeDtypeStruct((RANK, COLS), F32),
+            pltpu.VMEM((1, TOK, COLS), BF16),
+            pltpu.VMEM((1, COLS, COLS), BF16),
+        ],
+        in_specs=[SM, ANY, ANY, VM, VM, VM, ANY],
+        out_specs=[VM] * 3,
+        scratch_shapes=[pltpu.SemaphoreType.DMA((2, 1))],
+        compiler_params=params(8),
+        cost_estimate=cost(2 * 256 * COLS * (TOK + COLS), 2 * MB),
+        name="left_own",
+    )(me, acts, error, qt, t3, came, after)
+    return p0, {0: (acts_v, 0)}, {0: (err_v, 0)}
+
+
+def memory_blocks(rs, held_a, held_e, grad_v, after, load=(), me=None, acts=None):
+    n, m = len(rs), len(load)
+
+    def body(*refs):
+        g_ref, rest = refs[2 * n], refs[2 * n + 2 :]
+        copies = []
+        if m:
+            me_ref, acts_hbm, sem = rest[0], rest[1], rest[-1]
+            rest = rest[2:-1]
+            copies = copies_in(me_ref, load, acts_hbm, rest[n], sem)
+        for c in copies:
+            c.start()
+        for i, r in enumerate(rs):
+            a_ref, e_ref = refs[2 * i : 2 * i + 2]
+            grad = lax.dot_general(
+                a_ref[held_a[r][1]], g_ref[...], TN, preferred_element_type=F32
+            )
+            rest[i][...] = grad + e_ref[held_e[r][1]].astype(F32)
+        for c in copies:
+            c.wait()
+
+    shapes = [pltpu.VMEM((COLS, COLS), F32)] * n
+    args = [x for r in rs for x in (held_a[r][0], held_e[r][0])] + [grad_v, after]
+    in_specs = [VM] * (2 * n + 1) + [ANY]
+    if m:
+        shapes.append(pltpu.VMEM((m, TOK, COLS), BF16))
+        args += [me, acts]
+        in_specs += [SM, ANY]
+    out = pl.pallas_call(
+        body,
+        out_shape=shapes,
         in_specs=in_specs,
-        out_specs=[VM] * len(out_shape),
-        scratch_shapes=scratch,
-        compiler_params=params(limit),
-        cost_estimate=cost(2 * n * 256 * COLS * (TOK + COLS), n * 2 * MB),
-        name="left_first" if first else "left_more",
-    )(*args)
-    return p, {r: (acts_v, err_v, k) for k, r in enumerate(rs)}, more
-
-
-def memory_blocks(rs, held, grad_v, after):
-    n = len(rs)
-
-    def body(*refs):
-        g_ref, outs = refs[2 * n], refs[2 * n + 2 :]
-        for i, r in enumerate(rs):
-            a_ref, e_ref, k = refs[2 * i], refs[2 * i + 1], held[r][2]
-            grad = lax.dot_general(a_ref[k], g_ref[...], TN, preferred_element_type=F32)
-            outs[i][...] = grad + e_ref[k].astype(F32)
-
-    out = pl.pallas_call(
-        body,
-        out_shape=[pltpu.VMEM((COLS, COLS), F32)] * n,
-        in_specs=[VM] * (2 * n + 1) + [ANY],
-        out_specs=[VM] * n,
+        out_specs=[VM] * len(shapes),
+        scratch_shapes=[pltpu.SemaphoreType.DMA((m,))] if m else [],
         compiler_params=params(8),
         cost_estimate=cost(2 * n * COLS * COLS * TOK),
         name="memory_blocks",
-    )(*(x for r in rs for x in held[r][:2]), grad_v, after)
-    return dict(zip(rs, out))
-
-
-def right(work, held, grad_v, earlier=None, last=False):
+    )(*args)
+    return dict(zip(rs, out)), {r: (out[n], k) for k, r in enumerate(load)}
+
+
+def right(work, held_a, held_e, grad_v, earlier=None, last=False):
     n = len(work)
 
     def body(*refs):
@@ -169,10 +274,10 @@
         tmp, q, gram = (x[...] for x in given) if earlier else (0.0, 0.0, 0.0)
         for i, (r, _, entry) in enumerate(work):
             block, a_ref, e_ref = refs[3 * i : 3 * i + 3]
-            k = held[r][2]
+            a, e = a_ref[held_a[r][1]], e_ref[held_e[r][1]]
             p = split3(block[...] if entry is None else block[entry])
-            tmp = tmp + fold3(lax.dot_general(p, a_ref[k], NT, preferred_element_type=F32))
-            q = q + fold3(jnp.dot(p, e_ref[k], preferred_element_type=F32))
+            tmp = tmp + fold3(lax.dot_general(p, a, NT, preferred_element_type=F32))
+            q = q + fold3(jnp.dot(p, e, preferred_element_type=F32))
             gram = gram + lax.dot_general(p, p, NT, preferred_element_type=F32)
         if last:
             q = q + fold3(jnp.dot(split3(tmp), g_ref[...], preferred_element_type=F32))
@@ -190,7 +295,7 @@
     ]
     if last:
         shapes = shapes[1:]
-    args = [x for r, array, _ in work for x in (array, *held[r][:2])]
+    args = [x for r, array, _ in work for x in (array, held_a[r][0], held_e[r][0])]
     args += [grad_v, *(earlier or ())]
     return pl.pallas_call(
         body,
@@ -358,43 +463,49 @@
     out_grad = pltpu.with_memory_space_constraint(out_grad, pltpu.HBM)
     seed = pltpu.with_memory_space_constraint(q_seed.T, pltpu.HBM)
 
-    held = {}
-
-    def left_of(rs, limit, grad, seed, t3, after):
-        p, more_held, more = left(rs, limit, me, acts, error, grad, seed, t3, after)
-        held.update(more_held)
-        return p, more
-
-    away, (grad_v, t3, qt) = left_of((1, 3, 5, 7), 8, out_grad, seed, None, ())
+    away, held_e, grad_v, qt = left_away(me, error, out_grad, seed)
     came = core(away)
-    kept, _ = left_of((2, 4, 6), 8, grad_v, qt, t3, ())
-    part = kept + came[1:]
+    kept, held_a, more_e = left_kept(me, acts, error, qt)
+    held_e |= more_e
+    part, more_a, t3 = left_sum(me, acts, held_a[2][0], kept, away, came)
+    held_a |= more_a
     from_ring = [exchange(part[r - 1], OWNER, r) for r in RING]
-    kept, _ = left_of((0,), 8, grad_v, qt, t3, (part,))
-    memory = memory_blocks((2,), held, grad_v, part)
-    own = sum_after([kept[0], came[0], *from_ring], [memory[2]])
+    own, more_a, more_e = left_own(me, acts, error, qt, t3, came, part)
+    held_a |= more_a
+    held_e |= more_e
+    memory = {}
+
+    def memory_of(rs, after, load=()):
+        blocks, more = memory_blocks(rs, held_a, held_e, grad_v, after, load, me, acts)
+        memory.update(blocks)
+        held_a.update(more)
+
+    memory_of((2,), part)
+    own = sum_after([own, *from_ring], [memory[2]])
 
     from_ring = ring(own, SECOND)
-    memory |= memory_blocks((0, 3), held, grad_v, own)
+    memory_of((0,), own, (1, 3))
     own = sum_after([own, *from_ring], [memory[0]])
     from_ring = ring(own, THIRD)
-    memory |= memory_blocks((1, 4), held, grad_v, own)
-    own = sum_after([own, *from_ring], [memory[1]])
+    memory_of((4,), own, (5, 7))
+    own = sum_after([own, *from_ring], [memory[4]])
 
     other = core(own)
     mine = ring(own, OWNER)
-    memory |= memory_blocks((5,), held, grad_v, own)
-    early = right([(0, own, None), (1, other, None)], held, grad_v)
-    theirs = core(stack_after(mine, [early[0], memory[5]]))
-    mid = right([(2 * r, x, None) for r, x in zip(RING, mine)], held, grad_v, early)
-    q, gram = right([(2 * r + 1, theirs, i) for i, r in enumerate(RING)], held, grad_v, mid, True)
+    memory_of((1,), own)
+    held = (held_a, held_e, grad_v)
+    early = right([(0, own, None), (1, other, None)], *held)
+    early = right([(2 * RING[2], mine[2], None)], *held, early)
+    theirs = core(stack_after(mine, [early[0], memory[1]]))
+    mid = right([(2 * r, x, None) for r, x in zip(RING[:2], mine)], *held, early)
+    q, gram = right([(2 * r + 1, theirs, i) for i, r in enumerate(RING)], *held, mid, True)
 
     from_ring = ring(q, DP_FIRST)
     p3, inv = orthonormal(gram, [own, other, *mine], theirs)
-    memory |= memory_blocks((6,), held, grad_v, q)
-    q = sum_after([q, *from_ring], [inv, memory[6]])
+    memory_of((3,), q)
+    q = sum_after([q, *from_ring], [inv, memory[3]])
     from_ring = ring(q, DP_SECOND)
-    memory |= memory_blocks((7,), held, grad_v, q)
+    memory_of((5, 6, 7), q)
     q_factor, new_error = update(me, [q, *from_ring], inv, dither.T, p3, [memory[r] for r in ORDER])
     return (q_factor.T, new_error)
 

time: 68.9 us -> 68.5 us (level)
  waiting for transfers between devices: 9.87 us -> 7.06 us
  Pallas kernels: 31.5 us -> 33.7 us
    ppermute x18, waiting for transfers between devices: 9.86 us -> 6.87 us  [exchange(): return lax.ppermute(v, ('dp', 'tensor'), pairs)]
    pallas_call x9 -> x10, Pallas kernels: 20.2 us -> 22.3 us  [the longest x6 12 us: memory_blocks(): pl.pallas_call(body, out_shape=shapes, in_specs=in_specs, out_specs=[VM]...]
    pallas_call x3 -> x4, Pallas kernels: 5.27 us -> 5.4 us  [right(): pl.pallas_call(body, out_shape=shapes, in_specs=[VM] * len(args), out_spe...]
  transfers between devices with their start and end apart: 21 -> 21, of which waited for: 7 -> 5; matrix products, arithmetic and copies ran while one was open for 0% -> 0% of each run, Pallas kernels for 29% -> 32%
where the time goes in v5:
time: 68.5 us; the launch traced here: 68.2 us
  Pallas kernels  33.7 us (49%)
  starting transfers between devices  26.4 us (39%)
  waiting for transfers between devices  7.06 us (10%)
  between operations  1.02 us (1%)
    ppermute x18, starting transfers between devices, exchange(): return lax.ppermute(v, ('dp', 'tensor'), pairs)  25.9 us
    pallas_call x6, Pallas kernels, memory_blocks(): pl.pallas_call(body, out_shape=shapes, in_specs=in_specs, out_specs=[VM]...  12 us
    ppermute x18, waiting for transfers between devices, exchange(): return lax.ppermute(v, ('dp', 'tensor'), pairs)  6.87 us
    pallas_call x4, Pallas kernels, right(): pl.pallas_call(body, out_shape=shapes, in_specs=[VM] * len(args), out_spe...  5.4 us
    pallas_call x1, Pallas kernels, update(): pl.pallas_call(update_body, out_shape=(jax.ShapeDtypeStruct((RANK, COLS),...  4.06 us
    pallas_call x1, Pallas kernels, left_away(): pl.pallas_call(body, out_shape=[jax.ShapeDtypeStruct((RANK, HALF * COLS +...  3.53 us
    pallas_call x1, Pallas kernels, left_kept(): pl.pallas_call(body, out_shape=[jax.ShapeDtypeStruct((3, RANK, COLS), F32...  2.47 us
    pallas_call x1, Pallas kernels, left_sum(): pl.pallas_call(body, out_shape=[jax.ShapeDtypeStruct((3, RANK, COLS), F32...  2.32 us
  transfers between devices with their start and end apart: 21, of which 5 were waited for; matrix products, arithmetic and copies ran while one was open for 0% of the time, Pallas kernels for 32%

profile of v5, /device:TPU:0, one launch (start us, length us, event | category | flops | bytes accessed | tf_op | source)
XLA Modules:
  0.0 68.2 jit_solution(2407683216486365343)
XLA Ops:
  0.6 3.5 %left_away.1 = (f32[32,3584]{1,0:T(8,128)S(1)}, bf16[4,640,640]{2,1,0:T(8,128)(2,1)S(1)}, bf16[1024,640]{1,0:T(8,128)(2,1)S(1)}, bf16[32,640]{1,0:T(8,128)(2,1)S(1)}) custom-call(s32[1]{0:T(128)} %bitcast.me_ref.refs_4_, bf16[5120,640]{1,0:T(8,128)(2,1)} %err_hbm.5, bf16[1024,640]{1,0:T(8,128)(2,1)} %grad_hbm.1, s32[32,640]{1,0:T(8,128)} %bitcast.11), custom_call_target="tpu_custom_call" | custom-call | flops 838860800 | bytes 5242880 | tf_op jit(solution)/shard_map/left_away/pallas_call | solution.py:111
  4.3 2.5 %left_kept.1 = (f32[3,32,640]{2,1,0:T(8,128)S(1)}, bf16[1,1024,640]{2,1,0:T(8,128)(2,1)S(1)}, bf16[3,640,640]{2,1,0:T(8,128)(2,1)S(1)}) custom-call(s32[1]{0:T(128)} %bitcast.me_ref.refs_4_, bf16[1024,5120]{1,0:T(8,128)(2,1)} %refs_5_.3, bf16[5120,640]{1,0:T(8,128)(2,1)} %err_hbm.5, bf16[32,640]{1,0:T(8,128)(2,1)S(1)} %get-tuple-element.37.qt_ref), custom_call_target="tpu_custom_call" | custom-call | flops 629145600 | bytes 4194304 | tf_op jit(solution)/shard_map/left_kept/pallas_call | solution.py:147
  6.8 2.3 %left_sum.1 = (f32[3,32,640]{2,1,0:T(8,128)S(1)}, bf16[2,1024,640]{2,1,0:T(8,128)(2,1)S(1)}, bf16[96,1024]{1,0:T(8,128)(2,1)S(1)}) custom-call(s32[1]{0:T(128)} %bitcast.me_ref.refs_4_, bf16[1024,5120]{1,0:T(8,128)(2,1)} %refs_5_.3, bf16[1,1024,640]{2,1,0:T(8,128)(2,1)S(1)} %get-tuple-element.38.first.refs_0_.refs_1_, ...), custom_call_target="tpu_custom_call" | custom-call | flops 1006632960 | bytes 3145728 | tf_op jit(solution)/shard_map/left_sum/pallas_call | solution.py:180
  9.1 2.9 %collective-permute-start.3 = (f32[32,640]{1,0:T(8,128)S(1)}, f32[32,640]{1,0:T(8,128)S(1)}, u32[]{:S(2)}, u32[]{:S(2)}) collective-permute-start(f32[32,640]{1,0:T(8,128)S(1)} %get-tuple-element.72), channel_id=1, source_target_pairs={{0,24},{1,7},{2,26},{3,5},{4,28},{5,3},{6,30},{7,1},{8,16},{9,15},... | collective-permute-start | bytes 245768 | tf_op jit(solution)/shard_map/ppermute | solution.py:448
  12.0 0.8 %collective-permute-start.2 = (f32[32,640]{1,0:T(8,128)S(1)}, f32[32,640]{1,0:T(8,128)S(1)}, u32[]{:S(2)}, u32[]{:S(2)}) collective-permute-start(f32[32,640]{1,0:T(8,128)S(1)} %get-tuple-element.73), channel_id=1, source_target_pairs={{0,16},{1,5},{2,18},{3,7},{4,20},{5,1},{6,22},{7,3},{8,24},{9,13},... | collective-permute-start | bytes 245768 | tf_op jit(solution)/shard_map/ppermute | solution.py:448
  13.3 2.0 %left_own.1 = (f32[32,640]{1,0:T(8,128)S(1)}, bf16[1,1024,640]{2,1,0:T(8,128)(2,1)S(1)}, bf16[1,640,640]{2,1,0:T(8,128)(2,1)S(1)}) custom-call(s32[1]{0:T(128)} %bitcast.me_ref.refs_4_, bf16[1024,5120]{1,0:T(8,128)(2,1)} %refs_5_.3, bf16[5120,640]{1,0:T(8,128)(2,1)} %err_hbm.5, bf16[32,640]{1,0:T(8,128)(2,1)S(1)} %get-tuple-element.37.qt_ref, ...), custom_call_target="tpu_custom_call" | custom-call | flops 545259520 | bytes 2097152 | tf_op jit(solution)/shard_map/left_own/pallas_call | solution.py:210
  15.3 1.2 %memory_blocks.6.refs_4_.rest_2_ = f32[640,640]{1,0:T(8,128)S(1)} custom-call(bf16[1,1024,640]{2,1,0:T(8,128)(2,1)S(1)} %get-tuple-element.38.first.refs_0_.refs_1_, bf16[3,640,640]{2,1,0:T(8,128)(2,1)S(1)} %get-tuple-element.44.refs_1_.refs_2_.refs_5_.refs_3_, bf16[1024,640]{1,0:T(8,128)(2,1)S(1)} %get-tuple-element.45.refs_2_.refs_6_.refs_3_.refs_9_, ...), custom_call_target="tpu_custom_call" | custom-call | flops 838860800 | tf_op jit(solution)/shard_map/memory_blocks/pallas_call | solution.py:255
  16.5 1.5 %collective-permute-done.2.refs_2_ = f32[32,640]{1,0:T(8,128)S(1)} collective-permute-done((f32[32,640]{1,0:T(8,128)S(1)}, f32[32,640]{1,0:T(8,128)S(1)}, u32[]{:S(2)}, u32[]{:S(2)}) %collective-permute-start.2) | collective-permute-done | bytes 81952 | tf_op jit(solution)/shard_map/ppermute | solution.py:448
  18.0 3.1 %collective-permute-start.6 = (f32[32,640]{1,0:T(8,128)S(1)}, f32[32,640]{1,0:T(8,128)S(1)}, u32[]{:S(2)}, u32[]{:S(2)}) collective-permute-start(f32[32,640]{1,0:T(8,128)S(1)} %sum_after.4.refs_3_.refs_0_), channel_id=1, source_target_pairs={{0,96},{1,25},{2,98},{3,27},{4,100},{5,29},{6,102},{7,31},{8,104},... | collective-permute-start | bytes 245768 | tf_op jit(solution)/shard_map/ppermute | solution.py:448
  22.2 2.5 %memory_blocks.7 = (f32[640,640]{1,0:T(8,128)S(1)}, bf16[2,1024,640]{2,1,0:T(8,128)(2,1)S(1)}) custom-call(bf16[1,1024,640]{2,1,0:T(8,128)(2,1)S(1)} %get-tuple-element.46.refs_0_.refs_1_, bf16[1,640,640]{2,1,0:T(8,128)(2,1)S(1)} %get-tuple-element.47.refs_1_.refs_2_, bf16[1024,640]{1,0:T(8,128)(2,1)S(1)} %get-tuple-element.45.refs_2_.refs_6_.refs_3_.refs_9_, ...), custom_call_target="tpu_custom_call" | custom-call | flops 838860800 | tf_op jit(solution)/shard_map/memory_blocks/pallas_call | solution.py:255
  24.7 2.3 %collective-permute-done.5.refs_2_ = f32[32,640]{1,0:T(8,128)S(1)} collective-permute-done((f32[32,640]{1,0:T(8,128)S(1)}, f32[32,640]{1,0:T(8,128)S(1)}, u32[]{:S(2)}, u32[]{:S(2)}) %collective-permute-start.5) | collective-permute-done | bytes 81952 | tf_op jit(solution)/shard_map/ppermute | solution.py:448
  27.1 4.1 %collective-permute-start.9 = (f32[32,640]{1,0:T(8,128)S(1)}, f32[32,640]{1,0:T(8,128)S(1)}, u32[]{:S(2)}, u32[]{:S(2)}) collective-permute-start(f32[32,640]{1,0:T(8,128)S(1)} %sum_after.5.refs_3_.refs_0_), channel_id=1, source_target_pairs={{0,6},{1,97},{2,4},{3,99},{4,2},{5,101},{6,0},{7,103},{8,14},{9,10... | collective-permute-start | bytes 245768 | tf_op jit(solution)/shard_map/ppermute | solution.py:448
  31.2 0.9 %collective-permute-start.7 = (f32[32,640]{1,0:T(8,128)S(1)}, f32[32,640]{1,0:T(8,128)S(1)}, u32[]{:S(2)}, u32[]{:S(2)}) collective-permute-start(f32[32,640]{1,0:T(8,128)S(1)} %sum_after.5.refs_3_.refs_0_), channel_id=1, source_target_pairs={{0,2},{1,33},{2,0},{3,35},{4,6},{5,37},{6,4},{7,39},{8,10},{9,41},... | collective-permute-start | bytes 245768 | tf_op jit(solution)/shard_map/ppermute | solution.py:448
  32.1 2.5 %memory_blocks.8 = (f32[640,640]{1,0:T(8,128)S(1)}, bf16[2,1024,640]{2,1,0:T(8,128)(2,1)S(1)}) custom-call(bf16[2,1024,640]{2,1,0:T(8,128)(2,1)S(1)} %get-tuple-element.49.refs_0_.refs_1_.refs_4_.refs_2_, bf16[3,640,640]{2,1,0:T(8,128)(2,1)S(1)} %get-tuple-element.44.refs_1_.refs_2_.refs_5_.refs_3_, ...), custom_call_target="tpu_custom_call" | custom-call | flops 838860800 | tf_op jit(solution)/shard_map/memory_blocks/pallas_call | solution.py:255
  34.7 2.4 %collective-permute-done.8.refs_2_ = f32[32,640]{1,0:T(8,128)S(1)} collective-permute-done((f32[32,640]{1,0:T(8,128)S(1)}, f32[32,640]{1,0:T(8,128)S(1)}, u32[]{:S(2)}, u32[]{:S(2)}) %collective-permute-start.8) | collective-permute-done | bytes 81952 | tf_op jit(solution)/shard_map/ppermute | solution.py:448
  37.3 1.5 %collective-permute-start.12 = (f32[32,640]{1,0:T(8,128)S(1)}, f32[32,640]{1,0:T(8,128)S(1)}, u32[]{:S(2)}, u32[]{:S(2)}) collective-permute-start(f32[32,640]{1,0:T(8,128)S(1)} %sum_after.6.refs_0_.refs_3_), channel_id=1, source_target_pairs={{0,24},{1,7},{2,26},{3,5},{4,28},{5,3},{6,30},{7,1},{8,16},{9,15},... | collective-permute-start | bytes 245768 | tf_op jit(solution)/shard_map/ppermute | solution.py:448
  38.8 0.9 %collective-permute-start.11 = (f32[32,640]{1,0:T(8,128)S(1)}, f32[32,640]{1,0:T(8,128)S(1)}, u32[]{:S(2)}, u32[]{:S(2)}) collective-permute-start(f32[32,640]{1,0:T(8,128)S(1)} %sum_after.6.refs_0_.refs_3_), channel_id=1, source_target_pairs={{0,16},{1,5},{2,18},{3,7},{4,20},{5,1},{6,22},{7,3},{8,24},{9,13},... | collective-permute-start | bytes 245768 | tf_op jit(solution)/shard_map/ppermute | solution.py:448
  39.6 1.8 %collective-permute-start.10 = (f32[32,640]{1,0:T(8,128)S(1)}, f32[32,640]{1,0:T(8,128)S(1)}, u32[]{:S(2)}, u32[]{:S(2)}) collective-permute-start(f32[32,640]{1,0:T(8,128)S(1)} %sum_after.6.refs_0_.refs_3_), channel_id=1, source_target_pairs={{0,8},{1,3},{2,10},{3,1},{4,12},{5,7},{6,14},{7,5},{8,0},{9,11},{1... | collective-permute-start | bytes 245768 | tf_op jit(solution)/shard_map/ppermute | solution.py:448
  41.4 1.2 %memory_blocks.9.refs_4_.rest_1_ = f32[640,640]{1,0:T(8,128)S(1)} custom-call(bf16[2,1024,640]{2,1,0:T(8,128)(2,1)S(1)} %get-tuple-element.51.refs_4_.refs_0_.refs_1_, bf16[4,640,640]{2,1,0:T(8,128)(2,1)S(1)} %get-tuple-element.52.refs_5_.refs_1_.refs_2_.refs_8_, bf16[1024,640]{1,0:T(8,128)(2,1)S(1)} %get-tuple-element.45.refs_2_.refs_6_.refs_3_.refs_9_, ...), custom_call_target="tpu_custom_call" | custom-call | flops 838860800 | tf_op jit(solution)/shard_map/memory_blocks/pallas_call | solution.py:255
  42.7 1.3 %right_part.3 = (f32[32,1024]{1,0:T(8,128)S(1)}, f32[32,640]{1,0:T(8,128)S(1)}, f32[96,96]{1,0:T(8,128)S(1)}) custom-call(f32[32,640]{1,0:T(8,128)S(1)} %sum_after.6.refs_0_.refs_3_, bf16[1,1024,640]{2,1,0:T(8,128)(2,1)S(1)} %get-tuple-element.46.refs_0_.refs_1_, bf16[1,640,640]{2,1,0:T(8,128)(2,1)S(1)} %get-tuple-element.47.refs_1_.refs_2_, ...), custom_call_target="tpu_custom_call" | custom-call | flops 1090519040 | tf_op jit(solution)/shard_map/right_part/pallas_call | solution.py:300
  45.0 1.3 %right_part.5 = (f32[32,1024]{1,0:T(8,128)S(1)}, f32[32,640]{1,0:T(8,128)S(1)}, f32[96,96]{1,0:T(8,128)S(1)}) custom-call(f32[32,640]{1,0:T(8,128)S(1)} %collective-permute-done.10.refs_0_.refs_2_, bf16[1,1024,640]{2,1,0:T(8,128)(2,1)S(1)} %get-tuple-element.38.first.refs_0_.refs_1_, ...), custom_call_target="tpu_custom_call" | custom-call | flops 1090519040 | tf_op jit(solution)/shard_map/right_part/pallas_call | solution.py:300
  46.5 2.1 %right_last.1 = (f32[32,640]{1,0:T(8,128)S(1)}, f32[96,96]{1,0:T(8,128)S(1)}) custom-call(f32[3,32,640]{2,1,0:T(8,128)S(1)} %collective-permute-done.14.refs_0_.refs_3_.refs_6_.refs_5_, bf16[2,1024,640]{2,1,0:T(8,128)(2,1)S(1)} %get-tuple-element.51.refs_4_.refs_0_.refs_1_, bf16[4,640,640]{2,1,0:T(8,128)(2,1)S(1)} %get-tuple-element.52.refs_5_.refs_1_.refs_2_.refs_8_, ...), custom_call_target="tpu_custom_call" | custom-call | flops 1635778560 | tf_op jit(solution)/shard_map/right_last/pallas_call | solution.py:300
  48.6 1.9 %collective-permute-start.17 = (f32[32,640]{1,0:T(8,128)S(1)}, f32[32,640]{1,0:T(8,128)S(1)}, u32[]{:S(2)}, u32[]{:S(2)}) collective-permute-start(f32[32,640]{1,0:T(8,128)S(1)} %get-tuple-element.63.refs_3_.refs_0_), channel_id=1, source_target_pairs={{0,24},{1,97},{2,26},{3,99},{4,28},{5,101},{6,30},{7,103},{8,16},{... | collective-permute-start | bytes 245768 | tf_op jit(solution)/shard_map/ppermute | solution.py:448
  50.5 1.4 %collective-permute-start.16 = (f32[32,640]{1,0:T(8,128)S(1)}, f32[32,640]{1,0:T(8,128)S(1)}, u32[]{:S(2)}, u32[]{:S(2)}) collective-permute-start(f32[32,640]{1,0:T(8,128)S(1)} %get-tuple-element.63.refs_3_.refs_0_), channel_id=1, source_target_pairs={{0,16},{1,65},{2,18},{3,67},{4,20},{5,69},{6,22},{7,71},{8,24},{9,... | collective-permute-start | bytes 245768 | tf_op jit(solution)/shard_map/ppermute | solution.py:448
  51.9 0.9 %collective-permute-start.15 = (f32[32,640]{1,0:T(8,128)S(1)}, f32[32,640]{1,0:T(8,128)S(1)}, u32[]{:S(2)}, u32[]{:S(2)}) collective-permute-start(f32[32,640]{1,0:T(8,128)S(1)} %get-tuple-element.63.refs_3_.refs_0_), channel_id=1, source_target_pairs={{0,8},{1,33},{2,10},{3,35},{4,12},{5,37},{6,14},{7,39},{8,0},{9,41... | collective-permute-start | bytes 245768 | tf_op jit(solution)/shard_map/ppermute | solution.py:448
  52.8 1.9 %orthonormal.1 = (bf16[8,640,128]{2,1,0:T(8,128)(2,1)S(1)}, f32[32,32]{1,0:T(8,128)S(1)}) custom-call(f32[96,96]{1,0:T(8,128)S(1)} %get-tuple-element.64.gram_ref, f32[32,640]{1,0:T(8,128)S(1)} %sum_after.6.refs_0_.refs_3_, f32[32,640]{1,0:T(8,128)S(1)} %collective-permute-done.13.refs_3_.refs_1_, f32[32,640]{1,0:T(8,128)S(1)} %collective-permute-done.10.refs_0_.refs_2_, ...), custom_call_target="tpu_custom_call" | custom-call | flops 2147483648 | tf_op jit(solution)/shard_map/orthonormal/pallas_call | solution.py:347
  54.7 1.2 %memory_blocks.10.refs_5_.rest_5_ = f32[640,640]{1,0:T(8,128)S(1)} custom-call(bf16[2,1024,640]{2,1,0:T(8,128)(2,1)S(1)} %get-tuple-element.51.refs_4_.refs_0_.refs_1_, bf16[4,640,640]{2,1,0:T(8,128)(2,1)S(1)} %get-tuple-element.52.refs_5_.refs_1_.refs_2_.refs_8_, bf16[1024,640]{1,0:T(8,128)(2,1)S(1)} %get-tuple-element.45.refs_2_.refs_6_.refs_3_.refs_9_, ...), custom_call_target="tpu_custom_call" | custom-call | flops 838860800 | tf_op jit(solution)/shard_map/memory_blocks/pallas_call | solution.py:255
  56.5 1.5 %collective-permute-start.20 = (f32[32,640]{1,0:T(8,128)S(1)}, f32[32,640]{1,0:T(8,128)S(1)}, u32[]{:S(2)}, u32[]{:S(2)}) collective-permute-start(f32[32,640]{1,0:T(8,128)S(1)} %sum_after.7.refs_7_.a_ref), channel_id=1, source_target_pairs={{0,96},{1,25},{2,98},{3,27},{4,100},{5,29},{6,102},{7,31},{8,104},... | collective-permute-start | bytes 245768 | tf_op jit(solution)/shard_map/ppermute | solution.py:448
  58.0 0.8 %collective-permute-start.19 = (f32[32,640]{1,0:T(8,128)S(1)}, f32[32,640]{1,0:T(8,128)S(1)}, u32[]{:S(2)}, u32[]{:S(2)}) collective-permute-start(f32[32,640]{1,0:T(8,128)S(1)} %sum_after.7.refs_7_.a_ref), channel_id=1, source_target_pairs={{0,64},{1,17},{2,66},{3,19},{4,68},{5,21},{6,70},{7,23},{8,72},{9,... | collective-permute-start | bytes 245768 | tf_op jit(solution)/shard_map/ppermute | solution.py:448
  58.8 1.9 %collective-permute-start.18 = (f32[32,640]{1,0:T(8,128)S(1)}, f32[32,640]{1,0:T(8,128)S(1)}, u32[]{:S(2)}, u32[]{:S(2)}) collective-permute-start(f32[32,640]{1,0:T(8,128)S(1)} %sum_after.7.refs_7_.a_ref), channel_id=1, source_target_pairs={{0,32},{1,9},{2,34},{3,11},{4,36},{5,13},{6,38},{7,15},{8,40},{9,1... | collective-permute-start | bytes 245768 | tf_op jit(solution)/shard_map/ppermute | solution.py:448
  60.7 3.2 %memory_blocks.11 = (f32[640,640]{1,0:T(8,128)S(1)}, f32[640,640]{1,0:T(8,128)S(1)}, f32[640,640]{1,0:T(8,128)S(1)}) custom-call(bf16[2,1024,640]{2,1,0:T(8,128)(2,1)S(1)} %get-tuple-element.57.refs_4_.refs_7_.refs_0_, bf16[4,640,640]{2,1,0:T(8,128)(2,1)S(1)} %get-tuple-element.52.refs_5_.refs_1_.refs_2_.refs_8_, ...), custom_call_target="tpu_custom_call" | custom-call | flops 2516582400 | tf_op jit(solution)/shard_map/memory_blocks/pallas_call | solution.py:255
  64.0 4.1 %update.1 = (bf16[32,640]{1,0:T(8,128)(2,1)}, bf16[5120,640]{1,0:T(8,128)(2,1)}) custom-call(s32[1]{0:T(128)} %bitcast.me_ref.refs_4_, f32[32,640]{1,0:T(8,128)S(1)} %sum_after.7.refs_7_.a_ref, f32[32,640]{1,0:T(8,128)S(1)} %collective-permute-done.18.b_ref, f32[32,640]{1,0:T(8,128)S(1)} %collective-permute-done.19.c_ref, ...), custom_call_target="tpu_custom_call" | custom-call | flops 1677721600 | bytes 7340032 | tf_op jit(solution)/shard_map/update/pallas_call | solution.py:382
  (34 shorter events, 3.6 us)
Async XLA Ops:
  4.2 2.6 %collective-permute-start = (f32[32,3584]{1,0:T(8,128)S(1)}, f32[32,3584]{1,0:T(8,128)S(1)}, u32[]{:S(2)}, u32[]{:S(2)}) collective-permute-start(f32[32,3584]{1,0:T(8,128)S(1)} %get-tuple-element.40.away), channel_id=1, source_target_pairs={{0,1},{1,0},{2,3},{3,2},{4,5},{5,4},{6,7},{7,6},{8,9},{9,8},{10,11... | collective-permute-start | bytes 1376264 | tf_op jit(solution)/shard_map/ppermute | solution.py:456
  9.1 7.4 %collective-permute-start.3 = (f32[32,640]{1,0:T(8,128)S(1)}, f32[32,640]{1,0:T(8,128)S(1)}, u32[]{:S(2)}, u32[]{:S(2)}) collective-permute-start(f32[32,640]{1,0:T(8,128)S(1)} %get-tuple-element.72), channel_id=1, source_target_pairs={{0,24},{1,7},{2,26},{3,5},{4,28},{5,3},{6,30},{7,1},{8,16},{9,15},... | collective-permute-start | bytes 245768 | tf_op jit(solution)/shard_map/ppermute | solution.py:448
  12.0 5.9 %collective-permute-start.2 = (f32[32,640]{1,0:T(8,128)S(1)}, f32[32,640]{1,0:T(8,128)S(1)}, u32[]{:S(2)}, u32[]{:S(2)}) collective-permute-start(f32[32,640]{1,0:T(8,128)S(1)} %get-tuple-element.73), channel_id=1, source_target_pairs={{0,16},{1,5},{2,18},{3,7},{4,20},{5,1},{6,22},{7,3},{8,24},{9,13},... | collective-permute-start | bytes 245768 | tf_op jit(solution)/shard_map/ppermute | solution.py:448
  12.8 5.1 %collective-permute-start.1 = (f32[32,640]{1,0:T(8,128)S(1)}, f32[32,640]{1,0:T(8,128)S(1)}, u32[]{:S(2)}, u32[]{:S(2)}) collective-permute-start(f32[32,640]{1,0:T(8,128)S(1)} %get-tuple-element.74), channel_id=1, source_target_pairs={{0,8},{1,3},{2,10},{3,1},{4,12},{5,7},{6,14},{7,5},{8,0},{9,11},{1... | collective-permute-start | bytes 245768 | tf_op jit(solution)/shard_map/ppermute | solution.py:448
  18.0 6.7 %collective-permute-start.6 = (f32[32,640]{1,0:T(8,128)S(1)}, f32[32,640]{1,0:T(8,128)S(1)}, u32[]{:S(2)}, u32[]{:S(2)}) collective-permute-start(f32[32,640]{1,0:T(8,128)S(1)} %sum_after.4.refs_3_.refs_0_), channel_id=1, source_target_pairs={{0,96},{1,25},{2,98},{3,27},{4,100},{5,29},{6,102},{7,31},{8,104},... | collective-permute-start | bytes 245768 | tf_op jit(solution)/shard_map/ppermute | solution.py:448
  21.1 5.9 %collective-permute-start.5 = (f32[32,640]{1,0:T(8,128)S(1)}, f32[32,640]{1,0:T(8,128)S(1)}, u32[]{:S(2)}, u32[]{:S(2)}) collective-permute-start(f32[32,640]{1,0:T(8,128)S(1)} %sum_after.4.refs_3_.refs_0_), channel_id=1, source_target_pairs={{0,64},{1,17},{2,66},{3,19},{4,68},{5,21},{6,70},{7,23},{8,72},{9,... | collective-permute-start | bytes 245768 | tf_op jit(solution)/shard_map/ppermute | solution.py:448
  21.7 5.3 %collective-permute-start.4 = (f32[32,640]{1,0:T(8,128)S(1)}, f32[32,640]{1,0:T(8,128)S(1)}, u32[]{:S(2)}, u32[]{:S(2)}) collective-permute-start(f32[32,640]{1,0:T(8,128)S(1)} %sum_after.4.refs_3_.refs_0_), channel_id=1, source_target_pairs={{0,32},{1,9},{2,34},{3,11},{4,36},{5,13},{6,38},{7,15},{8,40},{9,1... | collective-permute-start | bytes 245768 | tf_op jit(solution)/shard_map/ppermute | solution.py:448
  27.1 7.6 %collective-permute-start.9 = (f32[32,640]{1,0:T(8,128)S(1)}, f32[32,640]{1,0:T(8,128)S(1)}, u32[]{:S(2)}, u32[]{:S(2)}) collective-permute-start(f32[32,640]{1,0:T(8,128)S(1)} %sum_after.5.refs_3_.refs_0_), channel_id=1, source_target_pairs={{0,6},{1,97},{2,4},{3,99},{4,2},{5,101},{6,0},{7,103},{8,14},{9,10... | collective-permute-start | bytes 245768 | tf_op jit(solution)/shard_map/ppermute | solution.py:448
  31.2 5.9 %collective-permute-start.8 = (f32[32,640]{1,0:T(8,128)S(1)}, f32[32,640]{1,0:T(8,128)S(1)}, u32[]{:S(2)}, u32[]{:S(2)}) collective-permute-start(f32[32,640]{1,0:T(8,128)S(1)} %sum_after.5.refs_3_.refs_0_), channel_id=1, source_target_pairs={{0,4},{1,65},{2,6},{3,67},{4,0},{5,69},{6,2},{7,71},{8,12},{9,73},... | collective-permute-start | bytes 245768 | tf_op jit(solution)/shard_map/ppermute | solution.py:448
  31.2 5.9 %collective-permute-start.7 = (f32[32,640]{1,0:T(8,128)S(1)}, f32[32,640]{1,0:T(8,128)S(1)}, u32[]{:S(2)}, u32[]{:S(2)}) collective-permute-start(f32[32,640]{1,0:T(8,128)S(1)} %sum_after.5.refs_3_.refs_0_), channel_id=1, source_target_pairs={{0,2},{1,33},{2,0},{3,35},{4,6},{5,37},{6,4},{7,39},{8,10},{9,41},... | collective-permute-start | bytes 245768 | tf_op jit(solution)/shard_map/ppermute | solution.py:448
  37.2 5.5 %collective-permute-start.13 = (f32[32,640]{1,0:T(8,128)S(1)}, f32[32,640]{1,0:T(8,128)S(1)}, u32[]{:S(2)}, u32[]{:S(2)}) collective-permute-start(f32[32,640]{1,0:T(8,128)S(1)} %sum_after.6.refs_0_.refs_3_), channel_id=1, source_target_pairs={{0,1},{1,0},{2,3},{3,2},{4,5},{5,4},{6,7},{7,6},{8,9},{9,8},{10,11... | collective-permute-start | bytes 245768 | tf_op jit(solution)/shard_map/ppermute | solution.py:456
  37.3 6.7 %collective-permute-start.12 = (f32[32,640]{1,0:T(8,128)S(1)}, f32[32,640]{1,0:T(8,128)S(1)}, u32[]{:S(2)}, u32[]{:S(2)}) collective-permute-start(f32[32,640]{1,0:T(8,128)S(1)} %sum_after.6.refs_0_.refs_3_), channel_id=1, source_target_pairs={{0,24},{1,7},{2,26},{3,5},{4,28},{5,3},{6,30},{7,1},{8,16},{9,15},... | collective-permute-start | bytes 245768 | tf_op jit(solution)/shard_map/ppermute | solution.py:448
  38.8 5.9 %collective-permute-start.11 = (f32[32,640]{1,0:T(8,128)S(1)}, f32[32,640]{1,0:T(8,128)S(1)}, u32[]{:S(2)}, u32[]{:S(2)}) collective-permute-start(f32[32,640]{1,0:T(8,128)S(1)} %sum_after.6.refs_0_.refs_3_), channel_id=1, source_target_pairs={{0,16},{1,5},{2,18},{3,7},{4,20},{5,1},{6,22},{7,3},{8,24},{9,13},... | collective-permute-start | bytes 245768 | tf_op jit(solution)/shard_map/ppermute | solution.py:448
  39.6 5.1 %collective-permute-start.10 = (f32[32,640]{1,0:T(8,128)S(1)}, f32[32,640]{1,0:T(8,128)S(1)}, u32[]{:S(2)}, u32[]{:S(2)}) collective-permute-start(f32[32,640]{1,0:T(8,128)S(1)} %sum_after.6.refs_0_.refs_3_), channel_id=1, source_target_pairs={{0,8},{1,3},{2,10},{3,1},{4,12},{5,7},{6,14},{7,5},{8,0},{9,11},{1... | collective-permute-start | bytes 245768 | tf_op jit(solution)/shard_map/ppermute | solution.py:448
  44.7 1.8 %collective-permute-start.14 = (f32[3,32,640]{2,1,0:T(8,128)S(1)}, f32[3,32,640]{2,1,0:T(8,128)S(1)}, u32[]{:S(2)}, u32[]{:S(2)}) collective-permute-start(f32[3,32,640]{2,1,0:T(8,128)S(1)} %stack_after.1), channel_id=1, source_target_pairs={{0,1},{1,0},{2,3},{3,2},{4,5},{5,4},{6,7},{7,6},{8,9},{9,8},{10,11... | collective-permute-start | bytes 737288 | tf_op jit(solution)/shard_map/ppermute | solution.py:456
  48.6 7.3 %collective-permute-start.17 = (f32[32,640]{1,0:T(8,128)S(1)}, f32[32,640]{1,0:T(8,128)S(1)}, u32[]{:S(2)}, u32[]{:S(2)}) collective-permute-start(f32[32,640]{1,0:T(8,128)S(1)} %get-tuple-element.63.refs_3_.refs_0_), channel_id=1, source_target_pairs={{0,24},{1,97},{2,26},{3,99},{4,28},{5,101},{6,30},{7,103},{8,16},{... | collective-permute-start | bytes 245768 | tf_op jit(solution)/shard_map/ppermute | solution.py:448
  50.5 5.9 %collective-permute-start.16 = (f32[32,640]{1,0:T(8,128)S(1)}, f32[32,640]{1,0:T(8,128)S(1)}, u32[]{:S(2)}, u32[]{:S(2)}) collective-permute-start(f32[32,640]{1,0:T(8,128)S(1)} %get-tuple-element.63.refs_3_.refs_0_), channel_id=1, source_target_pairs={{0,16},{1,65},{2,18},{3,67},{4,20},{5,69},{6,22},{7,71},{8,24},{9,... | collective-permute-start | bytes 245768 | tf_op jit(solution)/shard_map/ppermute | solution.py:448
  51.9 4.5 %collective-permute-start.15 = (f32[32,640]{1,0:T(8,128)S(1)}, f32[32,640]{1,0:T(8,128)S(1)}, u32[]{:S(2)}, u32[]{:S(2)}) collective-permute-start(f32[32,640]{1,0:T(8,128)S(1)} %get-tuple-element.63.refs_3_.refs_0_), channel_id=1, source_target_pairs={{0,8},{1,33},{2,10},{3,35},{4,12},{5,37},{6,14},{7,39},{8,0},{9,41... | collective-permute-start | bytes 245768 | tf_op jit(solution)/shard_map/ppermute | solution.py:448
  56.5 7.5 %copy-start = (s32[640,32]{0,1:T(8,128)S(1)}, s32[640,32]{0,1:T(8,128)}, u32[]{:S(2)}) copy-start(s32[640,32]{0,1:T(8,128)} %param.9) | copy-start | bytes 245764
  56.5 7.4 %collective-permute-start.20 = (f32[32,640]{1,0:T(8,128)S(1)}, f32[32,640]{1,0:T(8,128)S(1)}, u32[]{:S(2)}, u32[]{:S(2)}) collective-permute-start(f32[32,640]{1,0:T(8,128)S(1)} %sum_after.7.refs_7_.a_ref), channel_id=1, source_target_pairs={{0,96},{1,25},{2,98},{3,27},{4,100},{5,29},{6,102},{7,31},{8,104},... | collective-permute-start | bytes 245768 | tf_op jit(solution)/shard_map/ppermute | solution.py:448
  58.0 5.9 %collective-permute-start.19 = (f32[32,640]{1,0:T(8,128)S(1)}, f32[32,640]{1,0:T(8,128)S(1)}, u32[]{:S(2)}, u32[]{:S(2)}) collective-permute-start(f32[32,640]{1,0:T(8,128)S(1)} %sum_after.7.refs_7_.a_ref), channel_id=1, source_target_pairs={{0,64},{1,17},{2,66},{3,19},{4,68},{5,21},{6,70},{7,23},{8,72},{9,... | collective-permute-start | bytes 245768 | tf_op jit(solution)/shard_map/ppermute | solution.py:448
  58.8 5.2 %collective-permute-start.18 = (f32[32,640]{1,0:T(8,128)S(1)}, f32[32,640]{1,0:T(8,128)S(1)}, u32[]{:S(2)}, u32[]{:S(2)}) collective-permute-start(f32[32,640]{1,0:T(8,128)S(1)} %sum_after.7.refs_7_.a_ref), channel_id=1, source_target_pairs={{0,32},{1,9},{2,34},{3,11},{4,36},{5,13},{6,38},{7,15},{8,40},{9,1... | collective-permute-start | bytes 245768 | tf_op jit(solution)/shard_map/ppermute | solution.py:448

commit v6 on v5

--- a/solution.py
+++ b/solution.py
@@ -135,7 +135,7 @@
 
     def body(me_ref, acts_hbm, err_hbm, qt_ref, kept, acts_v, err_v, sem, acts_sem):
         err_copy = copies_in_rows(me_ref, rs, err_hbm, err_v, sem)
-        acts_copy = copies_in(me_ref, rs[:1], acts_hbm, acts_v, acts_sem)
+        acts_copy = copies_in(me_ref, rs, acts_hbm, acts_v, acts_sem)
         for c in err_copy + acts_copy:
             c.start()
         for k, c in enumerate(err_copy):
@@ -148,50 +148,39 @@
         body,
         out_shape=[
             jax.ShapeDtypeStruct((3, RANK, COLS), F32),
-            pltpu.VMEM((1, TOK, COLS), BF16),
+            pltpu.VMEM((3, TOK, COLS), BF16),
             pltpu.VMEM((3, COLS, COLS), BF16),
         ],
         in_specs=[SM, ANY, ANY, VM],
         out_specs=[VM] * 3,
-        scratch_shapes=[pltpu.SemaphoreType.DMA((3,)), pltpu.SemaphoreType.DMA((1,))],
-        compiler_params=params(8),
-        cost_estimate=cost(2 * 3 * 256 * COLS * COLS, 4 * MB),
+        scratch_shapes=[pltpu.SemaphoreType.DMA((3,)), pltpu.SemaphoreType.DMA((3,))],
+        compiler_params=params(8),
+        cost_estimate=cost(2 * 3 * 256 * COLS * COLS, 6 * MB),
         name="left_kept",
     )(me, acts, error, qt)
-    return kept, {2: (acts_v, 0)}, {r: (err_v, k) for k, r in enumerate(rs)}
-
-
-def left_sum(me, acts, acts_2, kept, away, came):
-    rs = (4, 6)
-
-    def body(me_ref, acts_hbm, first, kept, away, came, part, acts_v, t3_ref, sem):
-        acts_copy = copies_in(me_ref, rs, acts_hbm, acts_v, sem)
-        for c in acts_copy:
-            c.start()
+    return kept, {r: (acts_v, k) for k, r in enumerate(rs)}, {r: (err_v, k) for k, r in enumerate(rs)}
+
+
+def left_sum(acts_v, kept, away, came):
+    def body(acts_v, kept, away, came, part, t3_ref):
         t3_ref[...] = split3(away[:, HALF * COLS :] + came[:, HALF * COLS :])
         for k in range(3):
-            if k:
-                acts_copy[k - 1].wait()
-            block = acts_v[k - 1] if k else first[0]
-            p = fold3(jnp.dot(t3_ref[...], block, preferred_element_type=F32))
+            p = fold3(jnp.dot(t3_ref[...], acts_v[k], preferred_element_type=F32))
             p = p + (kept[k] + came[:, (k + 1) * COLS : (k + 2) * COLS])
             part[k] = p * (1.0 / 32.0)
 
-    part, acts_v, t3 = pl.pallas_call(
+    return pl.pallas_call(
         body,
         out_shape=[
             jax.ShapeDtypeStruct((3, RANK, COLS), F32),
-            pltpu.VMEM((2, TOK, COLS), BF16),
             pltpu.VMEM((TRI, TOK), BF16),
         ],
-        in_specs=[SM, ANY] + [VM] * 4,
-        out_specs=[VM] * 3,
-        scratch_shapes=[pltpu.SemaphoreType.DMA((2,))],
-        compiler_params=params(8),
-        cost_estimate=cost(2 * 3 * 256 * COLS * TOK, 3 * MB),
+        in_specs=[VM] * 4,
+        out_specs=[VM] * 2,
+        compiler_params=params(8),
+        cost_estimate=cost(2 * 3 * 256 * COLS * TOK),
         name="left_sum",
-    )(me, acts, acts_2, kept, away, came)
-    return part, {r: (acts_v, k) for k, r in enumerate(rs)}, t3
+    )(acts_v, kept, away, came)
 
 
 def left_own(me, acts, error, qt, t3, came, after):
@@ -467,8 +456,7 @@
     came = core(away)
     kept, held_a, more_e = left_kept(me, acts, error, qt)
     held_e |= more_e
-    part, more_a, t3 = left_sum(me, acts, held_a[2][0], kept, away, came)
-    held_a |= more_a
+    part, t3 = left_sum(held_a[2][0], kept, away, came)
     from_ring = [exchange(part[r - 1], OWNER, r) for r in RING]
     own, more_a, more_e = left_own(me, acts, error, qt, t3, came, part)
     held_a |= more_a
@@ -484,19 +472,18 @@
     own = sum_after([own, *from_ring], [memory[2]])
 
     from_ring = ring(own, SECOND)
-    memory_of((0,), own, (1, 3))
+    memory_of((0,), own, (1, 3, 5))
     own = sum_after([own, *from_ring], [memory[0]])
     from_ring = ring(own, THIRD)
-    memory_of((4,), own, (5, 7))
+    memory_of((4, 1), own, (7,))
     own = sum_after([own, *from_ring], [memory[4]])
 
     other = core(own)
     mine = ring(own, OWNER)
-    memory_of((1,), own)
     held = (held_a, held_e, grad_v)
     early = right([(0, own, None), (1, other, None)], *held)
     early = right([(2 * RING[2], mine[2], None)], *held, early)
-    theirs = core(stack_after(mine, [early[0], memory[1]]))
+    theirs = core(stack_after(mine, [early[0]]))
     mid = right([(2 * r, x, None) for r, x in zip(RING[:2], mine)], *held, early)
     q, gram = right([(2 * r + 1, theirs, i) for i, r in enumerate(RING)], *held, mid, True)
 

time: 68.5 us -> 67.4 us (0.984)
  Pallas kernels: 33.7 us -> 31.9 us
  waiting for transfers between devices: 7.06 us -> 7.86 us
    pallas_call x1, Pallas kernels: 2.32 us -> 0.81 us  [left_sum(): pl.pallas_call(body, out_shape=[jax.ShapeDtypeStruct((3, RANK, COLS), F32...]
    pallas_call x6 -> x5, Pallas kernels: 12 us -> 11.2 us  [memory_blocks(): pl.pallas_call(body, out_shape=shapes, in_specs=in_specs, out_specs=[VM]...]
    ppermute x18, waiting for transfers between devices: 6.87 us -> 7.67 us  [exchange(): return lax.ppermute(v, ('dp', 'tensor'), pairs)]
  transfers between devices with their start and end apart: 21 -> 21, of which waited for: 5 -> 7; matrix products, arithmetic and copies ran while one was open for 0% -> 0% of each run, Pallas kernels for 32% -> 32%
where the time goes in v6:
time: 67.4 us; the launch traced here: 67.1 us
  Pallas kernels  31.9 us (47%)
  starting transfers between devices  26.4 us (39%)
  waiting for transfers between devices  7.86 us (12%)
  between operations  1.01 us (1%)
    ppermute x18, starting transfers between devices, exchange(): return lax.ppermute(v, ('dp', 'tensor'), pairs)  25.9 us
    pallas_call x5, Pallas kernels, memory_blocks(): pl.pallas_call(body, out_shape=shapes, in_specs=in_specs, out_specs=[VM]...  11.2 us
    ppermute x18, waiting for transfers between devices, exchange(): return lax.ppermute(v, ('dp', 'tensor'), pairs)  7.67 us
    pallas_call x4, Pallas kernels, right(): pl.pallas_call(body, out_shape=shapes, in_specs=[VM] * len(args), out_spe...  5.4 us
    pallas_call x1, Pallas kernels, update(): pl.pallas_call(update_body, out_shape=(jax.ShapeDtypeStruct((RANK, COLS),...  4.05 us
    pallas_call x1, Pallas kernels, left_away(): pl.pallas_call(body, out_shape=[jax.ShapeDtypeStruct((RANK, HALF * COLS +...  3.53 us
    pallas_call x1, Pallas kernels, left_kept(): pl.pallas_call(body, out_shape=[jax.ShapeDtypeStruct((3, RANK, COLS), F32...  2.94 us
    pallas_call x1, Pallas kernels, left_own(): pl.pallas_call(body, out_shape=[jax.ShapeDtypeStruct((RANK, COLS), F32),...  1.98 us
  transfers between devices with their start and end apart: 21, of which 7 were waited for; matrix products, arithmetic and copies ran while one was open for 0% of the time, Pallas kernels for 32%

profile of v6, /device:TPU:0, one launch (start us, length us, event | category | flops | bytes accessed | tf_op | source)
XLA Modules:
  0.0 67.1 jit_solution(12699933479976118735)
XLA Ops:
  0.6 3.5 %left_away.1 = (f32[32,3584]{1,0:T(8,128)S(1)}, bf16[4,640,640]{2,1,0:T(8,128)(2,1)S(1)}, bf16[1024,640]{1,0:T(8,128)(2,1)S(1)}, bf16[32,640]{1,0:T(8,128)(2,1)S(1)}) custom-call(s32[1]{0:T(128)} %bitcast.me_ref.refs_4_.refs_6_, bf16[5120,640]{1,0:T(8,128)(2,1)} %err_hbm.5, bf16[1024,640]{1,0:T(8,128)(2,1)} %grad_hbm.1, s32[32,640]{1,0:T(8,128)} %bitcast.11), custom_call_target="tpu_custom_call" | custom-call | flops 838860800 | bytes 5242880 | tf_op jit(solution)/shard_map/left_away/pallas_call | solution.py:111
  4.3 2.9 %left_kept.1 = (f32[3,32,640]{2,1,0:T(8,128)S(1)}, bf16[3,1024,640]{2,1,0:T(8,128)(2,1)S(1)}, bf16[3,640,640]{2,1,0:T(8,128)(2,1)S(1)}) custom-call(s32[1]{0:T(128)} %bitcast.me_ref.refs_4_.refs_6_, bf16[1024,5120]{1,0:T(8,128)(2,1)} %refs_7_.1, bf16[5120,640]{1,0:T(8,128)(2,1)} %err_hbm.5, bf16[32,640]{1,0:T(8,128)(2,1)S(1)} %get-tuple-element.37.qt_ref), custom_call_target="tpu_custom_call" | custom-call | flops 629145600 | bytes 6291456 | tf_op jit(solution)/shard_map/left_kept/pallas_call | solution.py:147
  7.2 0.8 %left_sum.1 = (f32[3,32,640]{2,1,0:T(8,128)S(1)}, bf16[96,1024]{1,0:T(8,128)(2,1)S(1)}) custom-call(bf16[3,1024,640]{2,1,0:T(8,128)(2,1)S(1)} %get-tuple-element.38.acts_v.refs_0_.refs_1_.refs_4_.refs_2_, f32[3,32,640]{2,1,0:T(8,128)S(1)} %get-tuple-element.39.kept, f32[32,3584]{1,0:T(8,128)S(1)} %get-tuple-element.40.away, ...), custom_call_target="tpu_custom_call" | custom-call | flops 1006632960 | tf_op jit(solution)/shard_map/left_sum/pallas_call | solution.py:172
  8.1 2.9 %collective-permute-start.3 = (f32[32,640]{1,0:T(8,128)S(1)}, f32[32,640]{1,0:T(8,128)S(1)}, u32[]{:S(2)}, u32[]{:S(2)}) collective-permute-start(f32[32,640]{1,0:T(8,128)S(1)} %get-tuple-element.72), channel_id=1, source_target_pairs={{0,24},{1,7},{2,26},{3,5},{4,28},{5,3},{6,30},{7,1},{8,16},{9,15},... | collective-permute-start | bytes 245768 | tf_op jit(solution)/shard_map/ppermute | solution.py:437
  11.0 0.8 %collective-permute-start.2 = (f32[32,640]{1,0:T(8,128)S(1)}, f32[32,640]{1,0:T(8,128)S(1)}, u32[]{:S(2)}, u32[]{:S(2)}) collective-permute-start(f32[32,640]{1,0:T(8,128)S(1)} %get-tuple-element.73), channel_id=1, source_target_pairs={{0,16},{1,5},{2,18},{3,7},{4,20},{5,1},{6,22},{7,3},{8,24},{9,13},... | collective-permute-start | bytes 245768 | tf_op jit(solution)/shard_map/ppermute | solution.py:437
  12.2 2.0 %left_own.1 = (f32[32,640]{1,0:T(8,128)S(1)}, bf16[1,1024,640]{2,1,0:T(8,128)(2,1)S(1)}, bf16[1,640,640]{2,1,0:T(8,128)(2,1)S(1)}) custom-call(s32[1]{0:T(128)} %bitcast.me_ref.refs_4_.refs_6_, bf16[1024,5120]{1,0:T(8,128)(2,1)} %refs_7_.1, bf16[5120,640]{1,0:T(8,128)(2,1)} %err_hbm.5, bf16[32,640]{1,0:T(8,128)(2,1)S(1)} %get-tuple-element.37.qt_ref, ...), custom_call_target="tpu_custom_call" | custom-call | flops 545259520 | bytes 2097152 | tf_op jit(solution)/shard_map/left_own/pallas_call | solution.py:199
  14.2 1.2 %memory_blocks.5.refs_4_.rest_2_ = f32[640,640]{1,0:T(8,128)S(1)} custom-call(bf16[3,1024,640]{2,1,0:T(8,128)(2,1)S(1)} %get-tuple-element.38.acts_v.refs_0_.refs_1_.refs_4_.refs_2_, bf16[3,640,640]{2,1,0:T(8,128)(2,1)S(1)} %get-tuple-element.44.refs_1_.refs_2_.refs_5_.refs_3_, ...), custom_call_target="tpu_custom_call" | custom-call | flops 838860800 | tf_op jit(solution)/shard_map/memory_blocks/pallas_call | solution.py:244
  15.5 1.5 %collective-permute-done.2.refs_2_ = f32[32,640]{1,0:T(8,128)S(1)} collective-permute-done((f32[32,640]{1,0:T(8,128)S(1)}, f32[32,640]{1,0:T(8,128)S(1)}, u32[]{:S(2)}, u32[]{:S(2)}) %collective-permute-start.2) | collective-permute-done | bytes 81952 | tf_op jit(solution)/shard_map/ppermute | solution.py:437
  17.0 3.1 %collective-permute-start.6 = (f32[32,640]{1,0:T(8,128)S(1)}, f32[32,640]{1,0:T(8,128)S(1)}, u32[]{:S(2)}, u32[]{:S(2)}) collective-permute-start(f32[32,640]{1,0:T(8,128)S(1)} %sum_after.4.refs_3_.refs_0_), channel_id=1, source_target_pairs={{0,96},{1,25},{2,98},{3,27},{4,100},{5,29},{6,102},{7,31},{8,104},... | collective-permute-start | bytes 245768 | tf_op jit(solution)/shard_map/ppermute | solution.py:437
  21.1 2.7 %memory_blocks.6 = (f32[640,640]{1,0:T(8,128)S(1)}, bf16[3,1024,640]{2,1,0:T(8,128)(2,1)S(1)}) custom-call(bf16[1,1024,640]{2,1,0:T(8,128)(2,1)S(1)} %get-tuple-element.46.refs_0_.refs_1_, bf16[1,640,640]{2,1,0:T(8,128)(2,1)S(1)} %get-tuple-element.47.refs_1_.refs_2_, bf16[1024,640]{1,0:T(8,128)(2,1)S(1)} %get-tuple-element.45.refs_2_.refs_4_.refs_6_.refs_3_.refs_9_, ...), custom_call_target="tpu_custom_call" | custom-call | flops 838860800 | tf_op jit(solution)/shard_map/memory_blocks/pallas_call | solution.py:244
  23.8 2.2 %collective-permute-done.5.refs_2_ = f32[32,640]{1,0:T(8,128)S(1)} collective-permute-done((f32[32,640]{1,0:T(8,128)S(1)}, f32[32,640]{1,0:T(8,128)S(1)}, u32[]{:S(2)}, u32[]{:S(2)}) %collective-permute-start.5) | collective-permute-done | bytes 81952 | tf_op jit(solution)/shard_map/ppermute | solution.py:437
  26.0 4.1 %collective-permute-start.9 = (f32[32,640]{1,0:T(8,128)S(1)}, f32[32,640]{1,0:T(8,128)S(1)}, u32[]{:S(2)}, u32[]{:S(2)}) collective-permute-start(f32[32,640]{1,0:T(8,128)S(1)} %sum_after.5.refs_5_.refs_0_), channel_id=1, source_target_pairs={{0,6},{1,97},{2,4},{3,99},{4,2},{5,101},{6,0},{7,103},{8,14},{9,10... | collective-permute-start | bytes 245768 | tf_op jit(solution)/shard_map/ppermute | solution.py:437
  30.1 0.9 %collective-permute-start.7 = (f32[32,640]{1,0:T(8,128)S(1)}, f32[32,640]{1,0:T(8,128)S(1)}, u32[]{:S(2)}, u32[]{:S(2)}) collective-permute-start(f32[32,640]{1,0:T(8,128)S(1)} %sum_after.5.refs_5_.refs_0_), channel_id=1, source_target_pairs={{0,2},{1,33},{2,0},{3,35},{4,6},{5,37},{6,4},{7,39},{8,10},{9,41},... | collective-permute-start | bytes 245768 | tf_op jit(solution)/shard_map/ppermute | solution.py:437
  31.1 2.9 %memory_blocks.7 = (f32[640,640]{1,0:T(8,128)S(1)}, f32[640,640]{1,0:T(8,128)S(1)}, bf16[1,1024,640]{2,1,0:T(8,128)(2,1)S(1)}) custom-call(bf16[3,1024,640]{2,1,0:T(8,128)(2,1)S(1)} %get-tuple-element.38.acts_v.refs_0_.refs_1_.refs_4_.refs_2_, bf16[3,640,640]{2,1,0:T(8,128)(2,1)S(1)} %get-tuple-element.44.refs_1_.refs_2_.refs_5_.refs_3_, ...), custom_call_target="tpu_custom_call" | custom-call | flops 1677721600 | tf_op jit(solution)/shard_map/memory_blocks/pallas_call | solution.py:244
  34.0 2.1 %collective-permute-done.8.refs_2_ = f32[32,640]{1,0:T(8,128)S(1)} collective-permute-done((f32[32,640]{1,0:T(8,128)S(1)}, f32[32,640]{1,0:T(8,128)S(1)}, u32[]{:S(2)}, u32[]{:S(2)}) %collective-permute-start.8) | collective-permute-done | bytes 81952 | tf_op jit(solution)/shard_map/ppermute | solution.py:437
  36.2 1.5 %collective-permute-start.12 = (f32[32,640]{1,0:T(8,128)S(1)}, f32[32,640]{1,0:T(8,128)S(1)}, u32[]{:S(2)}, u32[]{:S(2)}) collective-permute-start(f32[32,640]{1,0:T(8,128)S(1)} %sum_after.6.refs_0_), channel_id=1, source_target_pairs={{0,24},{1,7},{2,26},{3,5},{4,28},{5,3},{6,30},{7,1},{8,16},{9,15},... | collective-permute-start | bytes 245768 | tf_op jit(solution)/shard_map/ppermute | solution.py:437
  37.7 0.9 %collective-permute-start.11 = (f32[32,640]{1,0:T(8,128)S(1)}, f32[32,640]{1,0:T(8,128)S(1)}, u32[]{:S(2)}, u32[]{:S(2)}) collective-permute-start(f32[32,640]{1,0:T(8,128)S(1)} %sum_after.6.refs_0_), channel_id=1, source_target_pairs={{0,16},{1,5},{2,18},{3,7},{4,20},{5,1},{6,22},{7,3},{8,24},{9,13},... | collective-permute-start | bytes 245768 | tf_op jit(solution)/shard_map/ppermute | solution.py:437
  38.6 1.8 %collective-permute-start.10 = (f32[32,640]{1,0:T(8,128)S(1)}, f32[32,640]{1,0:T(8,128)S(1)}, u32[]{:S(2)}, u32[]{:S(2)}) collective-permute-start(f32[32,640]{1,0:T(8,128)S(1)} %sum_after.6.refs_0_), channel_id=1, source_target_pairs={{0,8},{1,3},{2,10},{3,1},{4,12},{5,7},{6,14},{7,5},{8,0},{9,11},{1... | collective-permute-start | bytes 245768 | tf_op jit(solution)/shard_map/ppermute | solution.py:437
  40.4 1.3 %right_part.3 = (f32[32,1024]{1,0:T(8,128)S(1)}, f32[32,640]{1,0:T(8,128)S(1)}, f32[96,96]{1,0:T(8,128)S(1)}) custom-call(f32[32,640]{1,0:T(8,128)S(1)} %sum_after.6.refs_0_, bf16[1,1024,640]{2,1,0:T(8,128)(2,1)S(1)} %get-tuple-element.46.refs_0_.refs_1_, bf16[1,640,640]{2,1,0:T(8,128)(2,1)S(1)} %get-tuple-element.47.refs_1_.refs_2_, ...), custom_call_target="tpu_custom_call" | custom-call | flops 1090519040 | tf_op jit(solution)/shard_map/right_part/pallas_call | solution.py:289
  42.7 1.0 %collective-permute-done.11.refs_1_.refs_3_ = f32[32,640]{1,0:T(8,128)S(1)} collective-permute-done((f32[32,640]{1,0:T(8,128)S(1)}, f32[32,640]{1,0:T(8,128)S(1)}, u32[]{:S(2)}, u32[]{:S(2)}) %collective-permute-start.11) | collective-permute-done | bytes 81952 | tf_op jit(solution)/shard_map/ppermute | solution.py:437
  44.0 1.3 %right_part.5 = (f32[32,1024]{1,0:T(8,128)S(1)}, f32[32,640]{1,0:T(8,128)S(1)}, f32[96,96]{1,0:T(8,128)S(1)}) custom-call(f32[32,640]{1,0:T(8,128)S(1)} %collective-permute-done.10.refs_0_.refs_2_, bf16[3,1024,640]{2,1,0:T(8,128)(2,1)S(1)} %get-tuple-element.38.acts_v.refs_0_.refs_1_.refs_4_.refs_2_, ...), custom_call_target="tpu_custom_call" | custom-call | flops 1090519040 | tf_op jit(solution)/shard_map/right_part/pallas_call | solution.py:289
  45.5 2.1 %right_last.1 = (f32[32,640]{1,0:T(8,128)S(1)}, f32[96,96]{1,0:T(8,128)S(1)}) custom-call(f32[3,32,640]{2,1,0:T(8,128)S(1)} %collective-permute-done.14.refs_0_.refs_3_.refs_6_.refs_5_, bf16[3,1024,640]{2,1,0:T(8,128)(2,1)S(1)} %get-tuple-element.49.refs_2_.refs_4_.refs_1_.refs_0_, ...), custom_call_target="tpu_custom_call" | custom-call | flops 1635778560 | tf_op jit(solution)/shard_map/right_last/pallas_call | solution.py:289
  47.6 1.9 %collective-permute-start.17 = (f32[32,640]{1,0:T(8,128)S(1)}, f32[32,640]{1,0:T(8,128)S(1)}, u32[]{:S(2)}, u32[]{:S(2)}) collective-permute-start(f32[32,640]{1,0:T(8,128)S(1)} %get-tuple-element.62.refs_3_.refs_0_), channel_id=1, source_target_pairs={{0,24},{1,97},{2,26},{3,99},{4,28},{5,101},{6,30},{7,103},{8,16},{... | collective-permute-start | bytes 245768 | tf_op jit(solution)/shard_map/ppermute | solution.py:437
  49.5 1.4 %collective-permute-start.16 = (f32[32,640]{1,0:T(8,128)S(1)}, f32[32,640]{1,0:T(8,128)S(1)}, u32[]{:S(2)}, u32[]{:S(2)}) collective-permute-start(f32[32,640]{1,0:T(8,128)S(1)} %get-tuple-element.62.refs_3_.refs_0_), channel_id=1, source_target_pairs={{0,16},{1,65},{2,18},{3,67},{4,20},{5,69},{6,22},{7,71},{8,24},{9,... | collective-permute-start | bytes 245768 | tf_op jit(solution)/shard_map/ppermute | solution.py:437
  50.9 0.9 %collective-permute-start.15 = (f32[32,640]{1,0:T(8,128)S(1)}, f32[32,640]{1,0:T(8,128)S(1)}, u32[]{:S(2)}, u32[]{:S(2)}) collective-permute-start(f32[32,640]{1,0:T(8,128)S(1)} %get-tuple-element.62.refs_3_.refs_0_), channel_id=1, source_target_pairs={{0,8},{1,33},{2,10},{3,35},{4,12},{5,37},{6,14},{7,39},{8,0},{9,41... | collective-permute-start | bytes 245768 | tf_op jit(solution)/shard_map/ppermute | solution.py:437
  51.8 1.9 %orthonormal.1 = (bf16[8,640,128]{2,1,0:T(8,128)(2,1)S(1)}, f32[32,32]{1,0:T(8,128)S(1)}) custom-call(f32[96,96]{1,0:T(8,128)S(1)} %get-tuple-element.63.gram_ref, f32[32,640]{1,0:T(8,128)S(1)} %sum_after.6.refs_0_, f32[32,640]{1,0:T(8,128)S(1)} %collective-permute-done.13.refs_3_.refs_1_, f32[32,640]{1,0:T(8,128)S(1)} %collective-permute-done.10.refs_0_.refs_2_, ...), custom_call_target="tpu_custom_call" | custom-call | flops 2147483648 | tf_op jit(solution)/shard_map/orthonormal/pallas_call | solution.py:336
  53.6 1.2 %memory_blocks.8.refs_5_.rest_5_ = f32[640,640]{1,0:T(8,128)S(1)} custom-call(bf16[3,1024,640]{2,1,0:T(8,128)(2,1)S(1)} %get-tuple-element.49.refs_2_.refs_4_.refs_1_.refs_0_, bf16[4,640,640]{2,1,0:T(8,128)(2,1)S(1)} %get-tuple-element.50.refs_3_.refs_5_.refs_2_.refs_8_.refs_1_, ...), custom_call_target="tpu_custom_call" | custom-call | flops 838860800 | tf_op jit(solution)/shard_map/memory_blocks/pallas_call | solution.py:244
  55.4 1.5 %collective-permute-start.20 = (f32[32,640]{1,0:T(8,128)S(1)}, f32[32,640]{1,0:T(8,128)S(1)}, u32[]{:S(2)}, u32[]{:S(2)}) collective-permute-start(f32[32,640]{1,0:T(8,128)S(1)} %sum_after.7.refs_7_.a_ref), channel_id=1, source_target_pairs={{0,96},{1,25},{2,98},{3,27},{4,100},{5,29},{6,102},{7,31},{8,104},... | collective-permute-start | bytes 245768 | tf_op jit(solution)/shard_map/ppermute | solution.py:437
  57.0 0.8 %collective-permute-start.19 = (f32[32,640]{1,0:T(8,128)S(1)}, f32[32,640]{1,0:T(8,128)S(1)}, u32[]{:S(2)}, u32[]{:S(2)}) collective-permute-start(f32[32,640]{1,0:T(8,128)S(1)} %sum_after.7.refs_7_.a_ref), channel_id=1, source_target_pairs={{0,64},{1,17},{2,66},{3,19},{4,68},{5,21},{6,70},{7,23},{8,72},{9,... | collective-permute-start | bytes 245768 | tf_op jit(solution)/shard_map/ppermute | solution.py:437
  57.7 1.9 %collective-permute-start.18 = (f32[32,640]{1,0:T(8,128)S(1)}, f32[32,640]{1,0:T(8,128)S(1)}, u32[]{:S(2)}, u32[]{:S(2)}) collective-permute-start(f32[32,640]{1,0:T(8,128)S(1)} %sum_after.7.refs_7_.a_ref), channel_id=1, source_target_pairs={{0,32},{1,9},{2,34},{3,11},{4,36},{5,13},{6,38},{7,15},{8,40},{9,1... | collective-permute-start | bytes 245768 | tf_op jit(solution)/shard_map/ppermute | solution.py:437
  59.6 3.2 %memory_blocks.9 = (f32[640,640]{1,0:T(8,128)S(1)}, f32[640,640]{1,0:T(8,128)S(1)}, f32[640,640]{1,0:T(8,128)S(1)}) custom-call(bf16[3,1024,640]{2,1,0:T(8,128)(2,1)S(1)} %get-tuple-element.49.refs_2_.refs_4_.refs_1_.refs_0_, bf16[4,640,640]{2,1,0:T(8,128)(2,1)S(1)} %get-tuple-element.50.refs_3_.refs_5_.refs_2_.refs_8_.refs_1_, ...), custom_call_target="tpu_custom_call" | custom-call | flops 2516582400 | tf_op jit(solution)/shard_map/memory_blocks/pallas_call | solution.py:244
  62.9 4.1 %update.1 = (bf16[32,640]{1,0:T(8,128)(2,1)}, bf16[5120,640]{1,0:T(8,128)(2,1)}) custom-call(s32[1]{0:T(128)} %bitcast.me_ref.refs_4_.refs_6_, f32[32,640]{1,0:T(8,128)S(1)} %sum_after.7.refs_7_.a_ref, f32[32,640]{1,0:T(8,128)S(1)} %collective-permute-done.18.b_ref, f32[32,640]{1,0:T(8,128)S(1)} %collective-permute-done.19.c_ref, ...), custom_call_target="tpu_custom_call" | custom-call | flops 1677721600 | bytes 7340032 | tf_op jit(solution)/shard_map/update/pallas_call | solution.py:371
  (33 shorter events, 3.9 us)
Async XLA Ops:
  4.2 3.0 %collective-permute-start = (f32[32,3584]{1,0:T(8,128)S(1)}, f32[32,3584]{1,0:T(8,128)S(1)}, u32[]{:S(2)}, u32[]{:S(2)}) collective-permute-start(f32[32,3584]{1,0:T(8,128)S(1)} %get-tuple-element.40.away), channel_id=1, source_target_pairs={{0,1},{1,0},{2,3},{3,2},{4,5},{5,4},{6,7},{7,6},{8,9},{9,8},{10,11... | collective-permute-start | bytes 1376264 | tf_op jit(solution)/shard_map/ppermute | solution.py:445
  8.1 7.4 %collective-permute-start.3 = (f32[32,640]{1,0:T(8,128)S(1)}, f32[32,640]{1,0:T(8,128)S(1)}, u32[]{:S(2)}, u32[]{:S(2)}) collective-permute-start(f32[32,640]{1,0:T(8,128)S(1)} %get-tuple-element.72), channel_id=1, source_target_pairs={{0,24},{1,7},{2,26},{3,5},{4,28},{5,3},{6,30},{7,1},{8,16},{9,15},... | collective-permute-start | bytes 245768 | tf_op jit(solution)/shard_map/ppermute | solution.py:437
  11.0 5.9 %collective-permute-start.2 = (f32[32,640]{1,0:T(8,128)S(1)}, f32[32,640]{1,0:T(8,128)S(1)}, u32[]{:S(2)}, u32[]{:S(2)}) collective-permute-start(f32[32,640]{1,0:T(8,128)S(1)} %get-tuple-element.73), channel_id=1, source_target_pairs={{0,16},{1,5},{2,18},{3,7},{4,20},{5,1},{6,22},{7,3},{8,24},{9,13},... | collective-permute-start | bytes 245768 | tf_op jit(solution)/shard_map/ppermute | solution.py:437
  11.8 5.1 %collective-permute-start.1 = (f32[32,640]{1,0:T(8,128)S(1)}, f32[32,640]{1,0:T(8,128)S(1)}, u32[]{:S(2)}, u32[]{:S(2)}) collective-permute-start(f32[32,640]{1,0:T(8,128)S(1)} %get-tuple-element.74), channel_id=1, source_target_pairs={{0,8},{1,3},{2,10},{3,1},{4,12},{5,7},{6,14},{7,5},{8,0},{9,11},{1... | collective-permute-start | bytes 245768 | tf_op jit(solution)/shard_map/ppermute | solution.py:437
  17.0 6.8 %collective-permute-start.6 = (f32[32,640]{1,0:T(8,128)S(1)}, f32[32,640]{1,0:T(8,128)S(1)}, u32[]{:S(2)}, u32[]{:S(2)}) collective-permute-start(f32[32,640]{1,0:T(8,128)S(1)} %sum_after.4.refs_3_.refs_0_), channel_id=1, source_target_pairs={{0,96},{1,25},{2,98},{3,27},{4,100},{5,29},{6,102},{7,31},{8,104},... | collective-permute-start | bytes 245768 | tf_op jit(solution)/shard_map/ppermute | solution.py:437
  20.1 5.9 %collective-permute-start.5 = (f32[32,640]{1,0:T(8,128)S(1)}, f32[32,640]{1,0:T(8,128)S(1)}, u32[]{:S(2)}, u32[]{:S(2)}) collective-permute-start(f32[32,640]{1,0:T(8,128)S(1)} %sum_after.4.refs_3_.refs_0_), channel_id=1, source_target_pairs={{0,64},{1,17},{2,66},{3,19},{4,68},{5,21},{6,70},{7,23},{8,72},{9,... | collective-permute-start | bytes 245768 | tf_op jit(solution)/shard_map/ppermute | solution.py:437
  20.7 5.3 %collective-permute-start.4 = (f32[32,640]{1,0:T(8,128)S(1)}, f32[32,640]{1,0:T(8,128)S(1)}, u32[]{:S(2)}, u32[]{:S(2)}) collective-permute-start(f32[32,640]{1,0:T(8,128)S(1)} %sum_after.4.refs_3_.refs_0_), channel_id=1, source_target_pairs={{0,32},{1,9},{2,34},{3,11},{4,36},{5,13},{6,38},{7,15},{8,40},{9,1... | collective-permute-start | bytes 245768 | tf_op jit(solution)/shard_map/ppermute | solution.py:437
  26.0 8.0 %collective-permute-start.9 = (f32[32,640]{1,0:T(8,128)S(1)}, f32[32,640]{1,0:T(8,128)S(1)}, u32[]{:S(2)}, u32[]{:S(2)}) collective-permute-start(f32[32,640]{1,0:T(8,128)S(1)} %sum_after.5.refs_5_.refs_0_), channel_id=1, source_target_pairs={{0,6},{1,97},{2,4},{3,99},{4,2},{5,101},{6,0},{7,103},{8,14},{9,10... | collective-permute-start | bytes 245768 | tf_op jit(solution)/shard_map/ppermute | solution.py:437
  30.1 5.9 %collective-permute-start.8 = (f32[32,640]{1,0:T(8,128)S(1)}, f32[32,640]{1,0:T(8,128)S(1)}, u32[]{:S(2)}, u32[]{:S(2)}) collective-permute-start(f32[32,640]{1,0:T(8,128)S(1)} %sum_after.5.refs_5_.refs_0_), channel_id=1, source_target_pairs={{0,4},{1,65},{2,6},{3,67},{4,0},{5,69},{6,2},{7,71},{8,12},{9,73},... | collective-permute-start | bytes 245768 | tf_op jit(solution)/shard_map/ppermute | solution.py:437
  30.1 5.9 %collective-permute-start.7 = (f32[32,640]{1,0:T(8,128)S(1)}, f32[32,640]{1,0:T(8,128)S(1)}, u32[]{:S(2)}, u32[]{:S(2)}) collective-permute-start(f32[32,640]{1,0:T(8,128)S(1)} %sum_after.5.refs_5_.refs_0_), channel_id=1, source_target_pairs={{0,2},{1,33},{2,0},{3,35},{4,6},{5,37},{6,4},{7,39},{8,10},{9,41},... | collective-permute-start | bytes 245768 | tf_op jit(solution)/shard_map/ppermute | solution.py:437
  36.1 4.3 %collective-permute-start.13 = (f32[32,640]{1,0:T(8,128)S(1)}, f32[32,640]{1,0:T(8,128)S(1)}, u32[]{:S(2)}, u32[]{:S(2)}) collective-permute-start(f32[32,640]{1,0:T(8,128)S(1)} %sum_after.6.refs_0_), channel_id=1, source_target_pairs={{0,1},{1,0},{2,3},{3,2},{4,5},{5,4},{6,7},{7,6},{8,9},{9,8},{10,11... | collective-permute-start | bytes 245768 | tf_op jit(solution)/shard_map/ppermute | solution.py:445
  36.2 5.7 %collective-permute-start.12 = (f32[32,640]{1,0:T(8,128)S(1)}, f32[32,640]{1,0:T(8,128)S(1)}, u32[]{:S(2)}, u32[]{:S(2)}) collective-permute-start(f32[32,640]{1,0:T(8,128)S(1)} %sum_after.6.refs_0_), channel_id=1, source_target_pairs={{0,24},{1,7},{2,26},{3,5},{4,28},{5,3},{6,30},{7,1},{8,16},{9,15},... | collective-permute-start | bytes 245768 | tf_op jit(solution)/shard_map/ppermute | solution.py:437
  37.7 5.9 %collective-permute-start.11 = (f32[32,640]{1,0:T(8,128)S(1)}, f32[32,640]{1,0:T(8,128)S(1)}, u32[]{:S(2)}, u32[]{:S(2)}) collective-permute-start(f32[32,640]{1,0:T(8,128)S(1)} %sum_after.6.refs_0_), channel_id=1, source_target_pairs={{0,16},{1,5},{2,18},{3,7},{4,20},{5,1},{6,22},{7,3},{8,24},{9,13},... | collective-permute-start | bytes 245768 | tf_op jit(solution)/shard_map/ppermute | solution.py:437
  38.6 5.1 %collective-permute-start.10 = (f32[32,640]{1,0:T(8,128)S(1)}, f32[32,640]{1,0:T(8,128)S(1)}, u32[]{:S(2)}, u32[]{:S(2)}) collective-permute-start(f32[32,640]{1,0:T(8,128)S(1)} %sum_after.6.refs_0_), channel_id=1, source_target_pairs={{0,8},{1,3},{2,10},{3,1},{4,12},{5,7},{6,14},{7,5},{8,0},{9,11},{1... | collective-permute-start | bytes 245768 | tf_op jit(solution)/shard_map/ppermute | solution.py:437
  43.7 1.8 %collective-permute-start.14 = (f32[3,32,640]{2,1,0:T(8,128)S(1)}, f32[3,32,640]{2,1,0:T(8,128)S(1)}, u32[]{:S(2)}, u32[]{:S(2)}) collective-permute-start(f32[3,32,640]{2,1,0:T(8,128)S(1)} %stack_after.1), channel_id=1, source_target_pairs={{0,1},{1,0},{2,3},{3,2},{4,5},{5,4},{6,7},{7,6},{8,9},{9,8},{10,11... | collective-permute-start | bytes 737288 | tf_op jit(solution)/shard_map/ppermute | solution.py:445
  47.6 7.3 %collective-permute-start.17 = (f32[32,640]{1,0:T(8,128)S(1)}, f32[32,640]{1,0:T(8,128)S(1)}, u32[]{:S(2)}, u32[]{:S(2)}) collective-permute-start(f32[32,640]{1,0:T(8,128)S(1)} %get-tuple-element.62.refs_3_.refs_0_), channel_id=1, source_target_pairs={{0,24},{1,97},{2,26},{3,99},{4,28},{5,101},{6,30},{7,103},{8,16},{... | collective-permute-start | bytes 245768 | tf_op jit(solution)/shard_map/ppermute | solution.py:437
  49.5 5.9 %collective-permute-start.16 = (f32[32,640]{1,0:T(8,128)S(1)}, f32[32,640]{1,0:T(8,128)S(1)}, u32[]{:S(2)}, u32[]{:S(2)}) collective-permute-start(f32[32,640]{1,0:T(8,128)S(1)} %get-tuple-element.62.refs_3_.refs_0_), channel_id=1, source_target_pairs={{0,16},{1,65},{2,18},{3,67},{4,20},{5,69},{6,22},{7,71},{8,24},{9,... | collective-permute-start | bytes 245768 | tf_op jit(solution)/shard_map/ppermute | solution.py:437
  50.9 4.5 %collective-permute-start.15 = (f32[32,640]{1,0:T(8,128)S(1)}, f32[32,640]{1,0:T(8,128)S(1)}, u32[]{:S(2)}, u32[]{:S(2)}) collective-permute-start(f32[32,640]{1,0:T(8,128)S(1)} %get-tuple-element.62.refs_3_.refs_0_), channel_id=1, source_target_pairs={{0,8},{1,33},{2,10},{3,35},{4,12},{5,37},{6,14},{7,39},{8,0},{9,41... | collective-permute-start | bytes 245768 | tf_op jit(solution)/shard_map/ppermute | solution.py:437
  55.4 7.5 %copy-start = (s32[640,32]{0,1:T(8,128)S(1)}, s32[640,32]{0,1:T(8,128)}, u32[]{:S(2)}) copy-start(s32[640,32]{0,1:T(8,128)} %param.9) | copy-start | bytes 245764
  55.4 7.4 %collective-permute-start.20 = (f32[32,640]{1,0:T(8,128)S(1)}, f32[32,640]{1,0:T(8,128)S(1)}, u32[]{:S(2)}, u32[]{:S(2)}) collective-permute-start(f32[32,640]{1,0:T(8,128)S(1)} %sum_after.7.refs_7_.a_ref), channel_id=1, source_target_pairs={{0,96},{1,25},{2,98},{3,27},{4,100},{5,29},{6,102},{7,31},{8,104},... | collective-permute-start | bytes 245768 | tf_op jit(solution)/shard_map/ppermute | solution.py:437
  57.0 5.9 %collective-permute-start.19 = (f32[32,640]{1,0:T(8,128)S(1)}, f32[32,640]{1,0:T(8,128)S(1)}, u32[]{:S(2)}, u32[]{:S(2)}) collective-permute-start(f32[32,640]{1,0:T(8,128)S(1)} %sum_after.7.refs_7_.a_ref), channel_id=1, source_target_pairs={{0,64},{1,17},{2,66},{3,19},{4,68},{5,21},{6,70},{7,23},{8,72},{9,... | collective-permute-start | bytes 245768 | tf_op jit(solution)/shard_map/ppermute | solution.py:437
  57.7 5.2 %collective-permute-start.18 = (f32[32,640]{1,0:T(8,128)S(1)}, f32[32,640]{1,0:T(8,128)S(1)}, u32[]{:S(2)}, u32[]{:S(2)}) collective-permute-start(f32[32,640]{1,0:T(8,128)S(1)} %sum_after.7.refs_7_.a_ref), channel_id=1, source_target_pairs={{0,32},{1,9},{2,34},{3,11},{4,36},{5,13},{6,38},{7,15},{8,40},{9,1... | collective-permute-start | bytes 245768 | tf_op jit(solution)/shard_map/ppermute | solution.py:437

commit v7 on v6

--- a/solution.py
+++ b/solution.py
@@ -357,12 +357,17 @@
     qf_ref[...] = qt
     q3 = jnp.concatenate([qt, qt, qt, jnp.zeros((RANK, COLS), BF16)], axis=0)
     copies = []
+    half = COLS // 2
     for k, r in enumerate(ORDER):
-        approx = jnp.dot(p3_ref[k], q3, preferred_element_type=F32)
-        stage[k] = (mem[k][...] - approx).astype(BF16)
-        at = pl.ds(rows_of(me_ref[0], r), COLS)
-        copies.append(pltpu.make_async_copy(stage.at[k], out_hbm.at[at, :], sem.at[k]))
-        copies[-1].start()
+        for i in range(2):
+            rows = pl.ds(i * half, half)
+            approx = jnp.dot(p3_ref[k, rows], q3, preferred_element_type=F32)
+            stage[k, rows] = (mem[k][rows] - approx).astype(BF16)
+            at = pl.ds(pl.multiple_of(rows_of(me_ref[0], r) + i * half, half), half)
+            copies.append(
+                pltpu.make_async_copy(stage.at[k, rows], out_hbm.at[at, :], sem.at[2 * k + i])
+            )
+            copies[-1].start()
     for c in copies:
         c.wait()
 
@@ -378,7 +383,7 @@
         out_specs=(VM, ANY),
         scratch_shapes=[
             pltpu.VMEM((NBLK, COLS, COLS), BF16),
-            pltpu.SemaphoreType.DMA((NBLK,)),
+            pltpu.SemaphoreType.DMA((2 * NBLK,)),
         ],
         compiler_params=params(16),
         cost_estimate=cost(2 * D * COLS * 256, 7 * MB),
@@ -480,10 +485,11 @@
 
     other = core(own)
     mine = ring(own, OWNER)
+    memory_of((6,), own)
     held = (held_a, held_e, grad_v)
     early = right([(0, own, None), (1, other, None)], *held)
     early = right([(2 * RING[2], mine[2], None)], *held, early)
-    theirs = core(stack_after(mine, [early[0]]))
+    theirs = core(stack_after(mine, [early[0], memory[6]]))
     mid = right([(2 * r, x, None) for r, x in zip(RING[:2], mine)], *held, early)
     q, gram = right([(2 * r + 1, theirs, i) for i, r in enumerate(RING)], *held, mid, True)
 
@@ -492,7 +498,7 @@
     memory_of((3,), q)
     q = sum_after([q, *from_ring], [inv, memory[3]])
     from_ring = ring(q, DP_SECOND)
-    memory_of((5, 6, 7), q)
+    memory_of((5, 7), q)
     q_factor, new_error = update(me, [q, *from_ring], inv, dither.T, p3, [memory[r] for r in ORDER])
     return (q_factor.T, new_error)
 

time: 67.4 us -> 67.4 us (level)
    pallas_call x5 -> x6, Pallas kernels: 11.2 us -> 11.5 us  [memory_blocks(): pl.pallas_call(body, out_shape=shapes, in_specs=in_specs, out_specs=[VM]...]
  transfers between devices with their start and end apart: 21 -> 21, of which waited for: 7 -> 6; matrix products, arithmetic and copies ran while one was open for 0% -> 0% of each run, Pallas kernels for 32% -> 32%
where the time goes in v7:
time: 67.4 us; the launch traced here: 67.1 us
  Pallas kernels  32.1 us (48%)
  starting transfers between devices  26.4 us (39%)
  waiting for transfers between devices  7.56 us (11%)
  between operations  1.02 us (2%)
    ppermute x18, starting transfers between devices, exchange(): return lax.ppermute(v, ('dp', 'tensor'), pairs)  25.9 us
    pallas_call x6, Pallas kernels, memory_blocks(): pl.pallas_call(body, out_shape=shapes, in_specs=in_specs, out_specs=[VM]...  11.5 us
    ppermute x18, waiting for transfers between devices, exchange(): return lax.ppermute(v, ('dp', 'tensor'), pairs)  7.36 us
    pallas_call x4, Pallas kernels, right(): pl.pallas_call(body, out_shape=shapes, in_specs=[VM] * len(args), out_spe...  5.42 us
    pallas_call x1, Pallas kernels, update(): pl.pallas_call(update_body, out_shape=(jax.ShapeDtypeStruct((RANK, COLS),...  3.97 us
    pallas_call x1, Pallas kernels, left_away(): pl.pallas_call(body, out_shape=[jax.ShapeDtypeStruct((RANK, HALF * COLS +...  3.53 us
    pallas_call x1, Pallas kernels, left_kept(): pl.pallas_call(body, out_shape=[jax.ShapeDtypeStruct((3, RANK, COLS), F32...  2.94 us
    pallas_call x1, Pallas kernels, left_own(): pl.pallas_call(body, out_shape=[jax.ShapeDtypeStruct((RANK, COLS), F32),...  1.98 us
  transfers between devices with their start and end apart: 21, of which 6 were waited for; matrix products, arithmetic and copies ran while one was open for 0% of the time, Pallas kernels for 32%

profile of v7, /device:TPU:0, one launch (start us, length us, event | category | flops | bytes accessed | tf_op | source)
XLA Modules:
  0.0 67.1 jit_solution(11222756243360953561)
XLA Ops:
  0.6 3.5 %left_away.1 = (f32[32,3584]{1,0:T(8,128)S(1)}, bf16[4,640,640]{2,1,0:T(8,128)(2,1)S(1)}, bf16[1024,640]{1,0:T(8,128)(2,1)S(1)}, bf16[32,640]{1,0:T(8,128)(2,1)S(1)}) custom-call(s32[1]{0:T(128)} %bitcast.me_ref.refs_4_.refs_6_, bf16[5120,640]{1,0:T(8,128)(2,1)} %err_hbm.5, bf16[1024,640]{1,0:T(8,128)(2,1)} %grad_hbm.1, s32[32,640]{1,0:T(8,128)} %bitcast.11), custom_call_target="tpu_custom_call" | custom-call | flops 838860800 | bytes 5242880 | tf_op jit(solution)/shard_map/left_away/pallas_call | solution.py:111
  4.3 2.9 %left_kept.1 = (f32[3,32,640]{2,1,0:T(8,128)S(1)}, bf16[3,1024,640]{2,1,0:T(8,128)(2,1)S(1)}, bf16[3,640,640]{2,1,0:T(8,128)(2,1)S(1)}) custom-call(s32[1]{0:T(128)} %bitcast.me_ref.refs_4_.refs_6_, bf16[1024,5120]{1,0:T(8,128)(2,1)} %refs_7_.1, bf16[5120,640]{1,0:T(8,128)(2,1)} %err_hbm.5, bf16[32,640]{1,0:T(8,128)(2,1)S(1)} %get-tuple-element.36.qt_ref), custom_call_target="tpu_custom_call" | custom-call | flops 629145600 | bytes 6291456 | tf_op jit(solution)/shard_map/left_kept/pallas_call | solution.py:147
  7.2 0.8 %left_sum.1 = (f32[3,32,640]{2,1,0:T(8,128)S(1)}, bf16[96,1024]{1,0:T(8,128)(2,1)S(1)}) custom-call(bf16[3,1024,640]{2,1,0:T(8,128)(2,1)S(1)} %get-tuple-element.37.acts_v.refs_0_.refs_1_.refs_4_, f32[3,32,640]{2,1,0:T(8,128)S(1)} %get-tuple-element.38.kept, f32[32,3584]{1,0:T(8,128)S(1)} %get-tuple-element.39.away, f32[32,3584]{1,0:T(8,128)S(1)} %collective-permute-done.came), custom_call_target="tpu_custom_call" | custom-call | flops 1006632960 | tf_op jit(solution)/shard_map/left_sum/pallas_call | solution.py:172
  8.1 2.9 %collective-permute-start.3 = (f32[32,640]{1,0:T(8,128)S(1)}, f32[32,640]{1,0:T(8,128)S(1)}, u32[]{:S(2)}, u32[]{:S(2)}) collective-permute-start(f32[32,640]{1,0:T(8,128)S(1)} %get-tuple-element.70), channel_id=1, source_target_pairs={{0,24},{1,7},{2,26},{3,5},{4,28},{5,3},{6,30},{7,1},{8,16},{9,15},... | collective-permute-start | bytes 245768 | tf_op jit(solution)/shard_map/ppermute | solution.py:442
  11.0 0.8 %collective-permute-start.2 = (f32[32,640]{1,0:T(8,128)S(1)}, f32[32,640]{1,0:T(8,128)S(1)}, u32[]{:S(2)}, u32[]{:S(2)}) collective-permute-start(f32[32,640]{1,0:T(8,128)S(1)} %get-tuple-element.71), channel_id=1, source_target_pairs={{0,16},{1,5},{2,18},{3,7},{4,20},{5,1},{6,22},{7,3},{8,24},{9,13},... | collective-permute-start | bytes 245768 | tf_op jit(solution)/shard_map/ppermute | solution.py:442
  12.3 2.0 %left_own.1 = (f32[32,640]{1,0:T(8,128)S(1)}, bf16[1,1024,640]{2,1,0:T(8,128)(2,1)S(1)}, bf16[1,640,640]{2,1,0:T(8,128)(2,1)S(1)}) custom-call(s32[1]{0:T(128)} %bitcast.me_ref.refs_4_.refs_6_, bf16[1024,5120]{1,0:T(8,128)(2,1)} %refs_7_.1, bf16[5120,640]{1,0:T(8,128)(2,1)} %err_hbm.5, bf16[32,640]{1,0:T(8,128)(2,1)S(1)} %get-tuple-element.36.qt_ref, ...), custom_call_target="tpu_custom_call" | custom-call | flops 545259520 | bytes 2097152 | tf_op jit(solution)/shard_map/left_own/pallas_call | solution.py:199
  14.2 1.2 %memory_blocks.6.refs_4_.rest_2_ = f32[640,640]{1,0:T(8,128)S(1)} custom-call(bf16[3,1024,640]{2,1,0:T(8,128)(2,1)S(1)} %get-tuple-element.37.acts_v.refs_0_.refs_1_.refs_4_, bf16[3,640,640]{2,1,0:T(8,128)(2,1)S(1)} %get-tuple-element.43.refs_1_.refs_2_.refs_5_, bf16[1024,640]{1,0:T(8,128)(2,1)S(1)} %get-tuple-element.44.refs_2_.refs_4_.refs_6_.refs_3_.refs_9_, ...), custom_call_target="tpu_custom_call" | custom-call | flops 838860800 | tf_op jit(solution)/shard_map/memory_blocks/pallas_call | solution.py:244
  15.5 1.5 %collective-permute-done.2.refs_2_ = f32[32,640]{1,0:T(8,128)S(1)} collective-permute-done((f32[32,640]{1,0:T(8,128)S(1)}, f32[32,640]{1,0:T(8,128)S(1)}, u32[]{:S(2)}, u32[]{:S(2)}) %collective-permute-start.2) | collective-permute-done | bytes 81952 | tf_op jit(solution)/shard_map/ppermute | solution.py:442
  17.0 3.1 %collective-permute-start.6 = (f32[32,640]{1,0:T(8,128)S(1)}, f32[32,640]{1,0:T(8,128)S(1)}, u32[]{:S(2)}, u32[]{:S(2)}) collective-permute-start(f32[32,640]{1,0:T(8,128)S(1)} %sum_after.4.refs_3_.refs_0_), channel_id=1, source_target_pairs={{0,96},{1,25},{2,98},{3,27},{4,100},{5,29},{6,102},{7,31},{8,104},... | collective-permute-start | bytes 245768 | tf_op jit(solution)/shard_map/ppermute | solution.py:442
  21.2 2.7 %memory_blocks.7 = (f32[640,640]{1,0:T(8,128)S(1)}, bf16[3,1024,640]{2,1,0:T(8,128)(2,1)S(1)}) custom-call(bf16[1,1024,640]{2,1,0:T(8,128)(2,1)S(1)} %get-tuple-element.45.refs_0_.refs_1_, bf16[1,640,640]{2,1,0:T(8,128)(2,1)S(1)} %get-tuple-element.46.refs_1_.refs_2_, bf16[1024,640]{1,0:T(8,128)(2,1)S(1)} %get-tuple-element.44.refs_2_.refs_4_.refs_6_.refs_3_.refs_9_, ...), custom_call_target="tpu_custom_call" | custom-call | flops 838860800 | tf_op jit(solution)/shard_map/memory_blocks/pallas_call | solution.py:244
  23.8 2.2 %collective-permute-done.5.refs_2_ = f32[32,640]{1,0:T(8,128)S(1)} collective-permute-done((f32[32,640]{1,0:T(8,128)S(1)}, f32[32,640]{1,0:T(8,128)S(1)}, u32[]{:S(2)}, u32[]{:S(2)}) %collective-permute-start.5) | collective-permute-done | bytes 81952 | tf_op jit(solution)/shard_map/ppermute | solution.py:442
  26.1 4.1 %collective-permute-start.9 = (f32[32,640]{1,0:T(8,128)S(1)}, f32[32,640]{1,0:T(8,128)S(1)}, u32[]{:S(2)}, u32[]{:S(2)}) collective-permute-start(f32[32,640]{1,0:T(8,128)S(1)} %sum_after.5.refs_5_.refs_0_), channel_id=1, source_target_pairs={{0,6},{1,97},{2,4},{3,99},{4,2},{5,101},{6,0},{7,103},{8,14},{9,10... | collective-permute-start | bytes 245768 | tf_op jit(solution)/shard_map/ppermute | solution.py:442
  30.2 0.9 %collective-permute-start.7 = (f32[32,640]{1,0:T(8,128)S(1)}, f32[32,640]{1,0:T(8,128)S(1)}, u32[]{:S(2)}, u32[]{:S(2)}) collective-permute-start(f32[32,640]{1,0:T(8,128)S(1)} %sum_after.5.refs_5_.refs_0_), channel_id=1, source_target_pairs={{0,2},{1,33},{2,0},{3,35},{4,6},{5,37},{6,4},{7,39},{8,10},{9,41},... | collective-permute-start | bytes 245768 | tf_op jit(solution)/shard_map/ppermute | solution.py:442
  31.1 2.9 %memory_blocks.8 = (f32[640,640]{1,0:T(8,128)S(1)}, f32[640,640]{1,0:T(8,128)S(1)}, bf16[1,1024,640]{2,1,0:T(8,128)(2,1)S(1)}) custom-call(bf16[3,1024,640]{2,1,0:T(8,128)(2,1)S(1)} %get-tuple-element.37.acts_v.refs_0_.refs_1_.refs_4_, bf16[3,640,640]{2,1,0:T(8,128)(2,1)S(1)} %get-tuple-element.43.refs_1_.refs_2_.refs_5_, ...), custom_call_target="tpu_custom_call" | custom-call | flops 1677721600 | tf_op jit(solution)/shard_map/memory_blocks/pallas_call | solution.py:244
  34.0 2.1 %collective-permute-done.8.refs_2_ = f32[32,640]{1,0:T(8,128)S(1)} collective-permute-done((f32[32,640]{1,0:T(8,128)S(1)}, f32[32,640]{1,0:T(8,128)S(1)}, u32[]{:S(2)}, u32[]{:S(2)}) %collective-permute-start.8) | collective-permute-done | bytes 81952 | tf_op jit(solution)/shard_map/ppermute | solution.py:442
  36.2 1.5 %collective-permute-start.12 = (f32[32,640]{1,0:T(8,128)S(1)}, f32[32,640]{1,0:T(8,128)S(1)}, u32[]{:S(2)}, u32[]{:S(2)}) collective-permute-start(f32[32,640]{1,0:T(8,128)S(1)} %sum_after.6.refs_0_.refs_3_), channel_id=1, source_target_pairs={{0,24},{1,7},{2,26},{3,5},{4,28},{5,3},{6,30},{7,1},{8,16},{9,15},... | collective-permute-start | bytes 245768 | tf_op jit(solution)/shard_map/ppermute | solution.py:442
  37.8 0.9 %collective-permute-start.11 = (f32[32,640]{1,0:T(8,128)S(1)}, f32[32,640]{1,0:T(8,128)S(1)}, u32[]{:S(2)}, u32[]{:S(2)}) collective-permute-start(f32[32,640]{1,0:T(8,128)S(1)} %sum_after.6.refs_0_.refs_3_), channel_id=1, source_target_pairs={{0,16},{1,5},{2,18},{3,7},{4,20},{5,1},{6,22},{7,3},{8,24},{9,13},... | collective-permute-start | bytes 245768 | tf_op jit(solution)/shard_map/ppermute | solution.py:442
  38.6 1.8 %collective-permute-start.10 = (f32[32,640]{1,0:T(8,128)S(1)}, f32[32,640]{1,0:T(8,128)S(1)}, u32[]{:S(2)}, u32[]{:S(2)}) collective-permute-start(f32[32,640]{1,0:T(8,128)S(1)} %sum_after.6.refs_0_.refs_3_), channel_id=1, source_target_pairs={{0,8},{1,3},{2,10},{3,1},{4,12},{5,7},{6,14},{7,5},{8,0},{9,11},{1... | collective-permute-start | bytes 245768 | tf_op jit(solution)/shard_map/ppermute | solution.py:442
  40.4 1.2 %memory_blocks.9.refs_4_.rest_4_ = f32[640,640]{1,0:T(8,128)S(1)} custom-call(bf16[3,1024,640]{2,1,0:T(8,128)(2,1)S(1)} %get-tuple-element.37.acts_v.refs_0_.refs_1_.refs_4_, bf16[3,640,640]{2,1,0:T(8,128)(2,1)S(1)} %get-tuple-element.43.refs_1_.refs_2_.refs_5_, bf16[1024,640]{1,0:T(8,128)(2,1)S(1)} %get-tuple-element.44.refs_2_.refs_4_.refs_6_.refs_3_.refs_9_, ...), custom_call_target="tpu_custom_call" | custom-call | flops 838860800 | tf_op jit(solution)/shard_map/memory_blocks/pallas_call | solution.py:244
  41.6 1.3 %right_part.3 = (f32[32,1024]{1,0:T(8,128)S(1)}, f32[32,640]{1,0:T(8,128)S(1)}, f32[96,96]{1,0:T(8,128)S(1)}) custom-call(f32[32,640]{1,0:T(8,128)S(1)} %sum_after.6.refs_0_.refs_3_, bf16[1,1024,640]{2,1,0:T(8,128)(2,1)S(1)} %get-tuple-element.45.refs_0_.refs_1_, bf16[1,640,640]{2,1,0:T(8,128)(2,1)S(1)} %get-tuple-element.46.refs_1_.refs_2_, ...), custom_call_target="tpu_custom_call" | custom-call | flops 1090519040 | tf_op jit(solution)/shard_map/right_part/pallas_call | solution.py:289
  44.0 1.3 %right_part.5 = (f32[32,1024]{1,0:T(8,128)S(1)}, f32[32,640]{1,0:T(8,128)S(1)}, f32[96,96]{1,0:T(8,128)S(1)}) custom-call(f32[32,640]{1,0:T(8,128)S(1)} %collective-permute-done.10.refs_0_.refs_2_, bf16[3,1024,640]{2,1,0:T(8,128)(2,1)S(1)} %get-tuple-element.37.acts_v.refs_0_.refs_1_.refs_4_, ...), custom_call_target="tpu_custom_call" | custom-call | flops 1090519040 | tf_op jit(solution)/shard_map/right_part/pallas_call | solution.py:289
  45.5 2.1 %right_last.1 = (f32[32,640]{1,0:T(8,128)S(1)}, f32[96,96]{1,0:T(8,128)S(1)}) custom-call(f32[3,32,640]{2,1,0:T(8,128)S(1)} %collective-permute-done.14.refs_0_.refs_3_.refs_6_.refs_5_, bf16[3,1024,640]{2,1,0:T(8,128)(2,1)S(1)} %get-tuple-element.48.refs_2_.refs_4_.refs_1_.refs_0_, ...), custom_call_target="tpu_custom_call" | custom-call | flops 1635778560 | tf_op jit(solution)/shard_map/right_last/pallas_call | solution.py:289
  47.6 1.9 %collective-permute-start.17 = (f32[32,640]{1,0:T(8,128)S(1)}, f32[32,640]{1,0:T(8,128)S(1)}, u32[]{:S(2)}, u32[]{:S(2)}) collective-permute-start(f32[32,640]{1,0:T(8,128)S(1)} %get-tuple-element.61.refs_3_.refs_0_), channel_id=1, source_target_pairs={{0,24},{1,97},{2,26},{3,99},{4,28},{5,101},{6,30},{7,103},{8,16},{... | collective-permute-start | bytes 245768 | tf_op jit(solution)/shard_map/ppermute | solution.py:442
  49.5 1.4 %collective-permute-start.16 = (f32[32,640]{1,0:T(8,128)S(1)}, f32[32,640]{1,0:T(8,128)S(1)}, u32[]{:S(2)}, u32[]{:S(2)}) collective-permute-start(f32[32,640]{1,0:T(8,128)S(1)} %get-tuple-element.61.refs_3_.refs_0_), channel_id=1, source_target_pairs={{0,16},{1,65},{2,18},{3,67},{4,20},{5,69},{6,22},{7,71},{8,24},{9,... | collective-permute-start | bytes 245768 | tf_op jit(solution)/shard_map/ppermute | solution.py:442
  50.9 0.9 %collective-permute-start.15 = (f32[32,640]{1,0:T(8,128)S(1)}, f32[32,640]{1,0:T(8,128)S(1)}, u32[]{:S(2)}, u32[]{:S(2)}) collective-permute-start(f32[32,640]{1,0:T(8,128)S(1)} %get-tuple-element.61.refs_3_.refs_0_), channel_id=1, source_target_pairs={{0,8},{1,33},{2,10},{3,35},{4,12},{5,37},{6,14},{7,39},{8,0},{9,41... | collective-permute-start | bytes 245768 | tf_op jit(solution)/shard_map/ppermute | solution.py:442
  51.8 1.9 %orthonormal.1 = (bf16[8,640,128]{2,1,0:T(8,128)(2,1)S(1)}, f32[32,32]{1,0:T(8,128)S(1)}) custom-call(f32[96,96]{1,0:T(8,128)S(1)} %get-tuple-element.62.gram_ref, f32[32,640]{1,0:T(8,128)S(1)} %sum_after.6.refs_0_.refs_3_, f32[32,640]{1,0:T(8,128)S(1)} %collective-permute-done.13.refs_3_.refs_1_, f32[32,640]{1,0:T(8,128)S(1)} %collective-permute-done.10.refs_0_.refs_2_, ...), custom_call_target="tpu_custom_call" | custom-call | flops 2147483648 | tf_op jit(solution)/shard_map/orthonormal/pallas_call | solution.py:336
  53.7 1.2 %memory_blocks.10.refs_5_.rest_5_ = f32[640,640]{1,0:T(8,128)S(1)} custom-call(bf16[3,1024,640]{2,1,0:T(8,128)(2,1)S(1)} %get-tuple-element.48.refs_2_.refs_4_.refs_1_.refs_0_, bf16[4,640,640]{2,1,0:T(8,128)(2,1)S(1)} %get-tuple-element.49.refs_3_.refs_5_.refs_2_.refs_8_.refs_1_, ...), custom_call_target="tpu_custom_call" | custom-call | flops 838860800 | tf_op jit(solution)/shard_map/memory_blocks/pallas_call | solution.py:244
  55.5 1.5 %collective-permute-start.20 = (f32[32,640]{1,0:T(8,128)S(1)}, f32[32,640]{1,0:T(8,128)S(1)}, u32[]{:S(2)}, u32[]{:S(2)}) collective-permute-start(f32[32,640]{1,0:T(8,128)S(1)} %sum_after.7.refs_5_.a_ref), channel_id=1, source_target_pairs={{0,96},{1,25},{2,98},{3,27},{4,100},{5,29},{6,102},{7,31},{8,104},... | collective-permute-start | bytes 245768 | tf_op jit(solution)/shard_map/ppermute | solution.py:442
  57.8 1.9 %collective-permute-start.18 = (f32[32,640]{1,0:T(8,128)S(1)}, f32[32,640]{1,0:T(8,128)S(1)}, u32[]{:S(2)}, u32[]{:S(2)}) collective-permute-start(f32[32,640]{1,0:T(8,128)S(1)} %sum_after.7.refs_5_.a_ref), channel_id=1, source_target_pairs={{0,32},{1,9},{2,34},{3,11},{4,36},{5,13},{6,38},{7,15},{8,40},{9,1... | collective-permute-start | bytes 245768 | tf_op jit(solution)/shard_map/ppermute | solution.py:442
  59.7 2.2 %memory_blocks.11 = (f32[640,640]{1,0:T(8,128)S(1)}, f32[640,640]{1,0:T(8,128)S(1)}) custom-call(bf16[3,1024,640]{2,1,0:T(8,128)(2,1)S(1)} %get-tuple-element.48.refs_2_.refs_4_.refs_1_.refs_0_, bf16[4,640,640]{2,1,0:T(8,128)(2,1)S(1)} %get-tuple-element.49.refs_3_.refs_5_.refs_2_.refs_8_.refs_1_, ...), custom_call_target="tpu_custom_call" | custom-call | flops 1677721600 | tf_op jit(solution)/shard_map/memory_blocks/pallas_call | solution.py:244
  61.9 1.0 %collective-permute-done.19.c_ref = f32[32,640]{1,0:T(8,128)S(1)} collective-permute-done((f32[32,640]{1,0:T(8,128)S(1)}, f32[32,640]{1,0:T(8,128)S(1)}, u32[]{:S(2)}, u32[]{:S(2)}) %collective-permute-start.19) | collective-permute-done | bytes 81952 | tf_op jit(solution)/shard_map/ppermute | solution.py:442
  63.0 4.0 %update.1 = (bf16[32,640]{1,0:T(8,128)(2,1)}, bf16[5120,640]{1,0:T(8,128)(2,1)}) custom-call(s32[1]{0:T(128)} %bitcast.me_ref.refs_4_.refs_6_, f32[32,640]{1,0:T(8,128)S(1)} %sum_after.7.refs_5_.a_ref, f32[32,640]{1,0:T(8,128)S(1)} %collective-permute-done.18.b_ref, f32[32,640]{1,0:T(8,128)S(1)} %collective-permute-done.19.c_ref, ...), custom_call_target="tpu_custom_call" | custom-call | flops 1677721600 | bytes 7340032 | tf_op jit(solution)/shard_map/update/pallas_call | solution.py:376
  (34 shorter events, 4.4 us)
Async XLA Ops:
  4.2 3.0 %collective-permute-start = (f32[32,3584]{1,0:T(8,128)S(1)}, f32[32,3584]{1,0:T(8,128)S(1)}, u32[]{:S(2)}, u32[]{:S(2)}) collective-permute-start(f32[32,3584]{1,0:T(8,128)S(1)} %get-tuple-element.39.away), channel_id=1, source_target_pairs={{0,1},{1,0},{2,3},{3,2},{4,5},{5,4},{6,7},{7,6},{8,9},{9,8},{10,11... | collective-permute-start | bytes 1376264 | tf_op jit(solution)/shard_map/ppermute | solution.py:450
  8.1 7.4 %collective-permute-start.3 = (f32[32,640]{1,0:T(8,128)S(1)}, f32[32,640]{1,0:T(8,128)S(1)}, u32[]{:S(2)}, u32[]{:S(2)}) collective-permute-start(f32[32,640]{1,0:T(8,128)S(1)} %get-tuple-element.70), channel_id=1, source_target_pairs={{0,24},{1,7},{2,26},{3,5},{4,28},{5,3},{6,30},{7,1},{8,16},{9,15},... | collective-permute-start | bytes 245768 | tf_op jit(solution)/shard_map/ppermute | solution.py:442
  11.0 5.9 %collective-permute-start.2 = (f32[32,640]{1,0:T(8,128)S(1)}, f32[32,640]{1,0:T(8,128)S(1)}, u32[]{:S(2)}, u32[]{:S(2)}) collective-permute-start(f32[32,640]{1,0:T(8,128)S(1)} %get-tuple-element.71), channel_id=1, source_target_pairs={{0,16},{1,5},{2,18},{3,7},{4,20},{5,1},{6,22},{7,3},{8,24},{9,13},... | collective-permute-start | bytes 245768 | tf_op jit(solution)/shard_map/ppermute | solution.py:442
  11.8 5.1 %collective-permute-start.1 = (f32[32,640]{1,0:T(8,128)S(1)}, f32[32,640]{1,0:T(8,128)S(1)}, u32[]{:S(2)}, u32[]{:S(2)}) collective-permute-start(f32[32,640]{1,0:T(8,128)S(1)} %get-tuple-element.72), channel_id=1, source_target_pairs={{0,8},{1,3},{2,10},{3,1},{4,12},{5,7},{6,14},{7,5},{8,0},{9,11},{1... | collective-permute-start | bytes 245768 | tf_op jit(solution)/shard_map/ppermute | solution.py:442
  17.0 6.8 %collective-permute-start.6 = (f32[32,640]{1,0:T(8,128)S(1)}, f32[32,640]{1,0:T(8,128)S(1)}, u32[]{:S(2)}, u32[]{:S(2)}) collective-permute-start(f32[32,640]{1,0:T(8,128)S(1)} %sum_after.4.refs_3_.refs_0_), channel_id=1, source_target_pairs={{0,96},{1,25},{2,98},{3,27},{4,100},{5,29},{6,102},{7,31},{8,104},... | collective-permute-start | bytes 245768 | tf_op jit(solution)/shard_map/ppermute | solution.py:442
  20.1 5.9 %collective-permute-start.5 = (f32[32,640]{1,0:T(8,128)S(1)}, f32[32,640]{1,0:T(8,128)S(1)}, u32[]{:S(2)}, u32[]{:S(2)}) collective-permute-start(f32[32,640]{1,0:T(8,128)S(1)} %sum_after.4.refs_3_.refs_0_), channel_id=1, source_target_pairs={{0,64},{1,17},{2,66},{3,19},{4,68},{5,21},{6,70},{7,23},{8,72},{9,... | collective-permute-start | bytes 245768 | tf_op jit(solution)/shard_map/ppermute | solution.py:442
  20.7 5.3 %collective-permute-start.4 = (f32[32,640]{1,0:T(8,128)S(1)}, f32[32,640]{1,0:T(8,128)S(1)}, u32[]{:S(2)}, u32[]{:S(2)}) collective-permute-start(f32[32,640]{1,0:T(8,128)S(1)} %sum_after.4.refs_3_.refs_0_), channel_id=1, source_target_pairs={{0,32},{1,9},{2,34},{3,11},{4,36},{5,13},{6,38},{7,15},{8,40},{9,1... | collective-permute-start | bytes 245768 | tf_op jit(solution)/shard_map/ppermute | solution.py:442
  26.1 8.0 %collective-permute-start.9 = (f32[32,640]{1,0:T(8,128)S(1)}, f32[32,640]{1,0:T(8,128)S(1)}, u32[]{:S(2)}, u32[]{:S(2)}) collective-permute-start(f32[32,640]{1,0:T(8,128)S(1)} %sum_after.5.refs_5_.refs_0_), channel_id=1, source_target_pairs={{0,6},{1,97},{2,4},{3,99},{4,2},{5,101},{6,0},{7,103},{8,14},{9,10... | collective-permute-start | bytes 245768 | tf_op jit(solution)/shard_map/ppermute | solution.py:442
  30.2 5.9 %collective-permute-start.8 = (f32[32,640]{1,0:T(8,128)S(1)}, f32[32,640]{1,0:T(8,128)S(1)}, u32[]{:S(2)}, u32[]{:S(2)}) collective-permute-start(f32[32,640]{1,0:T(8,128)S(1)} %sum_after.5.refs_5_.refs_0_), channel_id=1, source_target_pairs={{0,4},{1,65},{2,6},{3,67},{4,0},{5,69},{6,2},{7,71},{8,12},{9,73},... | collective-permute-start | bytes 245768 | tf_op jit(solution)/shard_map/ppermute | solution.py:442
  30.2 5.9 %collective-permute-start.7 = (f32[32,640]{1,0:T(8,128)S(1)}, f32[32,640]{1,0:T(8,128)S(1)}, u32[]{:S(2)}, u32[]{:S(2)}) collective-permute-start(f32[32,640]{1,0:T(8,128)S(1)} %sum_after.5.refs_5_.refs_0_), channel_id=1, source_target_pairs={{0,2},{1,33},{2,0},{3,35},{4,6},{5,37},{6,4},{7,39},{8,10},{9,41},... | collective-permute-start | bytes 245768 | tf_op jit(solution)/shard_map/ppermute | solution.py:442
  36.1 5.5 %collective-permute-start.13 = (f32[32,640]{1,0:T(8,128)S(1)}, f32[32,640]{1,0:T(8,128)S(1)}, u32[]{:S(2)}, u32[]{:S(2)}) collective-permute-start(f32[32,640]{1,0:T(8,128)S(1)} %sum_after.6.refs_0_.refs_3_), channel_id=1, source_target_pairs={{0,1},{1,0},{2,3},{3,2},{4,5},{5,4},{6,7},{7,6},{8,9},{9,8},{10,11... | collective-permute-start | bytes 245768 | tf_op jit(solution)/shard_map/ppermute | solution.py:450
  36.2 6.7 %collective-permute-start.12 = (f32[32,640]{1,0:T(8,128)S(1)}, f32[32,640]{1,0:T(8,128)S(1)}, u32[]{:S(2)}, u32[]{:S(2)}) collective-permute-start(f32[32,640]{1,0:T(8,128)S(1)} %sum_after.6.refs_0_.refs_3_), channel_id=1, source_target_pairs={{0,24},{1,7},{2,26},{3,5},{4,28},{5,3},{6,30},{7,1},{8,16},{9,15},... | collective-permute-start | bytes 245768 | tf_op jit(solution)/shard_map/ppermute | solution.py:442
  37.8 5.9 %collective-permute-start.11 = (f32[32,640]{1,0:T(8,128)S(1)}, f32[32,640]{1,0:T(8,128)S(1)}, u32[]{:S(2)}, u32[]{:S(2)}) collective-permute-start(f32[32,640]{1,0:T(8,128)S(1)} %sum_after.6.refs_0_.refs_3_), channel_id=1, source_target_pairs={{0,16},{1,5},{2,18},{3,7},{4,20},{5,1},{6,22},{7,3},{8,24},{9,13},... | collective-permute-start | bytes 245768 | tf_op jit(solution)/shard_map/ppermute | solution.py:442
  38.6 5.1 %collective-permute-start.10 = (f32[32,640]{1,0:T(8,128)S(1)}, f32[32,640]{1,0:T(8,128)S(1)}, u32[]{:S(2)}, u32[]{:S(2)}) collective-permute-start(f32[32,640]{1,0:T(8,128)S(1)} %sum_after.6.refs_0_.refs_3_), channel_id=1, source_target_pairs={{0,8},{1,3},{2,10},{3,1},{4,12},{5,7},{6,14},{7,5},{8,0},{9,11},{1... | collective-permute-start | bytes 245768 | tf_op jit(solution)/shard_map/ppermute | solution.py:442
  43.7 1.8 %collective-permute-start.14 = (f32[3,32,640]{2,1,0:T(8,128)S(1)}, f32[3,32,640]{2,1,0:T(8,128)S(1)}, u32[]{:S(2)}, u32[]{:S(2)}) collective-permute-start(f32[3,32,640]{2,1,0:T(8,128)S(1)} %stack_after.1), channel_id=1, source_target_pairs={{0,1},{1,0},{2,3},{3,2},{4,5},{5,4},{6,7},{7,6},{8,9},{9,8},{10,11... | collective-permute-start | bytes 737288 | tf_op jit(solution)/shard_map/ppermute | solution.py:450
  47.6 7.3 %collective-permute-start.17 = (f32[32,640]{1,0:T(8,128)S(1)}, f32[32,640]{1,0:T(8,128)S(1)}, u32[]{:S(2)}, u32[]{:S(2)}) collective-permute-start(f32[32,640]{1,0:T(8,128)S(1)} %get-tuple-element.61.refs_3_.refs_0_), channel_id=1, source_target_pairs={{0,24},{1,97},{2,26},{3,99},{4,28},{5,101},{6,30},{7,103},{8,16},{... | collective-permute-start | bytes 245768 | tf_op jit(solution)/shard_map/ppermute | solution.py:442
  49.5 5.9 %collective-permute-start.16 = (f32[32,640]{1,0:T(8,128)S(1)}, f32[32,640]{1,0:T(8,128)S(1)}, u32[]{:S(2)}, u32[]{:S(2)}) collective-permute-start(f32[32,640]{1,0:T(8,128)S(1)} %get-tuple-element.61.refs_3_.refs_0_), channel_id=1, source_target_pairs={{0,16},{1,65},{2,18},{3,67},{4,20},{5,69},{6,22},{7,71},{8,24},{9,... | collective-permute-start | bytes 245768 | tf_op jit(solution)/shard_map/ppermute | solution.py:442
  50.9 4.5 %collective-permute-start.15 = (f32[32,640]{1,0:T(8,128)S(1)}, f32[32,640]{1,0:T(8,128)S(1)}, u32[]{:S(2)}, u32[]{:S(2)}) collective-permute-start(f32[32,640]{1,0:T(8,128)S(1)} %get-tuple-element.61.refs_3_.refs_0_), channel_id=1, source_target_pairs={{0,8},{1,33},{2,10},{3,35},{4,12},{5,37},{6,14},{7,39},{8,0},{9,41... | collective-permute-start | bytes 245768 | tf_op jit(solution)/shard_map/ppermute | solution.py:442
  55.5 7.5 %copy-start = (s32[640,32]{0,1:T(8,128)S(1)}, s32[640,32]{0,1:T(8,128)}, u32[]{:S(2)}) copy-start(s32[640,32]{0,1:T(8,128)} %param.9) | copy-start | bytes 245764
  55.5 6.4 %collective-permute-start.20 = (f32[32,640]{1,0:T(8,128)S(1)}, f32[32,640]{1,0:T(8,128)S(1)}, u32[]{:S(2)}, u32[]{:S(2)}) collective-permute-start(f32[32,640]{1,0:T(8,128)S(1)} %sum_after.7.refs_5_.a_ref), channel_id=1, source_target_pairs={{0,96},{1,25},{2,98},{3,27},{4,100},{5,29},{6,102},{7,31},{8,104},... | collective-permute-start | bytes 245768 | tf_op jit(solution)/shard_map/ppermute | solution.py:442
  57.0 5.9 %collective-permute-start.19 = (f32[32,640]{1,0:T(8,128)S(1)}, f32[32,640]{1,0:T(8,128)S(1)}, u32[]{:S(2)}, u32[]{:S(2)}) collective-permute-start(f32[32,640]{1,0:T(8,128)S(1)} %sum_after.7.refs_5_.a_ref), channel_id=1, source_target_pairs={{0,64},{1,17},{2,66},{3,19},{4,68},{5,21},{6,70},{7,23},{8,72},{9,... | collective-permute-start | bytes 245768 | tf_op jit(solution)/shard_map/ppermute | solution.py:442
  57.8 5.2 %collective-permute-start.18 = (f32[32,640]{1,0:T(8,128)S(1)}, f32[32,640]{1,0:T(8,128)S(1)}, u32[]{:S(2)}, u32[]{:S(2)}) collective-permute-start(f32[32,640]{1,0:T(8,128)S(1)} %sum_after.7.refs_5_.a_ref), channel_id=1, source_target_pairs={{0,32},{1,9},{2,34},{3,11},{4,36},{5,13},{6,38},{7,15},{8,40},{9,1... | collective-permute-start | bytes 245768 | tf_op jit(solution)/shard_map/ppermute | solution.py:442

commit v8 on v7

--- a/solution.py
+++ b/solution.py
@@ -297,8 +297,9 @@
     )(*args)
 
 
-def orthonormal_body(gram_ref, *refs):
-    blocks, theirs, p3_ref, inv_ref = refs[: HALF + 1], *refs[HALF + 1 :]
+def orthonormal_body(gram_ref, dither_ref, *refs):
+    blocks, theirs, p3_ref, inv_ref, scale_ref = refs[: HALF + 1], *refs[HALF + 1 :]
+    scale_ref[...] = 1.0 + (dither_ref[...].astype(F32) / 65536.0 - 0.5) / 4.0
     wide = fold3(gram_ref[...])
     gram = wide[:, :RANK] + wide[:, RANK : 2 * RANK] + wide[:, 2 * RANK :]
     rows = lax.broadcasted_iota(jnp.int32, (RANK, RANK), 0)
@@ -332,28 +333,28 @@
         p3_ref[k] = stacked.T.astype(BF16)
 
 
-def orthonormal(gram, blocks, theirs):
+def orthonormal(gram, dither, blocks, theirs):
     return pl.pallas_call(
         orthonormal_body,
         out_shape=(
             pltpu.VMEM((NBLK, COLS, 4 * RANK), BF16),
             jax.ShapeDtypeStruct((RANK, RANK), F32),
+            jax.ShapeDtypeStruct((RANK, COLS), F32),
         ),
-        in_specs=[VM] * (3 + HALF),
-        out_specs=(VM, VM),
+        in_specs=[VM] * (4 + HALF),
+        out_specs=(VM, VM, VM),
         compiler_params=params(8),
         cost_estimate=cost(1 << 31),
         name="orthonormal",
-    )(gram, *blocks, theirs)
-
-
-def update_body(me_ref, a_ref, b_ref, c_ref, d_ref, inv_ref, dither_ref, p3_ref, *rest):
+    )(gram, dither, *blocks, theirs)
+
+
+def update_body(me_ref, a_ref, b_ref, c_ref, d_ref, inv_ref, scale_ref, p3_ref, *rest):
     mem = rest[:NBLK]
     qf_ref, out_hbm, stage, sem = rest[NBLK:]
     total = (a_ref[...] + b_ref[...]) + (c_ref[...] + d_ref[...])
     qmat = jnp.dot(inv_ref[...], total, precision=HIGH, preferred_element_type=F32) / WORKERS
-    scale = 1.0 + (dither_ref[...].astype(F32) / 65536.0 - 0.5) / 4.0
-    qt = (qmat * scale).astype(BF16)
+    qt = (qmat * scale_ref[...]).astype(BF16)
     qf_ref[...] = qt
     q3 = jnp.concatenate([qt, qt, qt, jnp.zeros((RANK, COLS), BF16)], axis=0)
     copies = []
@@ -494,12 +495,12 @@
     q, gram = right([(2 * r + 1, theirs, i) for i, r in enumerate(RING)], *held, mid, True)
 
     from_ring = ring(q, DP_FIRST)
-    p3, inv = orthonormal(gram, [own, other, *mine], theirs)
+    p3, inv, scale = orthonormal(gram, dither.T, [own, other, *mine], theirs)
     memory_of((3,), q)
     q = sum_after([q, *from_ring], [inv, memory[3]])
     from_ring = ring(q, DP_SECOND)
     memory_of((5, 7), q)
-    q_factor, new_error = update(me, [q, *from_ring], inv, dither.T, p3, [memory[r] for r in ORDER])
+    q_factor, new_error = update(me, [q, *from_ring], inv, scale, p3, [memory[r] for r in ORDER])
     return (q_factor.T, new_error)
 
 

time: 67.4 us -> 67.4 us (level)
  no operation moved by 1% of the time
where the time goes in v8:
time: 67.4 us; the launch traced here: 67.1 us
  Pallas kernels  32.1 us (48%)
  starting transfers between devices  26.4 us (39%)
  waiting for transfers between devices  7.56 us (11%)
  between operations  1.02 us (2%)
    ppermute x18, starting transfers between devices, exchange(): return lax.ppermute(v, ('dp', 'tensor'), pairs)  25.9 us
    pallas_call x6, Pallas kernels, memory_blocks(): pl.pallas_call(body, out_shape=shapes, in_specs=in_specs, out_specs=[VM]...  11.5 us
    ppermute x18, waiting for transfers between devices, exchange(): return lax.ppermute(v, ('dp', 'tensor'), pairs)  7.36 us
    pallas_call x4, Pallas kernels, right(): pl.pallas_call(body, out_shape=shapes, in_specs=[VM] * len(args), out_spe...  5.42 us
    pallas_call x1, Pallas kernels, update(): pl.pallas_call(update_body, out_shape=(jax.ShapeDtypeStruct((RANK, COLS),...  3.98 us
    pallas_call x1, Pallas kernels, left_away(): pl.pallas_call(body, out_shape=[jax.ShapeDtypeStruct((RANK, HALF * COLS +...  3.53 us
    pallas_call x1, Pallas kernels, left_kept(): pl.pallas_call(body, out_shape=[jax.ShapeDtypeStruct((3, RANK, COLS), F32...  2.94 us
    pallas_call x1, Pallas kernels, left_own(): pl.pallas_call(body, out_shape=[jax.ShapeDtypeStruct((RANK, COLS), F32),...  1.98 us
  transfers between devices with their start and end apart: 21, of which 6 were waited for; matrix products, arithmetic and copies ran while one was open for 0% of the time, Pallas kernels for 32%

profile of v8, /device:TPU:0, one launch (start us, length us, event | category | flops | bytes accessed | tf_op | source)
XLA Modules:
  0.0 67.1 jit_solution(11537246333569206129)
XLA Ops:
  0.6 3.5 %left_away.1 = (f32[32,3584]{1,0:T(8,128)S(1)}, bf16[4,640,640]{2,1,0:T(8,128)(2,1)S(1)}, bf16[1024,640]{1,0:T(8,128)(2,1)S(1)}, bf16[32,640]{1,0:T(8,128)(2,1)S(1)}) custom-call(s32[1]{0:T(128)} %bitcast.me_ref.refs_4_.refs_6_, bf16[5120,640]{1,0:T(8,128)(2,1)} %err_hbm.5, bf16[1024,640]{1,0:T(8,128)(2,1)} %grad_hbm.1, s32[32,640]{1,0:T(8,128)} %bitcast.11), custom_call_target="tpu_custom_call" | custom-call | flops 838860800 | bytes 5242880 | tf_op jit(solution)/shard_map/left_away/pallas_call | solution.py:111
  4.3 2.9 %left_kept.1 = (f32[3,32,640]{2,1,0:T(8,128)S(1)}, bf16[3,1024,640]{2,1,0:T(8,128)(2,1)S(1)}, bf16[3,640,640]{2,1,0:T(8,128)(2,1)S(1)}) custom-call(s32[1]{0:T(128)} %bitcast.me_ref.refs_4_.refs_6_, bf16[1024,5120]{1,0:T(8,128)(2,1)} %refs_7_.1, bf16[5120,640]{1,0:T(8,128)(2,1)} %err_hbm.5, bf16[32,640]{1,0:T(8,128)(2,1)S(1)} %get-tuple-element.37.qt_ref), custom_call_target="tpu_custom_call" | custom-call | flops 629145600 | bytes 6291456 | tf_op jit(solution)/shard_map/left_kept/pallas_call | solution.py:147
  7.2 0.8 %left_sum.1 = (f32[3,32,640]{2,1,0:T(8,128)S(1)}, bf16[96,1024]{1,0:T(8,128)(2,1)S(1)}) custom-call(bf16[3,1024,640]{2,1,0:T(8,128)(2,1)S(1)} %get-tuple-element.38.acts_v.refs_0_.refs_1_.refs_4_, f32[3,32,640]{2,1,0:T(8,128)S(1)} %get-tuple-element.39.kept, f32[32,3584]{1,0:T(8,128)S(1)} %get-tuple-element.40.away, f32[32,3584]{1,0:T(8,128)S(1)} %collective-permute-done.came), custom_call_target="tpu_custom_call" | custom-call | flops 1006632960 | tf_op jit(solution)/shard_map/left_sum/pallas_call | solution.py:172
  8.1 2.9 %collective-permute-start.3 = (f32[32,640]{1,0:T(8,128)S(1)}, f32[32,640]{1,0:T(8,128)S(1)}, u32[]{:S(2)}, u32[]{:S(2)}) collective-permute-start(f32[32,640]{1,0:T(8,128)S(1)} %get-tuple-element.72), channel_id=1, source_target_pairs={{0,24},{1,7},{2,26},{3,5},{4,28},{5,3},{6,30},{7,1},{8,16},{9,15},... | collective-permute-start | bytes 245768 | tf_op jit(solution)/shard_map/ppermute | solution.py:443
  11.0 0.8 %collective-permute-start.2 = (f32[32,640]{1,0:T(8,128)S(1)}, f32[32,640]{1,0:T(8,128)S(1)}, u32[]{:S(2)}, u32[]{:S(2)}) collective-permute-start(f32[32,640]{1,0:T(8,128)S(1)} %get-tuple-element.73), channel_id=1, source_target_pairs={{0,16},{1,5},{2,18},{3,7},{4,20},{5,1},{6,22},{7,3},{8,24},{9,13},... | collective-permute-start | bytes 245768 | tf_op jit(solution)/shard_map/ppermute | solution.py:443
  12.3 2.0 %left_own.1 = (f32[32,640]{1,0:T(8,128)S(1)}, bf16[1,1024,640]{2,1,0:T(8,128)(2,1)S(1)}, bf16[1,640,640]{2,1,0:T(8,128)(2,1)S(1)}) custom-call(s32[1]{0:T(128)} %bitcast.me_ref.refs_4_.refs_6_, bf16[1024,5120]{1,0:T(8,128)(2,1)} %refs_7_.1, bf16[5120,640]{1,0:T(8,128)(2,1)} %err_hbm.5, bf16[32,640]{1,0:T(8,128)(2,1)S(1)} %get-tuple-element.37.qt_ref, ...), custom_call_target="tpu_custom_call" | custom-call | flops 545259520 | bytes 2097152 | tf_op jit(solution)/shard_map/left_own/pallas_call | solution.py:199
  14.2 1.2 %memory_blocks.6.refs_4_.rest_2_ = f32[640,640]{1,0:T(8,128)S(1)} custom-call(bf16[3,1024,640]{2,1,0:T(8,128)(2,1)S(1)} %get-tuple-element.38.acts_v.refs_0_.refs_1_.refs_4_, bf16[3,640,640]{2,1,0:T(8,128)(2,1)S(1)} %get-tuple-element.44.refs_1_.refs_2_.refs_5_, bf16[1024,640]{1,0:T(8,128)(2,1)S(1)} %get-tuple-element.45.refs_2_.refs_4_.refs_6_.refs_3_.refs_9_, ...), custom_call_target="tpu_custom_call" | custom-call | flops 838860800 | tf_op jit(solution)/shard_map/memory_blocks/pallas_call | solution.py:244
  15.5 1.5 %collective-permute-done.2.refs_2_ = f32[32,640]{1,0:T(8,128)S(1)} collective-permute-done((f32[32,640]{1,0:T(8,128)S(1)}, f32[32,640]{1,0:T(8,128)S(1)}, u32[]{:S(2)}, u32[]{:S(2)}) %collective-permute-start.2) | collective-permute-done | bytes 81952 | tf_op jit(solution)/shard_map/ppermute | solution.py:443
  17.0 3.1 %collective-permute-start.6 = (f32[32,640]{1,0:T(8,128)S(1)}, f32[32,640]{1,0:T(8,128)S(1)}, u32[]{:S(2)}, u32[]{:S(2)}) collective-permute-start(f32[32,640]{1,0:T(8,128)S(1)} %sum_after.4.refs_3_.refs_0_), channel_id=1, source_target_pairs={{0,96},{1,25},{2,98},{3,27},{4,100},{5,29},{6,102},{7,31},{8,104},... | collective-permute-start | bytes 245768 | tf_op jit(solution)/shard_map/ppermute | solution.py:443
  21.2 2.7 %memory_blocks.7 = (f32[640,640]{1,0:T(8,128)S(1)}, bf16[3,1024,640]{2,1,0:T(8,128)(2,1)S(1)}) custom-call(bf16[1,1024,640]{2,1,0:T(8,128)(2,1)S(1)} %get-tuple-element.46.refs_0_.refs_1_, bf16[1,640,640]{2,1,0:T(8,128)(2,1)S(1)} %get-tuple-element.47.refs_1_.refs_2_, bf16[1024,640]{1,0:T(8,128)(2,1)S(1)} %get-tuple-element.45.refs_2_.refs_4_.refs_6_.refs_3_.refs_9_, ...), custom_call_target="tpu_custom_call" | custom-call | flops 838860800 | tf_op jit(solution)/shard_map/memory_blocks/pallas_call | solution.py:244
  23.8 2.2 %collective-permute-done.5.refs_2_ = f32[32,640]{1,0:T(8,128)S(1)} collective-permute-done((f32[32,640]{1,0:T(8,128)S(1)}, f32[32,640]{1,0:T(8,128)S(1)}, u32[]{:S(2)}, u32[]{:S(2)}) %collective-permute-start.5) | collective-permute-done | bytes 81952 | tf_op jit(solution)/shard_map/ppermute | solution.py:443
  26.1 4.1 %collective-permute-start.9 = (f32[32,640]{1,0:T(8,128)S(1)}, f32[32,640]{1,0:T(8,128)S(1)}, u32[]{:S(2)}, u32[]{:S(2)}) collective-permute-start(f32[32,640]{1,0:T(8,128)S(1)} %sum_after.5.refs_5_.refs_0_), channel_id=1, source_target_pairs={{0,6},{1,97},{2,4},{3,99},{4,2},{5,101},{6,0},{7,103},{8,14},{9,10... | collective-permute-start | bytes 245768 | tf_op jit(solution)/shard_map/ppermute | solution.py:443
  30.2 0.9 %collective-permute-start.7 = (f32[32,640]{1,0:T(8,128)S(1)}, f32[32,640]{1,0:T(8,128)S(1)}, u32[]{:S(2)}, u32[]{:S(2)}) collective-permute-start(f32[32,640]{1,0:T(8,128)S(1)} %sum_after.5.refs_5_.refs_0_), channel_id=1, source_target_pairs={{0,2},{1,33},{2,0},{3,35},{4,6},{5,37},{6,4},{7,39},{8,10},{9,41},... | collective-permute-start | bytes 245768 | tf_op jit(solution)/shard_map/ppermute | solution.py:443
  31.1 2.9 %memory_blocks.8 = (f32[640,640]{1,0:T(8,128)S(1)}, f32[640,640]{1,0:T(8,128)S(1)}, bf16[1,1024,640]{2,1,0:T(8,128)(2,1)S(1)}) custom-call(bf16[3,1024,640]{2,1,0:T(8,128)(2,1)S(1)} %get-tuple-element.38.acts_v.refs_0_.refs_1_.refs_4_, bf16[3,640,640]{2,1,0:T(8,128)(2,1)S(1)} %get-tuple-element.44.refs_1_.refs_2_.refs_5_, ...), custom_call_target="tpu_custom_call" | custom-call | flops 1677721600 | tf_op jit(solution)/shard_map/memory_blocks/pallas_call | solution.py:244
  34.0 2.1 %collective-permute-done.8.refs_2_ = f32[32,640]{1,0:T(8,128)S(1)} collective-permute-done((f32[32,640]{1,0:T(8,128)S(1)}, f32[32,640]{1,0:T(8,128)S(1)}, u32[]{:S(2)}, u32[]{:S(2)}) %collective-permute-start.8) | collective-permute-done | bytes 81952 | tf_op jit(solution)/shard_map/ppermute | solution.py:443
  36.2 1.5 %collective-permute-start.12 = (f32[32,640]{1,0:T(8,128)S(1)}, f32[32,640]{1,0:T(8,128)S(1)}, u32[]{:S(2)}, u32[]{:S(2)}) collective-permute-start(f32[32,640]{1,0:T(8,128)S(1)} %sum_after.6.refs_0_.refs_3_), channel_id=1, source_target_pairs={{0,24},{1,7},{2,26},{3,5},{4,28},{5,3},{6,30},{7,1},{8,16},{9,15},... | collective-permute-start | bytes 245768 | tf_op jit(solution)/shard_map/ppermute | solution.py:443
  37.8 0.9 %collective-permute-start.11 = (f32[32,640]{1,0:T(8,128)S(1)}, f32[32,640]{1,0:T(8,128)S(1)}, u32[]{:S(2)}, u32[]{:S(2)}) collective-permute-start(f32[32,640]{1,0:T(8,128)S(1)} %sum_after.6.refs_0_.refs_3_), channel_id=1, source_target_pairs={{0,16},{1,5},{2,18},{3,7},{4,20},{5,1},{6,22},{7,3},{8,24},{9,13},... | collective-permute-start | bytes 245768 | tf_op jit(solution)/shard_map/ppermute | solution.py:443
  38.6 1.8 %collective-permute-start.10 = (f32[32,640]{1,0:T(8,128)S(1)}, f32[32,640]{1,0:T(8,128)S(1)}, u32[]{:S(2)}, u32[]{:S(2)}) collective-permute-start(f32[32,640]{1,0:T(8,128)S(1)} %sum_after.6.refs_0_.refs_3_), channel_id=1, source_target_pairs={{0,8},{1,3},{2,10},{3,1},{4,12},{5,7},{6,14},{7,5},{8,0},{9,11},{1... | collective-permute-start | bytes 245768 | tf_op jit(solution)/shard_map/ppermute | solution.py:443
  40.4 1.2 %memory_blocks.9.refs_4_.rest_4_ = f32[640,640]{1,0:T(8,128)S(1)} custom-call(bf16[3,1024,640]{2,1,0:T(8,128)(2,1)S(1)} %get-tuple-element.38.acts_v.refs_0_.refs_1_.refs_4_, bf16[3,640,640]{2,1,0:T(8,128)(2,1)S(1)} %get-tuple-element.44.refs_1_.refs_2_.refs_5_, bf16[1024,640]{1,0:T(8,128)(2,1)S(1)} %get-tuple-element.45.refs_2_.refs_4_.refs_6_.refs_3_.refs_9_, ...), custom_call_target="tpu_custom_call" | custom-call | flops 838860800 | tf_op jit(solution)/shard_map/memory_blocks/pallas_call | solution.py:244
  41.6 1.3 %right_part.3 = (f32[32,1024]{1,0:T(8,128)S(1)}, f32[32,640]{1,0:T(8,128)S(1)}, f32[96,96]{1,0:T(8,128)S(1)}) custom-call(f32[32,640]{1,0:T(8,128)S(1)} %sum_after.6.refs_0_.refs_3_, bf16[1,1024,640]{2,1,0:T(8,128)(2,1)S(1)} %get-tuple-element.46.refs_0_.refs_1_, bf16[1,640,640]{2,1,0:T(8,128)(2,1)S(1)} %get-tuple-element.47.refs_1_.refs_2_, ...), custom_call_target="tpu_custom_call" | custom-call | flops 1090519040 | tf_op jit(solution)/shard_map/right_part/pallas_call | solution.py:289
  44.0 1.3 %right_part.5 = (f32[32,1024]{1,0:T(8,128)S(1)}, f32[32,640]{1,0:T(8,128)S(1)}, f32[96,96]{1,0:T(8,128)S(1)}) custom-call(f32[32,640]{1,0:T(8,128)S(1)} %collective-permute-done.10.refs_0_.refs_2_, bf16[3,1024,640]{2,1,0:T(8,128)(2,1)S(1)} %get-tuple-element.38.acts_v.refs_0_.refs_1_.refs_4_, ...), custom_call_target="tpu_custom_call" | custom-call | flops 1090519040 | tf_op jit(solution)/shard_map/right_part/pallas_call | solution.py:289
  45.5 2.1 %right_last.1 = (f32[32,640]{1,0:T(8,128)S(1)}, f32[96,96]{1,0:T(8,128)S(1)}) custom-call(f32[3,32,640]{2,1,0:T(8,128)S(1)} %collective-permute-done.14.refs_0_.refs_3_.refs_6_.refs_5_, bf16[3,1024,640]{2,1,0:T(8,128)(2,1)S(1)} %get-tuple-element.49.refs_2_.refs_4_.refs_1_.refs_0_, ...), custom_call_target="tpu_custom_call" | custom-call | flops 1635778560 | tf_op jit(solution)/shard_map/right_last/pallas_call | solution.py:289
  47.6 1.9 %collective-permute-start.17 = (f32[32,640]{1,0:T(8,128)S(1)}, f32[32,640]{1,0:T(8,128)S(1)}, u32[]{:S(2)}, u32[]{:S(2)}) collective-permute-start(f32[32,640]{1,0:T(8,128)S(1)} %get-tuple-element.62.refs_3_.refs_0_), channel_id=1, source_target_pairs={{0,24},{1,97},{2,26},{3,99},{4,28},{5,101},{6,30},{7,103},{8,16},{... | collective-permute-start | bytes 245768 | tf_op jit(solution)/shard_map/ppermute | solution.py:443
  49.5 1.4 %collective-permute-start.16 = (f32[32,640]{1,0:T(8,128)S(1)}, f32[32,640]{1,0:T(8,128)S(1)}, u32[]{:S(2)}, u32[]{:S(2)}) collective-permute-start(f32[32,640]{1,0:T(8,128)S(1)} %get-tuple-element.62.refs_3_.refs_0_), channel_id=1, source_target_pairs={{0,16},{1,65},{2,18},{3,67},{4,20},{5,69},{6,22},{7,71},{8,24},{9,... | collective-permute-start | bytes 245768 | tf_op jit(solution)/shard_map/ppermute | solution.py:443
  50.9 0.9 %collective-permute-start.15 = (f32[32,640]{1,0:T(8,128)S(1)}, f32[32,640]{1,0:T(8,128)S(1)}, u32[]{:S(2)}, u32[]{:S(2)}) collective-permute-start(f32[32,640]{1,0:T(8,128)S(1)} %get-tuple-element.62.refs_3_.refs_0_), channel_id=1, source_target_pairs={{0,8},{1,33},{2,10},{3,35},{4,12},{5,37},{6,14},{7,39},{8,0},{9,41... | collective-permute-start | bytes 245768 | tf_op jit(solution)/shard_map/ppermute | solution.py:443
  51.8 1.9 %orthonormal.1 = (bf16[8,640,128]{2,1,0:T(8,128)(2,1)S(1)}, f32[32,32]{1,0:T(8,128)S(1)}, f32[32,640]{1,0:T(8,128)S(1)}) custom-call(f32[96,96]{1,0:T(8,128)S(1)} %get-tuple-element.63.gram_ref, s32[32,640]{1,0:T(8,128)S(1)} %bitcast.10, f32[32,640]{1,0:T(8,128)S(1)} %sum_after.6.refs_0_.refs_3_, f32[32,640]{1,0:T(8,128)S(1)} %collective-permute-done.13.refs_3_.refs_1_, ...), custom_call_target="tpu_custom_call" | custom-call | flops 2147483648 | tf_op jit(solution)/shard_map/orthonormal/pallas_call | solution.py:337
  53.7 1.2 %memory_blocks.10.refs_5_.rest_5_ = f32[640,640]{1,0:T(8,128)S(1)} custom-call(bf16[3,1024,640]{2,1,0:T(8,128)(2,1)S(1)} %get-tuple-element.49.refs_2_.refs_4_.refs_1_.refs_0_, bf16[4,640,640]{2,1,0:T(8,128)(2,1)S(1)} %get-tuple-element.50.refs_3_.refs_5_.refs_2_.refs_8_.refs_1_, ...), custom_call_target="tpu_custom_call" | custom-call | flops 838860800 | tf_op jit(solution)/shard_map/memory_blocks/pallas_call | solution.py:244
  55.5 1.5 %collective-permute-start.20 = (f32[32,640]{1,0:T(8,128)S(1)}, f32[32,640]{1,0:T(8,128)S(1)}, u32[]{:S(2)}, u32[]{:S(2)}) collective-permute-start(f32[32,640]{1,0:T(8,128)S(1)} %sum_after.7.refs_5_.a_ref), channel_id=1, source_target_pairs={{0,96},{1,25},{2,98},{3,27},{4,100},{5,29},{6,102},{7,31},{8,104},... | collective-permute-start | bytes 245768 | tf_op jit(solution)/shard_map/ppermute | solution.py:443
  57.8 1.9 %collective-permute-start.18 = (f32[32,640]{1,0:T(8,128)S(1)}, f32[32,640]{1,0:T(8,128)S(1)}, u32[]{:S(2)}, u32[]{:S(2)}) collective-permute-start(f32[32,640]{1,0:T(8,128)S(1)} %sum_after.7.refs_5_.a_ref), channel_id=1, source_target_pairs={{0,32},{1,9},{2,34},{3,11},{4,36},{5,13},{6,38},{7,15},{8,40},{9,1... | collective-permute-start | bytes 245768 | tf_op jit(solution)/shard_map/ppermute | solution.py:443
  59.7 2.2 %memory_blocks.11 = (f32[640,640]{1,0:T(8,128)S(1)}, f32[640,640]{1,0:T(8,128)S(1)}) custom-call(bf16[3,1024,640]{2,1,0:T(8,128)(2,1)S(1)} %get-tuple-element.49.refs_2_.refs_4_.refs_1_.refs_0_, bf16[4,640,640]{2,1,0:T(8,128)(2,1)S(1)} %get-tuple-element.50.refs_3_.refs_5_.refs_2_.refs_8_.refs_1_, ...), custom_call_target="tpu_custom_call" | custom-call | flops 1677721600 | tf_op jit(solution)/shard_map/memory_blocks/pallas_call | solution.py:244
  61.9 1.0 %collective-permute-done.19.c_ref = f32[32,640]{1,0:T(8,128)S(1)} collective-permute-done((f32[32,640]{1,0:T(8,128)S(1)}, f32[32,640]{1,0:T(8,128)S(1)}, u32[]{:S(2)}, u32[]{:S(2)}) %collective-permute-start.19) | collective-permute-done | bytes 81952 | tf_op jit(solution)/shard_map/ppermute | solution.py:443
  62.9 4.0 %update.1 = (bf16[32,640]{1,0:T(8,128)(2,1)}, bf16[5120,640]{1,0:T(8,128)(2,1)}) custom-call(s32[1]{0:T(128)} %bitcast.me_ref.refs_4_.refs_6_, f32[32,640]{1,0:T(8,128)S(1)} %sum_after.7.refs_5_.a_ref, f32[32,640]{1,0:T(8,128)S(1)} %collective-permute-done.18.b_ref, f32[32,640]{1,0:T(8,128)S(1)} %collective-permute-done.19.c_ref, ...), custom_call_target="tpu_custom_call" | custom-call | flops 1677721600 | bytes 7340032 | tf_op jit(solution)/shard_map/update/pallas_call | solution.py:377
  (34 shorter events, 4.4 us)
Async XLA Ops:
  4.2 3.0 %collective-permute-start = (f32[32,3584]{1,0:T(8,128)S(1)}, f32[32,3584]{1,0:T(8,128)S(1)}, u32[]{:S(2)}, u32[]{:S(2)}) collective-permute-start(f32[32,3584]{1,0:T(8,128)S(1)} %get-tuple-element.40.away), channel_id=1, source_target_pairs={{0,1},{1,0},{2,3},{3,2},{4,5},{5,4},{6,7},{7,6},{8,9},{9,8},{10,11... | collective-permute-start | bytes 1376264 | tf_op jit(solution)/shard_map/ppermute | solution.py:451
  8.1 7.4 %collective-permute-start.3 = (f32[32,640]{1,0:T(8,128)S(1)}, f32[32,640]{1,0:T(8,128)S(1)}, u32[]{:S(2)}, u32[]{:S(2)}) collective-permute-start(f32[32,640]{1,0:T(8,128)S(1)} %get-tuple-element.72), channel_id=1, source_target_pairs={{0,24},{1,7},{2,26},{3,5},{4,28},{5,3},{6,30},{7,1},{8,16},{9,15},... | collective-permute-start | bytes 245768 | tf_op jit(solution)/shard_map/ppermute | solution.py:443
  11.0 5.9 %collective-permute-start.2 = (f32[32,640]{1,0:T(8,128)S(1)}, f32[32,640]{1,0:T(8,128)S(1)}, u32[]{:S(2)}, u32[]{:S(2)}) collective-permute-start(f32[32,640]{1,0:T(8,128)S(1)} %get-tuple-element.73), channel_id=1, source_target_pairs={{0,16},{1,5},{2,18},{3,7},{4,20},{5,1},{6,22},{7,3},{8,24},{9,13},... | collective-permute-start | bytes 245768 | tf_op jit(solution)/shard_map/ppermute | solution.py:443
  11.8 5.1 %collective-permute-start.1 = (f32[32,640]{1,0:T(8,128)S(1)}, f32[32,640]{1,0:T(8,128)S(1)}, u32[]{:S(2)}, u32[]{:S(2)}) collective-permute-start(f32[32,640]{1,0:T(8,128)S(1)} %get-tuple-element.74), channel_id=1, source_target_pairs={{0,8},{1,3},{2,10},{3,1},{4,12},{5,7},{6,14},{7,5},{8,0},{9,11},{1... | collective-permute-start | bytes 245768 | tf_op jit(solution)/shard_map/ppermute | solution.py:443
  17.0 6.8 %collective-permute-start.6 = (f32[32,640]{1,0:T(8,128)S(1)}, f32[32,640]{1,0:T(8,128)S(1)}, u32[]{:S(2)}, u32[]{:S(2)}) collective-permute-start(f32[32,640]{1,0:T(8,128)S(1)} %sum_after.4.refs_3_.refs_0_), channel_id=1, source_target_pairs={{0,96},{1,25},{2,98},{3,27},{4,100},{5,29},{6,102},{7,31},{8,104},... | collective-permute-start | bytes 245768 | tf_op jit(solution)/shard_map/ppermute | solution.py:443
  20.1 5.9 %collective-permute-start.5 = (f32[32,640]{1,0:T(8,128)S(1)}, f32[32,640]{1,0:T(8,128)S(1)}, u32[]{:S(2)}, u32[]{:S(2)}) collective-permute-start(f32[32,640]{1,0:T(8,128)S(1)} %sum_after.4.refs_3_.refs_0_), channel_id=1, source_target_pairs={{0,64},{1,17},{2,66},{3,19},{4,68},{5,21},{6,70},{7,23},{8,72},{9,... | collective-permute-start | bytes 245768 | tf_op jit(solution)/shard_map/ppermute | solution.py:443
  20.7 5.3 %collective-permute-start.4 = (f32[32,640]{1,0:T(8,128)S(1)}, f32[32,640]{1,0:T(8,128)S(1)}, u32[]{:S(2)}, u32[]{:S(2)}) collective-permute-start(f32[32,640]{1,0:T(8,128)S(1)} %sum_after.4.refs_3_.refs_0_), channel_id=1, source_target_pairs={{0,32},{1,9},{2,34},{3,11},{4,36},{5,13},{6,38},{7,15},{8,40},{9,1... | collective-permute-start | bytes 245768 | tf_op jit(solution)/shard_map/ppermute | solution.py:443
  26.1 8.0 %collective-permute-start.9 = (f32[32,640]{1,0:T(8,128)S(1)}, f32[32,640]{1,0:T(8,128)S(1)}, u32[]{:S(2)}, u32[]{:S(2)}) collective-permute-start(f32[32,640]{1,0:T(8,128)S(1)} %sum_after.5.refs_5_.refs_0_), channel_id=1, source_target_pairs={{0,6},{1,97},{2,4},{3,99},{4,2},{5,101},{6,0},{7,103},{8,14},{9,10... | collective-permute-start | bytes 245768 | tf_op jit(solution)/shard_map/ppermute | solution.py:443
  30.2 5.9 %collective-permute-start.8 = (f32[32,640]{1,0:T(8,128)S(1)}, f32[32,640]{1,0:T(8,128)S(1)}, u32[]{:S(2)}, u32[]{:S(2)}) collective-permute-start(f32[32,640]{1,0:T(8,128)S(1)} %sum_after.5.refs_5_.refs_0_), channel_id=1, source_target_pairs={{0,4},{1,65},{2,6},{3,67},{4,0},{5,69},{6,2},{7,71},{8,12},{9,73},... | collective-permute-start | bytes 245768 | tf_op jit(solution)/shard_map/ppermute | solution.py:443
  30.2 5.9 %collective-permute-start.7 = (f32[32,640]{1,0:T(8,128)S(1)}, f32[32,640]{1,0:T(8,128)S(1)}, u32[]{:S(2)}, u32[]{:S(2)}) collective-permute-start(f32[32,640]{1,0:T(8,128)S(1)} %sum_after.5.refs_5_.refs_0_), channel_id=1, source_target_pairs={{0,2},{1,33},{2,0},{3,35},{4,6},{5,37},{6,4},{7,39},{8,10},{9,41},... | collective-permute-start | bytes 245768 | tf_op jit(solution)/shard_map/ppermute | solution.py:443
  36.1 5.5 %collective-permute-start.13 = (f32[32,640]{1,0:T(8,128)S(1)}, f32[32,640]{1,0:T(8,128)S(1)}, u32[]{:S(2)}, u32[]{:S(2)}) collective-permute-start(f32[32,640]{1,0:T(8,128)S(1)} %sum_after.6.refs_0_.refs_3_), channel_id=1, source_target_pairs={{0,1},{1,0},{2,3},{3,2},{4,5},{5,4},{6,7},{7,6},{8,9},{9,8},{10,11... | collective-permute-start | bytes 245768 | tf_op jit(solution)/shard_map/ppermute | solution.py:451
  36.2 6.7 %collective-permute-start.12 = (f32[32,640]{1,0:T(8,128)S(1)}, f32[32,640]{1,0:T(8,128)S(1)}, u32[]{:S(2)}, u32[]{:S(2)}) collective-permute-start(f32[32,640]{1,0:T(8,128)S(1)} %sum_after.6.refs_0_.refs_3_), channel_id=1, source_target_pairs={{0,24},{1,7},{2,26},{3,5},{4,28},{5,3},{6,30},{7,1},{8,16},{9,15},... | collective-permute-start | bytes 245768 | tf_op jit(solution)/shard_map/ppermute | solution.py:443
  37.8 5.9 %collective-permute-start.11 = (f32[32,640]{1,0:T(8,128)S(1)}, f32[32,640]{1,0:T(8,128)S(1)}, u32[]{:S(2)}, u32[]{:S(2)}) collective-permute-start(f32[32,640]{1,0:T(8,128)S(1)} %sum_after.6.refs_0_.refs_3_), channel_id=1, source_target_pairs={{0,16},{1,5},{2,18},{3,7},{4,20},{5,1},{6,22},{7,3},{8,24},{9,13},... | collective-permute-start | bytes 245768 | tf_op jit(solution)/shard_map/ppermute | solution.py:443
  38.6 5.1 %collective-permute-start.10 = (f32[32,640]{1,0:T(8,128)S(1)}, f32[32,640]{1,0:T(8,128)S(1)}, u32[]{:S(2)}, u32[]{:S(2)}) collective-permute-start(f32[32,640]{1,0:T(8,128)S(1)} %sum_after.6.refs_0_.refs_3_), channel_id=1, source_target_pairs={{0,8},{1,3},{2,10},{3,1},{4,12},{5,7},{6,14},{7,5},{8,0},{9,11},{1... | collective-permute-start | bytes 245768 | tf_op jit(solution)/shard_map/ppermute | solution.py:443
  43.7 1.8 %collective-permute-start.14 = (f32[3,32,640]{2,1,0:T(8,128)S(1)}, f32[3,32,640]{2,1,0:T(8,128)S(1)}, u32[]{:S(2)}, u32[]{:S(2)}) collective-permute-start(f32[3,32,640]{2,1,0:T(8,128)S(1)} %stack_after.1), channel_id=1, source_target_pairs={{0,1},{1,0},{2,3},{3,2},{4,5},{5,4},{6,7},{7,6},{8,9},{9,8},{10,11... | collective-permute-start | bytes 737288 | tf_op jit(solution)/shard_map/ppermute | solution.py:451
  45.5 6.3 %copy-start = (s32[640,32]{0,1:T(8,128)S(1)}, s32[640,32]{0,1:T(8,128)}, u32[]{:S(2)}) copy-start(s32[640,32]{0,1:T(8,128)} %param.9) | copy-start | bytes 245764
  47.6 7.3 %collective-permute-start.17 = (f32[32,640]{1,0:T(8,128)S(1)}, f32[32,640]{1,0:T(8,128)S(1)}, u32[]{:S(2)}, u32[]{:S(2)}) collective-permute-start(f32[32,640]{1,0:T(8,128)S(1)} %get-tuple-element.62.refs_3_.refs_0_), channel_id=1, source_target_pairs={{0,24},{1,97},{2,26},{3,99},{4,28},{5,101},{6,30},{7,103},{8,16},{... | collective-permute-start | bytes 245768 | tf_op jit(solution)/shard_map/ppermute | solution.py:443
  49.5 5.9 %collective-permute-start.16 = (f32[32,640]{1,0:T(8,128)S(1)}, f32[32,640]{1,0:T(8,128)S(1)}, u32[]{:S(2)}, u32[]{:S(2)}) collective-permute-start(f32[32,640]{1,0:T(8,128)S(1)} %get-tuple-element.62.refs_3_.refs_0_), channel_id=1, source_target_pairs={{0,16},{1,65},{2,18},{3,67},{4,20},{5,69},{6,22},{7,71},{8,24},{9,... | collective-permute-start | bytes 245768 | tf_op jit(solution)/shard_map/ppermute | solution.py:443
  50.9 4.5 %collective-permute-start.15 = (f32[32,640]{1,0:T(8,128)S(1)}, f32[32,640]{1,0:T(8,128)S(1)}, u32[]{:S(2)}, u32[]{:S(2)}) collective-permute-start(f32[32,640]{1,0:T(8,128)S(1)} %get-tuple-element.62.refs_3_.refs_0_), channel_id=1, source_target_pairs={{0,8},{1,33},{2,10},{3,35},{4,12},{5,37},{6,14},{7,39},{8,0},{9,41... | collective-permute-start | bytes 245768 | tf_op jit(solution)/shard_map/ppermute | solution.py:443
  55.5 6.4 %collective-permute-start.20 = (f32[32,640]{1,0:T(8,128)S(1)}, f32[32,640]{1,0:T(8,128)S(1)}, u32[]{:S(2)}, u32[]{:S(2)}) collective-permute-start(f32[32,640]{1,0:T(8,128)S(1)} %sum_after.7.refs_5_.a_ref), channel_id=1, source_target_pairs={{0,96},{1,25},{2,98},{3,27},{4,100},{5,29},{6,102},{7,31},{8,104},... | collective-permute-start | bytes 245768 | tf_op jit(solution)/shard_map/ppermute | solution.py:443
  57.0 5.9 %collective-permute-start.19 = (f32[32,640]{1,0:T(8,128)S(1)}, f32[32,640]{1,0:T(8,128)S(1)}, u32[]{:S(2)}, u32[]{:S(2)}) collective-permute-start(f32[32,640]{1,0:T(8,128)S(1)} %sum_after.7.refs_5_.a_ref), channel_id=1, source_target_pairs={{0,64},{1,17},{2,66},{3,19},{4,68},{5,21},{6,70},{7,23},{8,72},{9,... | collective-permute-start | bytes 245768 | tf_op jit(solution)/shard_map/ppermute | solution.py:443
  57.8 5.2 %collective-permute-start.18 = (f32[32,640]{1,0:T(8,128)S(1)}, f32[32,640]{1,0:T(8,128)S(1)}, u32[]{:S(2)}, u32[]{:S(2)}) collective-permute-start(f32[32,640]{1,0:T(8,128)S(1)} %sum_after.7.refs_5_.a_ref), channel_id=1, source_target_pairs={{0,32},{1,9},{2,34},{3,11},{4,36},{5,13},{6,38},{7,15},{8,40},{9,1... | collective-permute-start | bytes 245768 | tf_op jit(solution)/shard_map/ppermute | solution.py:443
